TPU v7x, 256 devices: a whole 4x4x8 slice. The times are simulated.
256 devices in a mesh: row: 32 (over z, y_hi, core), col: 8 (over y_lo, x).
Axes of the slice: x: 4, y: 4 (y_hi: 2, y_lo: 2; y = y_hi * 2 + y_lo), z: 8, core: 2. Of those that a mesh axis runs over, the one named last changes fastest.
Arguments:
- density: bfloat16 [8192, 8192], P('row', 'col'), as said below
- pattern: int32 [32, 32], replicated, may hold values from 0 to 1, as said below
- tile_perm: int32 [32], replicated, may hold values from 0 to 31, each once
Outputs:
- square: float32 [8192, 8192], P('row', 'col')
- cubed: float32 [8192, 8192], P('row', 'col')
Inputs may be any that keep to these rules, and one draw needn't show every extreme that they name: `pattern`: zero below the diagonal, one on the diagonal, ones above it near the diagonal and scattered further away; every tile row of sym_pattern holds at most 13 ones, and some tile row holds exactly 13. density is exactly symmetric.
All inputs are finite; a program needn't handle non-finite values.
Results may differ from a plain program's by a relative error of at most 0.0021.
Values may be sent and summed in bfloat16 or wider, within the bound.
No kernel may reach another device: no remote copies, remote signals or barrier semaphores. Data moves between devices by JAX's collectives and lax.ppermute only.
A program may use at most 64 MiB of HBM per device.

v0:
```python
import jax
import jax.numpy as jnp
from jax import lax
from jax.sharding import PartitionSpec as P

TILE = 256


def local_mask(pattern, tile_perm, row_count, col_count):
    count = pattern.shape[0]
    tile_index = jnp.arange(count, dtype=jnp.int32)
    symmetric = jnp.where(tile_index[:, None] <= tile_index[None, :], pattern, pattern.T).astype(
        jnp.float32
    )
    one_hot = (tile_perm[:, None] == tile_index[None, :]).astype(jnp.float32)
    whole_mask = jnp.dot(
        jnp.dot(one_hot, symmetric, precision=lax.Precision.HIGHEST),
        one_hot.T,
        precision=lax.Precision.HIGHEST,
    )
    row_tiles = row_count // TILE
    col_tiles = col_count // TILE
    return lax.dynamic_slice(
        whole_mask,
        (lax.axis_index("row") * row_tiles, lax.axis_index("col") * col_tiles),
        (row_tiles, col_tiles),
    )


def mask_block(matrix, tile_mask):
    row_tiles, col_tiles = tile_mask.shape
    blocks = matrix.reshape(row_tiles, TILE, col_tiles, TILE) * tile_mask[:, None, :, None].astype(
        matrix.dtype
    )
    return blocks.reshape(matrix.shape)


def local(density, pattern, tile_perm):
    row_count, col_count = density.shape
    tile_mask = local_mask(pattern, tile_perm, row_count, col_count)
    matrix = mask_block(density, tile_mask)
    matrix_order = row_count * lax.axis_size("row")
    column = lax.all_gather(matrix, "row", axis=0, tiled=True)
    lower = column
    square = jnp.dot(
        lax.all_gather(matrix, "col", axis=1, tiled=True), lower, preferred_element_type=jnp.float32
    )
    square = mask_block(square, tile_mask)
    square_half = square.astype(jnp.bfloat16)
    lower = column
    cube_sum = jnp.dot(
        lax.all_gather(square_half, "col", axis=1, tiled=True),
        lower,
        preferred_element_type=jnp.float32,
    )
    scale_factor = (matrix_order / 2.0) ** (-0.25)
    cubed = mask_block(cube_sum, tile_mask) * scale_factor
    return (square, cubed)


def solution(mesh):
    placed = (P("row", "col"), P(), P())
    return jax.shard_map(
        local,
        mesh=mesh,
        in_specs=placed,
        out_specs=(P("row", "col"), P("row", "col")),
        check_vma=False,
    )
```

profile of v0, /device:TPU:1, one launch (start us, length us, event | category | flops | bytes accessed | tf_op | source)
XLA Modules:
  0.0 294.6 jit_solution(3492272612850143521)
XLA Ops:
  7.2 0.0 all-gather.4.cloned.1.call-start
  7.2 0.8 copy.5
  8.0 0.9 fusion.2
  8.9 0.9 fusion.4
  9.8 0.1 fusion.7
  9.9 0.1 broadcast_bitcast_fusion.1
  10.0 1.9 broadcast_multiply_fusion
  11.8 0.0 all-gather.4.cloned.1.call-update
  11.9 0.0 all-gather.6.cloned.1.call-start
  11.9 0.7 all-gather.6.cloned.1.call-update
  12.6 0.0 all-gather.8.cloned.1.call-start
  12.7 0.1 broadcast_bitcast_fusion
  12.7 58.2 %all-gather.4.cloned.1.call-done = bf16[256,8192]{1,0:T(8,128)(2,1)} async-done(((bf16[256,1024]{1,0:T(8,128)(2,1)}), bf16[256,8192]{1,0:T(8,128)(2,1)}) %all-gather.4.cloned.1.call-update) | async-done | bytes 4194320 | tf_op jit(solution)/shard_map/all_gather | solution.py:46
  71.0 140.4 %all-gather.6.cloned.1.call-done = bf16[8192,1024]{1,0:T(8,128)(2,1)} async-done(((bf16[256,1024]{1,0:T(8,128)(2,1)}), bf16[8192,1024]{1,0:T(8,128)(2,1)}) %all-gather.6.cloned.1.call-update) | async-done | bytes 16777232 | tf_op jit(solution)/shard_map/all_gather | solution.py:43
  211.4 12.7 %fusion.8 = (bf16[256,1024]{1,0:T(8,128)(2,1)}, f32[256,1024]{1,0:T(8,128)}) fusion(f32[1024]{0:T(1024)S(1)} %bitcast.20, bf16[256,8192]{1,0:T(8,128)(2,1)} %all-gather.4.cloned.1.call-done, bf16[8192,1024]{1,0:T(8,128)(2,1)} %all-gather.6.cloned.1.call-done), kind=kOutput, calls=%fused_computation.16 | convolution fusion | flops 4295491584 | bytes 22548480 | tf_op jit(solution)/shard_map/dot_general | solution.py:45
  224.0 0.0 all-gather.8.cloned.1.call-update
  224.0 51.6 %all-gather.8.cloned.1.call-done = bf16[256,8192]{1,0:T(8,128)(2,1)} async-done(((bf16[256,1024]{1,0:T(8,128)(2,1)}), bf16[256,8192]{1,0:T(8,128)(2,1)}) %all-gather.8.cloned.1.call-update) | async-done | bytes 4194320 | tf_op jit(solution)/shard_map/all_gather | solution.py:52
  275.6 12.5 %fusion = f32[256,1024]{1,0:T(8,128)} fusion(bf16[256,8192]{1,0:T(8,128)(2,1)} %all-gather.8.cloned.1.call-done, bf16[8192,1024]{1,0:T(8,128)(2,1)} %all-gather.6.cloned.1.call-done, f32[1024]{0:T(1024)S(1)} %bitcast.21), kind=kOutput, calls=%fused_computation.1 | convolution fusion | flops 4295491584 | bytes 22024192 | tf_op jit(solution)/shard_map/dot_general | solution.py:51
  (2 shorter events, 0.0 us)
Async XLA Ops:
  7.2 63.8 %all-gather.4.cloned.1.call-start = ((), (), s32[]{:S(2)}) async-start(), calls=%async_computation | async-start | bytes 4718592 | tf_op jit(solution)/shard_map/all_gather | solution.py:46
  11.9 199.5 %all-gather.6.cloned.1.call-start = ((), (), s32[]{:S(2)}) async-start(), calls=%async_computation.1 | async-start | bytes 17301504 | tf_op jit(solution)/shard_map/all_gather | solution.py:43
  12.6 263.0 %all-gather.8.cloned.1.call-start = ((), (), s32[]{:S(2)}) async-start(), calls=%async_computation.2 | async-start | bytes 4718592 | tf_op jit(solution)/shard_map/all_gather | solution.py:52
Sparse Core Ops, SparseCore 0:
  12.0 58.9 all-gather.3
  74.3 136.9 all-gather.5
  224.2 51.3 all-gather.7
where the time goes:
time: 295 us
  waiting for transfers between devices  251 us (85%)
  matrix products  27 us (9%)
  between operations  13.8 us (5%)
    all_gather x1, waiting for transfers between devices, local(): column = lax.all_gather(matrix, 'row', axis=0, tiled=True)  140 us
    all_gather x1, waiting for transfers between devices, local(): lax.all_gather(matrix, 'col', axis=1, tiled=True)  58.2 us
    all_gather x1, waiting for transfers between devices, local(): lax.all_gather(square_half, 'col', axis=1, tiled=True)  51.6 us
    dot_general x1, matrix products, local(): jnp.dot(lax.all_gather(matrix, 'col', axis=1, tiled=True), lower, preferr...  12.7 us
    dot_general x1, matrix products, local(): jnp.dot(lax.all_gather(square_half, 'col', axis=1, tiled=True), lower, pr...  12.5 us
  transfers between devices with their start and end apart: 3, of which 3 were waited for; matrix products, arithmetic and copies ran while one was open for 0% of the time, Pallas kernels for 0%

commit v1 on v0

v1 whole, which is shorter than its diff:
```python
import jax
import jax.numpy as jnp
from jax import lax
from jax.experimental import pallas as pl
from jax.experimental.pallas import tpu as pltpu
from jax.sharding import PartitionSpec as P

TILE = 256
SLOTS = 13
BOTH = ("row", "col")
VMEM_LIMIT = 48 * 1024 * 1024


def in_vmem(count):
    return [pl.BlockSpec(memory_space=pltpu.VMEM)] * count


def in_smem(count):
    return [pl.BlockSpec(memory_space=pltpu.SMEM)] * count


def params():
    return pltpu.CompilerParams(vmem_limit_bytes=VMEM_LIMIT)


SIZES = dict(z=8, y_hi=2, core=2, y_lo=2, x=4)


def shift_pairs(**steps):
    pairs = []
    for source in range(256):
        at, rest = {}, source
        for name in ("x", "y_lo", "core", "y_hi", "z"):
            at[name] = rest % SIZES[name]
            rest //= SIZES[name]
        for name, step in steps.items():
            at[name] = (at[name] + step) % SIZES[name]
        target = 0
        for name in ("z", "y_hi", "core", "y_lo", "x"):
            target = target * SIZES[name] + at[name]
        pairs.append((source, target))
    return pairs


def move(block, **steps):
    return lax.ppermute(block, BOTH, shift_pairs(**steps))


def spread_col(block):
    moved = []
    for y_step in (0, 1):
        for x_step in (1, 3, 2, 0):
            if y_step or x_step:
                moved.append((move(block, y_lo=y_step, x=x_step), y_step, x_step))
    return moved


COL_STEPS = [(y, x) for y in (0, 1) for x in (1, 3, 2, 0) if y or x]


def col_source(col, y_step, x_step):
    y_lo, x = col // 4, col % 4
    return ((y_lo + 2 - y_step) % 2) * 4 + (x + 4 - x_step) % 4


def table_kernel(pattern_ref, perm_ref, table_ref):
    count = pattern_ref.shape[0]
    first = lax.broadcasted_iota(jnp.int32, (count, count), 0)
    second = lax.broadcasted_iota(jnp.int32, (count, count), 1)
    pattern = pattern_ref[...].astype(jnp.float32)
    one_hot = (perm_ref[...] == second).astype(jnp.float32)
    upper = jnp.where(first <= second, pattern, 0.0)
    strict = jnp.where(first < second, pattern, 0.0)

    def dot(a, b, b_dim):
        return lax.dot_general(
            a, b, (((1,), (b_dim,)), ((), ())), preferred_element_type=jnp.float32
        )

    mask = dot(dot(one_hot, upper, 0) + dot(one_hot, strict, 1), one_hot, 1)
    rank = dot(mask, (first < second).astype(jnp.float32), 0).astype(jnp.int32)
    slot = jnp.where(mask > 0.5, rank, -1)
    table_ref[:, :count] = slot
    lane = lax.broadcasted_iota(jnp.int32, (count, count), 1)
    order = jnp.zeros((count, count), jnp.int32)
    for place in range(SLOTS):
        tile = jnp.sum(jnp.where(slot == place, second, 0), axis=1, keepdims=True)
        order = jnp.where(lane == place, tile, order)
    ones = jnp.sum((slot >= 0).astype(jnp.int32), axis=1, keepdims=True)
    order = jnp.where(lane == SLOTS, ones, order)
    table_ref[:, count:] = order


def tables(pattern, tile_perm):
    count = pattern.shape[0]
    return pl.pallas_call(
        table_kernel,
        out_shape=jax.ShapeDtypeStruct((count, 2 * count), jnp.int32),
        in_specs=in_vmem(2),
        out_specs=pl.BlockSpec(memory_space=pltpu.VMEM),
    )(pattern, tile_perm[:, None])


def pack_kernel(table_ref, strips_ref, packed_ref):
    count = table_ref.shape[0]
    row = lax.axis_index("row")
    per_col = strips_ref.shape[2] // TILE
    ones = table_ref[row, count + SLOTS]
    for place in range(SLOTS):
        tile = table_ref[row, count + place]
        start = pl.multiple_of((tile % per_col) * TILE, TILE)
        block = strips_ref[tile // per_col, :, pl.ds(start, TILE)]
        packed_ref[:, place * TILE : (place + 1) * TILE] = jnp.where(
            place < ones, block, jnp.zeros_like(block)
        )


def pack(table, strips):
    depth = strips.shape[1]
    return pl.pallas_call(
        pack_kernel,
        out_shape=jax.ShapeDtypeStruct((depth, SLOTS * TILE), strips.dtype),
        in_specs=in_smem(1) + in_vmem(1),
        out_specs=pl.BlockSpec(memory_space=pltpu.VMEM),
        compiler_params=params(),
    )(table, strips)


def square_kernel(table_ref, *refs, places):
    pieces, blocks = refs[:8], refs[8:40]
    half_ref, low_ref, factor_ref, band = refs[40:]
    count = table_ref.shape[0]
    row, col = lax.axis_index("row"), lax.axis_index("col")
    z, y_hi, core = row // 4, (row // 2) % 2, row % 2
    depth = pieces[0].shape[0]
    for piece, (y_step, x_step) in zip(pieces, [(0, 0)] + COL_STEPS):
        strip = col_source(col, y_step, x_step)
        band[pl.ds(pl.multiple_of(strip * depth, depth), depth), :] = piece[...]
    factor_ref[...] = jnp.zeros_like(factor_ref)
    ones = table_ref[row, count + SLOTS]
    for block, (z_step, y_step, core_step) in zip(blocks, places):
        other = ((z + 8 - z_step) % 8) * 4 + ((y_hi + y_step) % 2) * 2 + (core + core_step) % 2
        place = table_ref[row, other]

        @pl.when(place >= 0)
        def _():
            start = pl.multiple_of(place * depth, depth)

            def copy(inner, _):
                slot = table_ref[other, table_ref[row, count + inner]]

                @pl.when(slot >= 0)
                def _():
                    factor_ref[
                        pl.ds(start, depth), pl.ds(pl.multiple_of(inner * TILE, TILE), TILE)
                    ] = block[:, pl.ds(pl.multiple_of(slot * TILE, TILE), TILE)]

                return 0

            lax.fori_loop(0, ones, copy, 0)

    square = lax.dot_general(
        factor_ref[...], band[...], (((1,), (1,)), ((), ())), preferred_element_type=jnp.float32
    )
    half = square.astype(jnp.bfloat16)
    half_ref[...] = half
    low_ref[...] = (square - half.astype(jnp.float32)).astype(jnp.bfloat16)


def square_strips(table, pieces, blocks, places):
    depth, width = pieces[0].shape
    strip = jax.ShapeDtypeStruct((SLOTS * depth, TILE), jnp.bfloat16)
    return pl.pallas_call(
        lambda *refs: square_kernel(*refs, places=places),
        out_shape=(strip, strip, jax.ShapeDtypeStruct((SLOTS * depth, width), jnp.bfloat16)),
        in_specs=in_smem(1) + in_vmem(40),
        out_specs=[pl.BlockSpec(memory_space=pltpu.VMEM)] * 3,
        scratch_shapes=[pltpu.VMEM((TILE, width), jnp.bfloat16)],
        compiler_params=params(),
    )(table, *pieces, *blocks)


def cube_kernel(table_ref, factor_ref, low_ref, *refs, scale):
    pieces, (sent_ref, whole, total) = refs[:8], refs[8:]
    count = table_ref.shape[0]
    row, col = lax.axis_index("row"), lax.axis_index("col")
    depth = factor_ref.shape[0] // SLOTS
    for piece, (y_step, x_step) in zip(pieces, [(0, 0)] + COL_STEPS):
        strip = col_source(col, y_step, x_step)
        for place in range(SLOTS):
            start = pl.multiple_of(place * TILE + strip * depth, depth)
            whole[pl.ds(start, depth), :] = piece[place * depth : (place + 1) * depth, :]
    total[...] = scale * jnp.dot(
        factor_ref[...], whole[...], preferred_element_type=jnp.float32
    )
    per_col = sent_ref.shape[1] // 3
    for tile in range(count):
        place = table_ref[row, tile]
        start = pl.multiple_of(jnp.maximum(place, 0) * depth, depth)
        cube = jnp.where(place >= 0, total[pl.ds(start, depth), :], 0.0)
        low = low_ref[pl.ds(start, depth), :]
        high = cube.astype(jnp.bfloat16)
        to, spot = tile // per_col, tile % per_col
        sent_ref[to, spot] = high
        sent_ref[to, per_col + spot] = (cube - high.astype(jnp.float32)).astype(jnp.bfloat16)
        sent_ref[to, 2 * per_col + spot] = jnp.where(place >= 0, low, jnp.zeros_like(low))


def cube_strips(table, factor, low, pieces, per_col, cols, scale):
    depth = factor.shape[0] // SLOTS
    return pl.pallas_call(
        lambda *refs: cube_kernel(*refs, scale=scale),
        out_shape=jax.ShapeDtypeStruct((cols, 3 * per_col, depth, TILE), jnp.bfloat16),
        in_specs=in_smem(1) + in_vmem(10),
        out_specs=pl.BlockSpec(memory_space=pltpu.VMEM),
        scratch_shapes=[
            pltpu.VMEM((SLOTS * TILE, TILE), jnp.bfloat16),
            pltpu.VMEM((SLOTS * depth, TILE), jnp.float32),
        ],
        compiler_params=params(),
    )(table, factor, low, *pieces)


def home_kernel(table_ref, got_ref, *refs):
    pieces, (square_ref, cubed_ref, held) = refs[:8], refs[8:]
    row, col = lax.axis_index("row"), lax.axis_index("col")
    cols, _, depth, _ = got_ref.shape
    per_col = square_ref.shape[1] // TILE
    for spot in range(per_col):
        columns = slice(spot * TILE, (spot + 1) * TILE)
        for strip in range(cols):
            held[strip * depth : (strip + 1) * depth, :] = got_ref[strip, spot].astype(
                jnp.float32
            ) + got_ref[strip, per_col + spot].astype(jnp.float32)
        cubed_ref[:, columns] = held[...].T
        place = table_ref[row, col * per_col + spot]
        start = pl.multiple_of(jnp.maximum(place, 0) * depth, depth)
        for piece, (y_step, x_step) in zip(pieces, [(0, 0)] + COL_STEPS):
            strip = col_source(col, y_step, x_step)
            high = piece[pl.ds(start, depth), :].astype(jnp.float32)
            low = got_ref[strip, 2 * per_col + spot].astype(jnp.float32)
            held[pl.ds(pl.multiple_of(strip * depth, depth), depth), :] = jnp.where(
                place >= 0, high + low, 0.0
            )
        square_ref[:, columns] = held[...].T


def home(table, got, pieces, shape):
    out = jax.ShapeDtypeStruct(shape, jnp.float32)
    return pl.pallas_call(
        home_kernel,
        out_shape=(out, out),
        in_specs=in_smem(1) + in_vmem(9),
        out_specs=[pl.BlockSpec(memory_space=pltpu.VMEM)] * 2,
        scratch_shapes=[pltpu.VMEM((TILE, TILE), jnp.float32)],
        compiler_params=params(),
    )(table, got, *pieces)


def local(density, pattern, tile_perm):
    rows, columns = density.shape
    cols = lax.axis_size("col")
    per_col = columns // TILE
    table = tables(pattern, tile_perm)
    strips = lax.all_to_all(
        density.reshape(cols, rows // cols, columns), "col", split_axis=0, concat_axis=0
    )
    packed = pack(table, strips)
    pieces = [packed] + [block for block, _, _ in spread_col(packed)]
    blocks, places = [packed], [(0, 0, 0)]
    across = move(packed, y_hi=1)
    up, down = packed, packed
    up_across, down_across = across, across
    blocks.append(across)
    places.append((0, 1, 0))
    for step in (1, 2, 3, 4):
        up = move(up, z=1)
        blocks.append(up)
        places.append((step, 0, 0))
        down_across = move(down_across, z=-1)
        blocks.append(down_across)
        places.append((-step, 1, 0))
        if step < 4:
            down = move(down, z=-1)
            blocks.append(down)
            places.append((-step, 0, 0))
            up_across = move(up_across, z=1)
            blocks.append(up_across)
            places.append((step, 1, 0))
    swapped = [move(block, core=1) for block in blocks]
    places = places + [(z, y, 1) for z, y, _ in places]
    half, low, factor = square_strips(table, pieces, blocks + swapped, places)
    pieces = [half] + [block for block, _, _ in spread_col(half)]
    scale = (rows * lax.axis_size("row") / 2.0) ** (-0.25)
    sent = cube_strips(table, factor, low, pieces, per_col, cols, scale)
    got = lax.all_to_all(sent, "col", split_axis=0, concat_axis=0)
    return home(table, got, pieces, (rows, columns))


def solution(mesh):
    return jax.shard_map(
        local,
        mesh=mesh,
        in_specs=(P("row", "col"), P(), P()),
        out_specs=(P("row", "col"), P("row", "col")),
        check_vma=False,
    )
```

time: 295 us -> 165 us (0.56)
  waiting for transfers between devices: 251 us -> 53.8 us
  starting transfers between devices: 0.12 us -> 68.5 us
  matrix products: 27 us -> 0 us
  blocking collectives: 0 us -> 22.5 us
  Pallas kernels: 0 us -> 14.5 us
  between operations: 13.8 us -> 0.81 us
    all_gather x3 -> x0, waiting for transfers between devices: 250 us -> none  [the longest x1 140 us: local(): column = lax.all_gather(matrix, 'row', axis=0, tiled=True)]
    ppermute x0 -> x45, starting transfers between devices: none -> 62.6 us  [move(): return lax.ppermute(block, BOTH, shift_pairs(**steps))]
    ppermute x0 -> x45, waiting for transfers between devices: none -> 46.9 us  [move(): return lax.ppermute(block, BOTH, shift_pairs(**steps))]
    dot_general x4 -> x0, matrix products: 27 us -> none  [the longest x1 12.7 us: local(): jnp.dot(lax.all_gather(matrix, 'col', axis=1, tiled=True), lower, preferr...]
    all_to_all x0 -> x1, blocking collectives: none -> 22.5 us  [local(): got = lax.all_to_all(sent, 'col', split_axis=0, concat_axis=0)]
    pallas_call x0 -> x5, Pallas kernels: none -> 14.5 us  [the longest x1 5.85 us: square_strips(): pl.pallas_call(lambda *refs: square_kernel(*refs, places=places), out_sha...]
    all_to_all x0 -> x1, waiting for transfers between devices: none -> 6.82 us  [local(): lax.all_to_all(density.reshape(cols, rows // cols, columns), 'col', split...]
    all_to_all x0 -> x1, starting transfers between devices: none -> 5.87 us  [local(): lax.all_to_all(density.reshape(cols, rows // cols, columns), 'col', split...]
  transfers between devices with their start and end apart: 3 -> 46, of which waited for: 3 -> 16; matrix products, arithmetic and copies ran while one was open for 0% -> 1% of each run, Pallas kernels for 0% -> 1%
where the time goes in v1:
time: 165 us; the launch traced here: 163 us
  starting transfers between devices  68.5 us (42%)
  waiting for transfers between devices  53.8 us (33%)
  blocking collectives  22.5 us (14%)
  Pallas kernels  14.5 us (9%)
  local copies, waits for them, and re-layouts  3.09 us (2%)
    ppermute x45, starting transfers between devices, move(): return lax.ppermute(block, BOTH, shift_pairs(**steps))  62.6 us
    ppermute x45, waiting for transfers between devices, move(): return lax.ppermute(block, BOTH, shift_pairs(**steps))  46.9 us
    all_to_all x1, blocking collectives, local(): got = lax.all_to_all(sent, 'col', split_axis=0, concat_axis=0)  22.5 us
    all_to_all x1, waiting for transfers between devices, local(): lax.all_to_all(density.reshape(cols, rows // cols, columns), 'col', split...  6.82 us
    all_to_all x1, starting transfers between devices, local(): lax.all_to_all(density.reshape(cols, rows // cols, columns), 'col', split...  5.87 us
    pallas_call x1, Pallas kernels, square_strips(): pl.pallas_call(lambda *refs: square_kernel(*refs, places=places), out_sha...  5.85 us
  transfers between devices with their start and end apart: 46, of which 16 were waited for; matrix products, arithmetic and copies ran while one was open for 1% of the time, Pallas kernels for 1%

profile of v1, /device:TPU:1, one launch (start us, length us, event | category | flops | bytes accessed | tf_op | source)
XLA Modules:
  0.0 163.2 jit_solution(1228430183315161078)
XLA Ops:
  0.6 5.9 %all-to-all-start = ((bf16[8,32,1024]{2,1,0:T(8,128)(2,1)}), bf16[8,32,1024]{2,1,0:T(8,128)(2,1)S(1)}, u32[]{:S(2)}, u32[]{:S(2)}) async-start(bf16[8,32,1024]{2,1,0:T(8,128)(2,1)} %bitcast.2), calls=%async_computation | async-start | bytes 1048576 | tf_op jit(solution)/shard_map/all_to_all | solution.py:265
  7.8 2.0 %shard_map.50.table_ref.refs_0_ = s32[32,64]{1,0:T(8,128)} custom-call(s32[32,32]{1,0:T(8,128)} %pattern_ref.1, s32[32,1]{1,0:T(8,128)} %copy.5.perm_ref), custom_call_target="tpu_custom_call" | custom-call | tf_op jit(solution)/shard_map/pallas_call | solution.py:96
  9.9 6.8 %all-to-all-done.strips_ref = bf16[8,32,1024]{2,1,0:T(8,128)(2,1)S(1)} async-done(((bf16[8,32,1024]{2,1,0:T(8,128)(2,1)}), bf16[8,32,1024]{2,1,0:T(8,128)(2,1)S(1)}, u32[]{:S(2)}, u32[]{:S(2)}) %all-to-all-start) | async-done | bytes 524320 | tf_op jit(solution)/shard_map/all_to_all | solution.py:265
  19.3 5.6 %collective-permute-start.10 = (bf16[32,3328]{1,0:T(8,128)(2,1)S(1)}, bf16[32,3328]{1,0:T(8,128)(2,1)S(1)}, u32[]{:S(2)}, u32[]{:S(2)}) collective-permute-start(bf16[32,3328]{1,0:T(8,128)(2,1)S(1)} %shard_map.51.refs_1_.refs_9_), channel_id=1, source_target_pairs={{0,224},{1,225},{2,226},{3,227},{4,228},{5,229},{6,230},{7,231},{8... | collective-permute-start | bytes 638984 | tf_op jit(solution)/shard_map/ppermute | solution.py:46
  24.9 2.6 %collective-permute-start.7 = (bf16[32,3328]{1,0:T(8,128)(2,1)S(1)}, bf16[32,3328]{1,0:T(8,128)(2,1)S(1)}, u32[]{:S(2)}, u32[]{:S(2)}) collective-permute-start(bf16[32,3328]{1,0:T(8,128)(2,1)S(1)} %shard_map.51.refs_1_.refs_9_), channel_id=1, source_target_pairs={{0,16},{1,17},{2,18},{3,19},{4,20},{5,21},{6,22},{7,23},{8,24},{9,... | collective-permute-start | bytes 638984 | tf_op jit(solution)/shard_map/ppermute | solution.py:46
  27.5 1.8 %collective-permute-start.5 = (bf16[32,3328]{1,0:T(8,128)(2,1)S(1)}, bf16[32,3328]{1,0:T(8,128)(2,1)S(1)}, u32[]{:S(2)}, u32[]{:S(2)}) collective-permute-start(bf16[32,3328]{1,0:T(8,128)(2,1)S(1)} %shard_map.51.refs_1_.refs_9_), channel_id=1, source_target_pairs={{0,6},{1,7},{2,4},{3,5},{4,2},{5,3},{6,0},{7,1},{8,14},{9,15},{10,... | collective-permute-start | bytes 638984 | tf_op jit(solution)/shard_map/ppermute | solution.py:46
  29.5 1.9 %collective-permute-start.4 = (bf16[32,3328]{1,0:T(8,128)(2,1)S(1)}, bf16[32,3328]{1,0:T(8,128)(2,1)S(1)}, u32[]{:S(2)}, u32[]{:S(2)}) collective-permute-start(bf16[32,3328]{1,0:T(8,128)(2,1)S(1)} %shard_map.51.refs_1_.refs_9_), channel_id=1, source_target_pairs={{0,7},{1,4},{2,5},{3,6},{4,3},{5,0},{6,1},{7,2},{8,15},{9,12},{10,... | collective-permute-start | bytes 638984 | tf_op jit(solution)/shard_map/ppermute | solution.py:46
  33.1 1.8 %collective-permute-start.2 = (bf16[32,3328]{1,0:T(8,128)(2,1)S(1)}, bf16[32,3328]{1,0:T(8,128)(2,1)S(1)}, u32[]{:S(2)}, u32[]{:S(2)}) collective-permute-start(bf16[32,3328]{1,0:T(8,128)(2,1)S(1)} %shard_map.51.refs_1_.refs_9_), channel_id=1, source_target_pairs={{0,2},{1,3},{2,0},{3,1},{4,6},{5,7},{6,4},{7,5},{8,10},{9,11},{10,... | collective-permute-start | bytes 638984 | tf_op jit(solution)/shard_map/ppermute | solution.py:46
  34.9 15.5 %collective-permute-done.6.refs_8_ = bf16[32,3328]{1,0:T(8,128)(2,1)S(1)} collective-permute-done((bf16[32,3328]{1,0:T(8,128)(2,1)S(1)}, bf16[32,3328]{1,0:T(8,128)(2,1)S(1)}, u32[]{:S(2)}, u32[]{:S(2)}) %collective-permute-start.6) | collective-permute-done | bytes 213024 | tf_op jit(solution)/shard_map/ppermute | solution.py:46
  51.9 1.7 %collective-permute-start.26 = (bf16[32,3328]{1,0:T(8,128)(2,1)S(1)}, bf16[32,3328]{1,0:T(8,128)(2,1)S(1)}, u32[]{:S(2)}, u32[]{:S(2)}) collective-permute-start(bf16[32,3328]{1,0:T(8,128)(2,1)S(1)} %collective-permute-done.10.refs_13_), channel_id=1, source_target_pairs={{0,8},{1,9},{2,10},{3,11},{4,12},{5,13},{6,14},{7,15},{8,0},{9,1},... | collective-permute-start | bytes 638984 | tf_op jit(solution)/shard_map/ppermute | solution.py:46
  53.7 2.7 %collective-permute-start.14 = (bf16[32,3328]{1,0:T(8,128)(2,1)S(1)}, bf16[32,3328]{1,0:T(8,128)(2,1)S(1)}, u32[]{:S(2)}, u32[]{:S(2)}) collective-permute-start(bf16[32,3328]{1,0:T(8,128)(2,1)S(1)} %collective-permute-done.10.refs_13_), channel_id=1, source_target_pairs={{0,224},{1,225},{2,226},{3,227},{4,228},{5,229},{6,230},{7,231},{8... | collective-permute-start | bytes 638984 | tf_op jit(solution)/shard_map/ppermute | solution.py:46
  57.3 2.2 %collective-permute-done.refs_2_ = bf16[32,3328]{1,0:T(8,128)(2,1)S(1)} collective-permute-done((bf16[32,3328]{1,0:T(8,128)(2,1)S(1)}, bf16[32,3328]{1,0:T(8,128)(2,1)S(1)}, u32[]{:S(2)}, u32[]{:S(2)}) %collective-permute-start) | collective-permute-done | bytes 213024 | tf_op jit(solution)/shard_map/ppermute | solution.py:46
  61.2 3.2 %collective-permute-start.9 = (bf16[32,3328]{1,0:T(8,128)(2,1)S(1)}, bf16[32,3328]{1,0:T(8,128)(2,1)S(1)}, u32[]{:S(2)}, u32[]{:S(2)}) collective-permute-start(bf16[32,3328]{1,0:T(8,128)(2,1)S(1)} %collective-permute-done.7.refs_10_), channel_id=1, source_target_pairs={{0,224},{1,225},{2,226},{3,227},{4,228},{5,229},{6,230},{7,231},{8... | collective-permute-start | bytes 638984 | tf_op jit(solution)/shard_map/ppermute | solution.py:46
  67.0 3.1 %collective-permute-start.28 = (bf16[32,3328]{1,0:T(8,128)(2,1)S(1)}, bf16[32,3328]{1,0:T(8,128)(2,1)S(1)}, u32[]{:S(2)}, u32[]{:S(2)}) collective-permute-start(bf16[32,3328]{1,0:T(8,128)(2,1)S(1)} %collective-permute-done.12.refs_15_), channel_id=1, source_target_pairs={{0,8},{1,9},{2,10},{3,11},{4,12},{5,13},{6,14},{7,15},{8,0},{9,1},... | collective-permute-start | bytes 638984 | tf_op jit(solution)/shard_map/ppermute | solution.py:46
  70.4 2.7 %collective-permute-start.13 = (bf16[32,3328]{1,0:T(8,128)(2,1)S(1)}, bf16[32,3328]{1,0:T(8,128)(2,1)S(1)}, u32[]{:S(2)}, u32[]{:S(2)}) collective-permute-start(bf16[32,3328]{1,0:T(8,128)(2,1)S(1)} %collective-permute-done.9.refs_12_), channel_id=1, source_target_pairs={{0,224},{1,225},{2,226},{3,227},{4,228},{5,229},{6,230},{7,231},{8... | collective-permute-start | bytes 638984 | tf_op jit(solution)/shard_map/ppermute | solution.py:46
  73.1 1.9 %collective-permute-start.27 = (bf16[32,3328]{1,0:T(8,128)(2,1)S(1)}, bf16[32,3328]{1,0:T(8,128)(2,1)S(1)}, u32[]{:S(2)}, u32[]{:S(2)}) collective-permute-start(bf16[32,3328]{1,0:T(8,128)(2,1)S(1)} %collective-permute-done.11.refs_14_), channel_id=1, source_target_pairs={{0,8},{1,9},{2,10},{3,11},{4,12},{5,13},{6,14},{7,15},{8,0},{9,1},... | collective-permute-start | bytes 638984 | tf_op jit(solution)/shard_map/ppermute | solution.py:46
  75.1 1.9 %collective-permute-done.16.refs_19_ = bf16[32,3328]{1,0:T(8,128)(2,1)S(1)} collective-permute-done((bf16[32,3328]{1,0:T(8,128)(2,1)S(1)}, bf16[32,3328]{1,0:T(8,128)(2,1)S(1)}, u32[]{:S(2)}, u32[]{:S(2)}) %collective-permute-start.16) | collective-permute-done | bytes 213024 | tf_op jit(solution)/shard_map/ppermute | solution.py:46
  77.0 2.2 %collective-permute-start.34 = (bf16[32,3328]{1,0:T(8,128)(2,1)S(1)}, bf16[32,3328]{1,0:T(8,128)(2,1)S(1)}, u32[]{:S(2)}, u32[]{:S(2)}) collective-permute-start(bf16[32,3328]{1,0:T(8,128)(2,1)S(1)} %collective-permute-done.18.refs_21_), channel_id=1, source_target_pairs={{0,8},{1,9},{2,10},{3,11},{4,12},{5,13},{6,14},{7,15},{8,0},{9,1},... | collective-permute-start | bytes 638984 | tf_op jit(solution)/shard_map/ppermute | solution.py:46
  80.5 2.3 %collective-permute-start.32 = (bf16[32,3328]{1,0:T(8,128)(2,1)S(1)}, bf16[32,3328]{1,0:T(8,128)(2,1)S(1)}, u32[]{:S(2)}, u32[]{:S(2)}) collective-permute-start(bf16[32,3328]{1,0:T(8,128)(2,1)S(1)} %collective-permute-done.16.refs_19_), channel_id=1, source_target_pairs={{0,8},{1,9},{2,10},{3,11},{4,12},{5,13},{6,14},{7,15},{8,0},{9,1},... | collective-permute-start | bytes 638984 | tf_op jit(solution)/shard_map/ppermute | solution.py:46
  83.9 2.3 %collective-permute-done.17.refs_20_ = bf16[32,3328]{1,0:T(8,128)(2,1)S(1)} collective-permute-done((bf16[32,3328]{1,0:T(8,128)(2,1)S(1)}, bf16[32,3328]{1,0:T(8,128)(2,1)S(1)}, u32[]{:S(2)}, u32[]{:S(2)}) %collective-permute-start.17) | collective-permute-done | bytes 213024 | tf_op jit(solution)/shard_map/ppermute | solution.py:46
  86.9 2.9 %collective-permute-start.29 = (bf16[32,3328]{1,0:T(8,128)(2,1)S(1)}, bf16[32,3328]{1,0:T(8,128)(2,1)S(1)}, u32[]{:S(2)}, u32[]{:S(2)}) collective-permute-start(bf16[32,3328]{1,0:T(8,128)(2,1)S(1)} %collective-permute-done.13.refs_16_), channel_id=1, source_target_pairs={{0,8},{1,9},{2,10},{3,11},{4,12},{5,13},{6,14},{7,15},{8,0},{9,1},... | collective-permute-start | bytes 638984 | tf_op jit(solution)/shard_map/ppermute | solution.py:46
  89.8 3.4 %collective-permute-start.33 = (bf16[32,3328]{1,0:T(8,128)(2,1)S(1)}, bf16[32,3328]{1,0:T(8,128)(2,1)S(1)}, u32[]{:S(2)}, u32[]{:S(2)}) collective-permute-start(bf16[32,3328]{1,0:T(8,128)(2,1)S(1)} %collective-permute-done.17.refs_20_), channel_id=1, source_target_pairs={{0,8},{1,9},{2,10},{3,11},{4,12},{5,13},{6,14},{7,15},{8,0},{9,1},... | collective-permute-start | bytes 638984 | tf_op jit(solution)/shard_map/ppermute | solution.py:46
  94.2 2.0 %collective-permute-start.35 = (bf16[32,3328]{1,0:T(8,128)(2,1)S(1)}, bf16[32,3328]{1,0:T(8,128)(2,1)S(1)}, u32[]{:S(2)}, u32[]{:S(2)}) collective-permute-start(bf16[32,3328]{1,0:T(8,128)(2,1)S(1)} %collective-permute-done.19.refs_22_), channel_id=1, source_target_pairs={{0,8},{1,9},{2,10},{3,11},{4,12},{5,13},{6,14},{7,15},{8,0},{9,1},... | collective-permute-start | bytes 638984 | tf_op jit(solution)/shard_map/ppermute | solution.py:46
  98.7 5.9 %shard_map.52 = (bf16[416,256]{1,0:T(8,128)(2,1)S(1)}, bf16[416,256]{1,0:T(8,128)(2,1)S(1)}, bf16[416,3328]{1,0:T(8,128)(2,1)}) custom-call(s32[32,64]{1,0:T(8,128)S(1)} %copy-done, bf16[32,3328]{1,0:T(8,128)(2,1)S(1)} %shard_map.51.refs_1_.refs_9_, bf16[32,3328]{1,0:T(8,128)(2,1)S(1)} %collective-permute-done.refs_2_, ...), custom_call_target="tpu_custom_call" | custom-call | tf_op jit(solution)/shard_map/pallas_call | solution.py:173
  107.3 3.7 %collective-permute-start.42 = (bf16[416,256]{1,0:T(8,128)(2,1)S(1)}, bf16[416,256]{1,0:T(8,128)(2,1)S(1)}, u32[]{:S(2)}, u32[]{:S(2)}) collective-permute-start(bf16[416,256]{1,0:T(8,128)(2,1)S(1)} %get-tuple-element.7.refs_3_.refs_0_), channel_id=1, source_target_pairs={{0,7},{1,4},{2,5},{3,6},{4,3},{5,0},{6,1},{7,2},{8,15},{9,12},{10,... | collective-permute-start | bytes 638984 | tf_op jit(solution)/shard_map/ppermute | solution.py:46
  112.1 13.5 %collective-permute-done.44.refs_10_.refs_7_ = bf16[416,256]{1,0:T(8,128)(2,1)S(1)} collective-permute-done((bf16[416,256]{1,0:T(8,128)(2,1)S(1)}, bf16[416,256]{1,0:T(8,128)(2,1)S(1)}, u32[]{:S(2)}, u32[]{:S(2)}) %collective-permute-start.44) | collective-permute-done | bytes 213024 | tf_op jit(solution)/shard_map/ppermute | solution.py:46
  125.7 2.1 %collective-permute-start.39 = (bf16[416,256]{1,0:T(8,128)(2,1)S(1)}, bf16[416,256]{1,0:T(8,128)(2,1)S(1)}, u32[]{:S(2)}, u32[]{:S(2)}) collective-permute-start(bf16[416,256]{1,0:T(8,128)(2,1)S(1)} %get-tuple-element.7.refs_3_.refs_0_), channel_id=1, source_target_pairs={{0,3},{1,0},{2,1},{3,2},{4,7},{5,4},{6,5},{7,6},{8,11},{9,8},{10,9... | collective-permute-start | bytes 638984 | tf_op jit(solution)/shard_map/ppermute | solution.py:46
  128.9 3.4 %collective-permute-done.39.refs_5_.refs_2_ = bf16[416,256]{1,0:T(8,128)(2,1)S(1)} collective-permute-done((bf16[416,256]{1,0:T(8,128)(2,1)S(1)}, bf16[416,256]{1,0:T(8,128)(2,1)S(1)}, u32[]{:S(2)}, u32[]{:S(2)}) %collective-permute-start.39) | collective-permute-done | bytes 213024 | tf_op jit(solution)/shard_map/ppermute | solution.py:46
  132.3 2.7 %collective-permute-done.38.refs_4_.refs_1_ = bf16[416,256]{1,0:T(8,128)(2,1)S(1)} collective-permute-done((bf16[416,256]{1,0:T(8,128)(2,1)S(1)}, bf16[416,256]{1,0:T(8,128)(2,1)S(1)}, u32[]{:S(2)}, u32[]{:S(2)}) %collective-permute-start.38) | collective-permute-done | bytes 213024 | tf_op jit(solution)/shard_map/ppermute | solution.py:46
  135.0 3.0 %shard_map.53 = bf16[8,12,32,256]{3,2,1,0:T(8,128)(2,1)S(1)} custom-call(s32[32,64]{1,0:T(8,128)S(1)} %copy-done, bf16[416,3328]{1,0:T(8,128)(2,1)} %get-tuple-element.5.refs_1_, bf16[416,256]{1,0:T(8,128)(2,1)S(1)} %get-tuple-element.6.refs_2_, bf16[416,256]{1,0:T(8,128)(2,1)S(1)} %get-tuple-element.7.refs_3_.refs_0_, ...), custom_call_target="tpu_custom_call" | custom-call | tf_op jit(solution)/shard_map/pallas_call | solution.py:211
  138.0 22.5 %all_to_all.10.got_ref = bf16[8,12,32,256]{3,2,1,0:T(8,128)(2,1)S(1)} all-to-all(bf16[8,12,32,256]{3,2,1,0:T(8,128)(2,1)S(1)} %shard_map.53), channel_id=1, replica_groups=mesh['row'=32,'col'=8] {'col'}, dimensions={0} | all-to-all | bytes 3145728 | tf_op jit(solution)/shard_map/all_to_all | solution.py:296
  160.5 2.7 %shard_map.54 = (f32[256,1024]{1,0:T(8,128)}, f32[256,1024]{1,0:T(8,128)}) custom-call(s32[32,64]{1,0:T(8,128)S(1)} %copy-done, bf16[8,12,32,256]{3,2,1,0:T(8,128)(2,1)S(1)} %all_to_all.10.got_ref, bf16[416,256]{1,0:T(8,128)(2,1)S(1)} %get-tuple-element.7.refs_3_.refs_0_, bf16[416,256]{1,0:T(8,128)(2,1)S(1)} %collective-permute-done.38.refs_4_.refs_1_, ...), custom_call_target="tpu_custom_call" | custom-call | tf_op jit(solution)/shard_map/pallas_call | solution.py:250
  (93 shorter events, 24.5 us)
Async XLA Ops:
  0.6 16.1 %all-to-all-start = ((bf16[8,32,1024]{2,1,0:T(8,128)(2,1)}), bf16[8,32,1024]{2,1,0:T(8,128)(2,1)S(1)}, u32[]{:S(2)}, u32[]{:S(2)}) async-start(bf16[8,32,1024]{2,1,0:T(8,128)(2,1)} %bitcast.2), calls=%async_computation | async-start | bytes 1048576 | tf_op jit(solution)/shard_map/all_to_all | solution.py:265
  18.3 9.2 %collective-permute-start.22 = (bf16[32,3328]{1,0:T(8,128)(2,1)S(1)}, bf16[32,3328]{1,0:T(8,128)(2,1)S(1)}, u32[]{:S(2)}, u32[]{:S(2)}) collective-permute-start(bf16[32,3328]{1,0:T(8,128)(2,1)S(1)} %shard_map.51.refs_1_.refs_9_), channel_id=1, source_target_pairs={{0,8},{1,9},{2,10},{3,11},{4,12},{5,13},{6,14},{7,15},{8,0},{9,1},... | collective-permute-start | bytes 638984 | tf_op jit(solution)/shard_map/ppermute | solution.py:46
  19.3 10.2 %collective-permute-start.10 = (bf16[32,3328]{1,0:T(8,128)(2,1)S(1)}, bf16[32,3328]{1,0:T(8,128)(2,1)S(1)}, u32[]{:S(2)}, u32[]{:S(2)}) collective-permute-start(bf16[32,3328]{1,0:T(8,128)(2,1)S(1)} %shard_map.51.refs_1_.refs_9_), channel_id=1, source_target_pairs={{0,224},{1,225},{2,226},{3,227},{4,228},{5,229},{6,230},{7,231},{8... | collective-permute-start | bytes 638984 | tf_op jit(solution)/shard_map/ppermute | solution.py:46
  24.9 7.7 %collective-permute-start.8 = (bf16[32,3328]{1,0:T(8,128)(2,1)S(1)}, bf16[32,3328]{1,0:T(8,128)(2,1)S(1)}, u32[]{:S(2)}, u32[]{:S(2)}) collective-permute-start(bf16[32,3328]{1,0:T(8,128)(2,1)S(1)} %shard_map.51.refs_1_.refs_9_), channel_id=1, source_target_pairs={{0,32},{1,33},{2,34},{3,35},{4,36},{5,37},{6,38},{7,39},{8,40},{9,... | collective-permute-start | bytes 638984 | tf_op jit(solution)/shard_map/ppermute | solution.py:46
  24.9 8.3 %collective-permute-start.7 = (bf16[32,3328]{1,0:T(8,128)(2,1)S(1)}, bf16[32,3328]{1,0:T(8,128)(2,1)S(1)}, u32[]{:S(2)}, u32[]{:S(2)}) collective-permute-start(bf16[32,3328]{1,0:T(8,128)(2,1)S(1)} %shard_map.51.refs_1_.refs_9_), channel_id=1, source_target_pairs={{0,16},{1,17},{2,18},{3,19},{4,20},{5,21},{6,22},{7,23},{8,24},{9,... | collective-permute-start | bytes 638984 | tf_op jit(solution)/shard_map/ppermute | solution.py:46
  27.5 22.9 %collective-permute-start.6 = (bf16[32,3328]{1,0:T(8,128)(2,1)S(1)}, bf16[32,3328]{1,0:T(8,128)(2,1)S(1)}, u32[]{:S(2)}, u32[]{:S(2)}) collective-permute-start(bf16[32,3328]{1,0:T(8,128)(2,1)S(1)} %shard_map.51.refs_1_.refs_9_), channel_id=1, source_target_pairs={{0,4},{1,5},{2,6},{3,7},{4,0},{5,1},{6,2},{7,3},{8,12},{9,13},{10,... | collective-permute-start | bytes 638984 | tf_op jit(solution)/shard_map/ppermute | solution.py:46
  27.5 24.1 %collective-permute-start.5 = (bf16[32,3328]{1,0:T(8,128)(2,1)S(1)}, bf16[32,3328]{1,0:T(8,128)(2,1)S(1)}, u32[]{:S(2)}, u32[]{:S(2)}) collective-permute-start(bf16[32,3328]{1,0:T(8,128)(2,1)S(1)} %shard_map.51.refs_1_.refs_9_), channel_id=1, source_target_pairs={{0,6},{1,7},{2,4},{3,5},{4,2},{5,3},{6,0},{7,1},{8,14},{9,15},{10,... | collective-permute-start | bytes 638984 | tf_op jit(solution)/shard_map/ppermute | solution.py:46
  29.5 22.4 %collective-permute-start.4 = (bf16[32,3328]{1,0:T(8,128)(2,1)S(1)}, bf16[32,3328]{1,0:T(8,128)(2,1)S(1)}, u32[]{:S(2)}, u32[]{:S(2)}) collective-permute-start(bf16[32,3328]{1,0:T(8,128)(2,1)S(1)} %shard_map.51.refs_1_.refs_9_), channel_id=1, source_target_pairs={{0,7},{1,4},{2,5},{3,6},{4,3},{5,0},{6,1},{7,2},{8,15},{9,12},{10,... | collective-permute-start | bytes 638984 | tf_op jit(solution)/shard_map/ppermute | solution.py:46
  32.6 21.1 %collective-permute-start.3 = (bf16[32,3328]{1,0:T(8,128)(2,1)S(1)}, bf16[32,3328]{1,0:T(8,128)(2,1)S(1)}, u32[]{:S(2)}, u32[]{:S(2)}) collective-permute-start(bf16[32,3328]{1,0:T(8,128)(2,1)S(1)} %shard_map.51.refs_1_.refs_9_), channel_id=1, source_target_pairs={{0,5},{1,6},{2,7},{3,4},{4,1},{5,2},{6,3},{7,0},{8,13},{9,14},{10,... | collective-permute-start | bytes 638984 | tf_op jit(solution)/shard_map/ppermute | solution.py:46
  33.1 23.2 %collective-permute-start.2 = (bf16[32,3328]{1,0:T(8,128)(2,1)S(1)}, bf16[32,3328]{1,0:T(8,128)(2,1)S(1)}, u32[]{:S(2)}, u32[]{:S(2)}) collective-permute-start(bf16[32,3328]{1,0:T(8,128)(2,1)S(1)} %shard_map.51.refs_1_.refs_9_), channel_id=1, source_target_pairs={{0,2},{1,3},{2,0},{3,1},{4,6},{5,7},{6,4},{7,5},{8,10},{9,11},{10,... | collective-permute-start | bytes 638984 | tf_op jit(solution)/shard_map/ppermute | solution.py:46
  51.6 7.9 %collective-permute-start = (bf16[32,3328]{1,0:T(8,128)(2,1)S(1)}, bf16[32,3328]{1,0:T(8,128)(2,1)S(1)}, u32[]{:S(2)}, u32[]{:S(2)}) collective-permute-start(bf16[32,3328]{1,0:T(8,128)(2,1)S(1)} %shard_map.51.refs_1_.refs_9_), channel_id=1, source_target_pairs={{0,1},{1,2},{2,3},{3,0},{4,5},{5,6},{6,7},{7,4},{8,9},{9,10},{10,1... | collective-permute-start | bytes 638984 | tf_op jit(solution)/shard_map/ppermute | solution.py:46
  51.9 9.3 %collective-permute-start.26 = (bf16[32,3328]{1,0:T(8,128)(2,1)S(1)}, bf16[32,3328]{1,0:T(8,128)(2,1)S(1)}, u32[]{:S(2)}, u32[]{:S(2)}) collective-permute-start(bf16[32,3328]{1,0:T(8,128)(2,1)S(1)} %collective-permute-done.10.refs_13_), channel_id=1, source_target_pairs={{0,8},{1,9},{2,10},{3,11},{4,12},{5,13},{6,14},{7,15},{8,0},{9,1},... | collective-permute-start | bytes 638984 | tf_op jit(solution)/shard_map/ppermute | solution.py:46
  53.7 7.5 %collective-permute-start.14 = (bf16[32,3328]{1,0:T(8,128)(2,1)S(1)}, bf16[32,3328]{1,0:T(8,128)(2,1)S(1)}, u32[]{:S(2)}, u32[]{:S(2)}) collective-permute-start(bf16[32,3328]{1,0:T(8,128)(2,1)S(1)} %collective-permute-done.10.refs_13_), channel_id=1, source_target_pairs={{0,224},{1,225},{2,226},{3,227},{4,228},{5,229},{6,230},{7,231},{8... | collective-permute-start | bytes 638984 | tf_op jit(solution)/shard_map/ppermute | solution.py:46
  56.4 8.1 %collective-permute-start.24 = (bf16[32,3328]{1,0:T(8,128)(2,1)S(1)}, bf16[32,3328]{1,0:T(8,128)(2,1)S(1)}, u32[]{:S(2)}, u32[]{:S(2)}) collective-permute-start(bf16[32,3328]{1,0:T(8,128)(2,1)S(1)} %collective-permute-done.8.refs_11_), channel_id=1, source_target_pairs={{0,8},{1,9},{2,10},{3,11},{4,12},{5,13},{6,14},{7,15},{8,0},{9,1},... | collective-permute-start | bytes 638984 | tf_op jit(solution)/shard_map/ppermute | solution.py:46
  57.3 8.5 %collective-permute-start.12 = (bf16[32,3328]{1,0:T(8,128)(2,1)S(1)}, bf16[32,3328]{1,0:T(8,128)(2,1)S(1)}, u32[]{:S(2)}, u32[]{:S(2)}) collective-permute-start(bf16[32,3328]{1,0:T(8,128)(2,1)S(1)} %collective-permute-done.8.refs_11_), channel_id=1, source_target_pairs={{0,32},{1,33},{2,34},{3,35},{4,36},{5,37},{6,38},{7,39},{8,40},{9,... | collective-permute-start | bytes 638984 | tf_op jit(solution)/shard_map/ppermute | solution.py:46
  61.2 9.2 %collective-permute-start.11 = (bf16[32,3328]{1,0:T(8,128)(2,1)S(1)}, bf16[32,3328]{1,0:T(8,128)(2,1)S(1)}, u32[]{:S(2)}, u32[]{:S(2)}) collective-permute-start(bf16[32,3328]{1,0:T(8,128)(2,1)S(1)} %collective-permute-done.7.refs_10_), channel_id=1, source_target_pairs={{0,32},{1,33},{2,34},{3,35},{4,36},{5,37},{6,38},{7,39},{8,40},{9,... | collective-permute-start | bytes 638984 | tf_op jit(solution)/shard_map/ppermute | solution.py:46
  61.2 9.2 %collective-permute-start.9 = (bf16[32,3328]{1,0:T(8,128)(2,1)S(1)}, bf16[32,3328]{1,0:T(8,128)(2,1)S(1)}, u32[]{:S(2)}, u32[]{:S(2)}) collective-permute-start(bf16[32,3328]{1,0:T(8,128)(2,1)S(1)} %collective-permute-done.7.refs_10_), channel_id=1, source_target_pairs={{0,224},{1,225},{2,226},{3,227},{4,228},{5,229},{6,230},{7,231},{8... | collective-permute-start | bytes 638984 | tf_op jit(solution)/shard_map/ppermute | solution.py:46
  64.5 8.6 %collective-permute-start.30 = (bf16[32,3328]{1,0:T(8,128)(2,1)S(1)}, bf16[32,3328]{1,0:T(8,128)(2,1)S(1)}, u32[]{:S(2)}, u32[]{:S(2)}) collective-permute-start(bf16[32,3328]{1,0:T(8,128)(2,1)S(1)} %collective-permute-done.14.refs_17_), channel_id=1, source_target_pairs={{0,8},{1,9},{2,10},{3,11},{4,12},{5,13},{6,14},{7,15},{8,0},{9,1},... | collective-permute-start | bytes 638984 | tf_op jit(solution)/shard_map/ppermute | solution.py:46
  65.8 9.1 %collective-permute-start.18 = (bf16[32,3328]{1,0:T(8,128)(2,1)S(1)}, bf16[32,3328]{1,0:T(8,128)(2,1)S(1)}, u32[]{:S(2)}, u32[]{:S(2)}) collective-permute-start(bf16[32,3328]{1,0:T(8,128)(2,1)S(1)} %collective-permute-done.14.refs_17_), channel_id=1, source_target_pairs={{0,224},{1,225},{2,226},{3,227},{4,228},{5,229},{6,230},{7,231},{8... | collective-permute-start | bytes 638984 | tf_op jit(solution)/shard_map/ppermute | solution.py:46
  67.0 8.0 %collective-permute-start.28 = (bf16[32,3328]{1,0:T(8,128)(2,1)S(1)}, bf16[32,3328]{1,0:T(8,128)(2,1)S(1)}, u32[]{:S(2)}, u32[]{:S(2)}) collective-permute-start(bf16[32,3328]{1,0:T(8,128)(2,1)S(1)} %collective-permute-done.12.refs_15_), channel_id=1, source_target_pairs={{0,8},{1,9},{2,10},{3,11},{4,12},{5,13},{6,14},{7,15},{8,0},{9,1},... | collective-permute-start | bytes 638984 | tf_op jit(solution)/shard_map/ppermute | solution.py:46
  70.4 8.9 %collective-permute-start.13 = (bf16[32,3328]{1,0:T(8,128)(2,1)S(1)}, bf16[32,3328]{1,0:T(8,128)(2,1)S(1)}, u32[]{:S(2)}, u32[]{:S(2)}) collective-permute-start(bf16[32,3328]{1,0:T(8,128)(2,1)S(1)} %collective-permute-done.9.refs_12_), channel_id=1, source_target_pairs={{0,224},{1,225},{2,226},{3,227},{4,228},{5,229},{6,230},{7,231},{8... | collective-permute-start | bytes 638984 | tf_op jit(solution)/shard_map/ppermute | solution.py:46
  74.9 7.8 %collective-permute-start.15 = (bf16[32,3328]{1,0:T(8,128)(2,1)S(1)}, bf16[32,3328]{1,0:T(8,128)(2,1)S(1)}, u32[]{:S(2)}, u32[]{:S(2)}) collective-permute-start(bf16[32,3328]{1,0:T(8,128)(2,1)S(1)} %collective-permute-done.11.refs_14_), channel_id=1, source_target_pairs={{0,32},{1,33},{2,34},{3,35},{4,36},{5,37},{6,38},{7,39},{8,40},{9,... | collective-permute-start | bytes 638984 | tf_op jit(solution)/shard_map/ppermute | solution.py:46
  75.0 7.8 %collective-permute-start.25 = (bf16[32,3328]{1,0:T(8,128)(2,1)S(1)}, bf16[32,3328]{1,0:T(8,128)(2,1)S(1)}, u32[]{:S(2)}, u32[]{:S(2)}) collective-permute-start(bf16[32,3328]{1,0:T(8,128)(2,1)S(1)} %collective-permute-done.9.refs_12_), channel_id=1, source_target_pairs={{0,8},{1,9},{2,10},{3,11},{4,12},{5,13},{6,14},{7,15},{8,0},{9,1},... | collective-permute-start | bytes 638984 | tf_op jit(solution)/shard_map/ppermute | solution.py:46
  82.8 10.5 %collective-permute-start.31 = (bf16[32,3328]{1,0:T(8,128)(2,1)S(1)}, bf16[32,3328]{1,0:T(8,128)(2,1)S(1)}, u32[]{:S(2)}, u32[]{:S(2)}) collective-permute-start(bf16[32,3328]{1,0:T(8,128)(2,1)S(1)} %collective-permute-done.15.refs_18_), channel_id=1, source_target_pairs={{0,8},{1,9},{2,10},{3,11},{4,12},{5,13},{6,14},{7,15},{8,0},{9,1},... | collective-permute-start | bytes 638984 | tf_op jit(solution)/shard_map/ppermute | solution.py:46
  83.8 10.3 %collective-permute-start.19 = (bf16[32,3328]{1,0:T(8,128)(2,1)S(1)}, bf16[32,3328]{1,0:T(8,128)(2,1)S(1)}, u32[]{:S(2)}, u32[]{:S(2)}) collective-permute-start(bf16[32,3328]{1,0:T(8,128)(2,1)S(1)} %collective-permute-done.15.refs_18_), channel_id=1, source_target_pairs={{0,32},{1,33},{2,34},{3,35},{4,36},{5,37},{6,38},{7,39},{8,40},{9,... | collective-permute-start | bytes 638984 | tf_op jit(solution)/shard_map/ppermute | solution.py:46
  86.1 10.0 %collective-permute-start.21 = (bf16[32,3328]{1,0:T(8,128)(2,1)S(1)}, bf16[32,3328]{1,0:T(8,128)(2,1)S(1)}, u32[]{:S(2)}, u32[]{:S(2)}) collective-permute-start(bf16[32,3328]{1,0:T(8,128)(2,1)S(1)} %collective-permute-done.17.refs_20_), channel_id=1, source_target_pairs={{0,224},{1,225},{2,226},{3,227},{4,228},{5,229},{6,230},{7,231},{8... | collective-permute-start | bytes 638984 | tf_op jit(solution)/shard_map/ppermute | solution.py:46
  86.9 9.3 %collective-permute-start.29 = (bf16[32,3328]{1,0:T(8,128)(2,1)S(1)}, bf16[32,3328]{1,0:T(8,128)(2,1)S(1)}, u32[]{:S(2)}, u32[]{:S(2)}) collective-permute-start(bf16[32,3328]{1,0:T(8,128)(2,1)S(1)} %collective-permute-done.13.refs_16_), channel_id=1, source_target_pairs={{0,8},{1,9},{2,10},{3,11},{4,12},{5,13},{6,14},{7,15},{8,0},{9,1},... | collective-permute-start | bytes 638984 | tf_op jit(solution)/shard_map/ppermute | solution.py:46
  104.6 21.1 %collective-permute-start.44 = (bf16[416,256]{1,0:T(8,128)(2,1)S(1)}, bf16[416,256]{1,0:T(8,128)(2,1)S(1)}, u32[]{:S(2)}, u32[]{:S(2)}) collective-permute-start(bf16[416,256]{1,0:T(8,128)(2,1)S(1)} %get-tuple-element.7.refs_3_.refs_0_), channel_id=1, source_target_pairs={{0,4},{1,5},{2,6},{3,7},{4,0},{5,1},{6,2},{7,3},{8,12},{9,13},{10,... | collective-permute-start | bytes 638984 | tf_op jit(solution)/shard_map/ppermute | solution.py:46
  106.3 21.5 %collective-permute-start.43 = (bf16[416,256]{1,0:T(8,128)(2,1)S(1)}, bf16[416,256]{1,0:T(8,128)(2,1)S(1)}, u32[]{:S(2)}, u32[]{:S(2)}) collective-permute-start(bf16[416,256]{1,0:T(8,128)(2,1)S(1)} %get-tuple-element.7.refs_3_.refs_0_), channel_id=1, source_target_pairs={{0,6},{1,7},{2,4},{3,5},{4,2},{5,3},{6,0},{7,1},{8,14},{9,15},{10,... | collective-permute-start | bytes 638984 | tf_op jit(solution)/shard_map/ppermute | solution.py:46
  107.3 20.5 %collective-permute-start.42 = (bf16[416,256]{1,0:T(8,128)(2,1)S(1)}, bf16[416,256]{1,0:T(8,128)(2,1)S(1)}, u32[]{:S(2)}, u32[]{:S(2)}) collective-permute-start(bf16[416,256]{1,0:T(8,128)(2,1)S(1)} %get-tuple-element.7.refs_3_.refs_0_), channel_id=1, source_target_pairs={{0,7},{1,4},{2,5},{3,6},{4,3},{5,0},{6,1},{7,2},{8,15},{9,12},{10,... | collective-permute-start | bytes 638984 | tf_op jit(solution)/shard_map/ppermute | solution.py:46
  110.9 16.8 %collective-permute-start.41 = (bf16[416,256]{1,0:T(8,128)(2,1)S(1)}, bf16[416,256]{1,0:T(8,128)(2,1)S(1)}, u32[]{:S(2)}, u32[]{:S(2)}) collective-permute-start(bf16[416,256]{1,0:T(8,128)(2,1)S(1)} %get-tuple-element.7.refs_3_.refs_0_), channel_id=1, source_target_pairs={{0,5},{1,6},{2,7},{3,4},{4,1},{5,2},{6,3},{7,0},{8,13},{9,14},{10,... | collective-permute-start | bytes 638984 | tf_op jit(solution)/shard_map/ppermute | solution.py:46
  110.9 17.9 %collective-permute-start.40 = (bf16[416,256]{1,0:T(8,128)(2,1)S(1)}, bf16[416,256]{1,0:T(8,128)(2,1)S(1)}, u32[]{:S(2)}, u32[]{:S(2)}) collective-permute-start(bf16[416,256]{1,0:T(8,128)(2,1)S(1)} %get-tuple-element.7.refs_3_.refs_0_), channel_id=1, source_target_pairs={{0,2},{1,3},{2,0},{3,1},{4,6},{5,7},{6,4},{7,5},{8,10},{9,11},{10,... | collective-permute-start | bytes 638984 | tf_op jit(solution)/shard_map/ppermute | solution.py:46
  (27 other events, 220.4 us)

commit v2 on v0

v2 whole, which is shorter than its diff:
```python
import functools

import jax
import jax.numpy as jnp
from jax import lax
from jax.experimental import pallas as pl
from jax.experimental.pallas import tpu as pltpu
from jax.sharding import PartitionSpec as P

TILE = 256
SLOTS = 13
BOTH = ("row", "col")
MIB = 1024 * 1024
VMEM = pl.BlockSpec(memory_space=pltpu.VMEM)
SMEM = pl.BlockSpec(memory_space=pltpu.SMEM)

Z, Y_HI, CORE, COL = 8, 2, 2, 8


def device(z, y_hi, core, col):
    return ((z % Z * Y_HI + y_hi % Y_HI) * CORE + core % CORE) * COL + col


def pairs(move):
    places = [
        (z, y_hi, core, col)
        for z in range(Z)
        for y_hi in range(Y_HI)
        for core in range(CORE)
        for col in range(COL)
    ]
    return [(device(*place), device(*move(*place))) for place in places]


def move(block, place):
    return lax.ppermute(block, BOTH, pairs(place))


def to_other_core(block):
    return move(block, lambda z, y, core, col: (z, y, core + 1, col))


def to_other_y(block):
    return move(block, lambda z, y, core, col: (z, y + 1, core, col))


def along_z(block, steps=1):
    return move(block, lambda z, y, core, col: (z + steps * (1 - 2 * core), y, core, col))


def call(kernel, out_shape, operands, tables=1, loose=0, limit=16, **options):
    held = len(operands) - tables - loose
    return pl.pallas_call(
        kernel,
        out_shape=out_shape,
        in_specs=[SMEM] * tables + [VMEM] * held + [pl.BlockSpec(memory_space=pltpu.HBM)] * loose,
        out_specs=jax.tree.map(lambda _: VMEM, out_shape),
        compiler_params=pltpu.CompilerParams(vmem_limit_bytes=limit * MIB),
        **options,
    )(*operands)


def table_kernel(pattern_ref, perm_ref, table_ref):
    count = pattern_ref.shape[0]
    first = lax.broadcasted_iota(jnp.int32, (count, count), 0)
    second = lax.broadcasted_iota(jnp.int32, (count, count), 1)
    pattern = pattern_ref[...].astype(jnp.float32)
    one_hot = (perm_ref[...] == second).astype(jnp.float32)
    upper = jnp.where(first <= second, pattern, 0.0)
    strict = jnp.where(first < second, pattern, 0.0)

    def dot(a, b, b_dim):
        return lax.dot_general(
            a, b, (((1,), (b_dim,)), ((), ())), preferred_element_type=jnp.float32
        )

    mask = dot(dot(one_hot, upper, 0) + dot(one_hot, strict, 1), one_hot, 1)
    rank = dot(mask, (first < second).astype(jnp.float32), 0).astype(jnp.int32)
    slot = jnp.where(mask > 0.5, rank, -1)
    order = jnp.zeros((count, count), jnp.int32)
    for place in range(SLOTS):
        tile = jnp.sum(jnp.where(slot == place, second, 0), axis=1, keepdims=True)
        order = jnp.where(second == place, tile, order)
    ones = jnp.sum((slot >= 0).astype(jnp.int32), axis=1, keepdims=True)
    order = jnp.where(second == SLOTS, ones, order)
    table_ref[:, :count] = slot
    table_ref[:, count:] = order


def tables(pattern, tile_perm):
    count = pattern.shape[0]
    shape = jax.ShapeDtypeStruct((count, 2 * count), jnp.int32)
    return call(table_kernel, shape, (pattern, tile_perm[:, None]), tables=0)


def place_of(row):
    return row // 4, (row // 2) % 2, row % 2


def pack_kernel(table_ref, strips_ref, packed_ref, spread_ref):
    count = table_ref.shape[0]
    row = lax.axis_index("row")
    per_col = strips_ref.shape[2] // TILE
    ones = table_ref[row, count + SLOTS]
    for place in range(SLOTS):
        tile = table_ref[row, count + place]
        start = pl.multiple_of((tile % per_col) * TILE, TILE)
        block = strips_ref[tile // per_col, :, pl.ds(start, TILE)]
        block = jnp.where(place < ones, block, jnp.zeros_like(block))
        columns = slice(place * TILE, (place + 1) * TILE)
        packed_ref[:, columns] = block
        for col in range(COL):
            spread_ref[col, :, columns] = block


def pack(table, strips):
    _, depth, _ = strips.shape
    width = SLOTS * TILE
    shapes = (
        jax.ShapeDtypeStruct((depth, width), strips.dtype),
        jax.ShapeDtypeStruct((COL, depth, width), strips.dtype),
    )
    return call(pack_kernel, shapes, (table, strips), limit=8)


def fill(table_ref, factor_ref, blocks, places, strips, arrived, fresh):
    count = table_ref.shape[0]
    depth = strips.shape[1]
    row = lax.axis_index("row")
    z, y_hi, core = place_of(row)
    ones = table_ref[row, count + SLOTS]
    jobs = []
    for block, (step, y_flip, core_flip) in zip(blocks, places):
        passed_by = core ^ core_flip
        z_of = (z + Z + step * (2 * passed_by - 1)) % Z
        for half in range(block.shape[0] // depth):
            other = (z_of * Y_HI + (y_hi ^ y_flip)) * CORE + (passed_by ^ half)
            index = len(jobs)
            fetch = pltpu.make_async_copy(
                block.at[pl.ds(half * depth, depth), :], strips.at[index], arrived.at[index]
            )
            jobs.append((table_ref[row, other], other, fetch))
    for place, _, fetch in jobs:
        pl.when(place >= 0)(fetch.start)
    if fresh:
        factor_ref[...] = jnp.zeros_like(factor_ref)
    for index, (place, other, fetch) in enumerate(jobs):

        @pl.when(place >= 0)
        def _(index=index, place=place, other=other, fetch=fetch):
            fetch.wait()
            start = pl.multiple_of(place * depth, depth)

            def copy(inner, _):
                slot = table_ref[other, table_ref[row, count + inner]]

                @pl.when(slot >= 0)
                def _():
                    factor_ref[
                        pl.ds(start, depth), pl.ds(pl.multiple_of(inner * TILE, TILE), TILE)
                    ] = strips[index, :, pl.ds(pl.multiple_of(slot * TILE, TILE), TILE)]

                return 0

            lax.fori_loop(0, ones, copy, 0)


def fill_scratch(blocks, depth):
    jobs = sum(block.shape[0] // depth for block in blocks)
    return [
        pltpu.VMEM((jobs, depth, blocks[0].shape[1]), blocks[0].dtype),
        pltpu.SemaphoreType.DMA((jobs,)),
    ]


def first_kernel(table_ref, *refs, places):
    fill(table_ref, refs[-3], refs[:-3], places, refs[-2], refs[-1], True)


def next_kernel(table_ref, _, *refs, places):
    fill(table_ref, refs[-3], refs[:-3], places, refs[-2], refs[-1], False)


def grow(table, factor, arrived, depth):
    blocks, places = zip(*arrived)
    width = blocks[0].shape[1]
    shape = jax.ShapeDtypeStruct((SLOTS * depth, width), blocks[0].dtype)
    options = dict(loose=len(blocks), limit=12, scratch_shapes=fill_scratch(blocks, depth))
    if factor is None:
        kernel = functools.partial(first_kernel, places=places)
        return call(kernel, shape, (table, *blocks), **options)
    kernel = functools.partial(next_kernel, places=places)
    return call(kernel, shape, (table, factor, *blocks), input_output_aliases={1: 0}, **options)


def square_kernel(table_ref, _, band_ref, *refs, places):
    blocks, (spread_ref, square_ref, factor_ref, strips, arrived) = refs[:-5], refs[-5:]
    fill(table_ref, factor_ref, blocks, places, strips, arrived, False)
    band = band_ref[...].reshape(TILE, band_ref.shape[2])
    square = lax.dot_general(
        factor_ref[...], band, (((1,), (1,)), ((), ())), preferred_element_type=jnp.float32
    )
    square_ref[...] = square
    half = square.astype(jnp.bfloat16)
    for col in range(COL):
        spread_ref[col] = half


def square_strips(table, factor, band, arrived):
    blocks, places = zip(*arrived)
    rows = factor.shape[0]
    shapes = (
        jax.ShapeDtypeStruct((COL, rows, TILE), jnp.bfloat16),
        jax.ShapeDtypeStruct((rows, TILE), jnp.float32),
        jax.ShapeDtypeStruct(factor.shape, factor.dtype),
    )
    return call(
        functools.partial(square_kernel, places=places),
        shapes,
        (table, factor, band, *blocks),
        loose=len(blocks),
        input_output_aliases={1: 2},
        scratch_shapes=fill_scratch(blocks, band.shape[1]),
    )


def code(values, coded_ref, to, first):
    rows = values.shape[0]
    largest = jnp.max(jnp.abs(values), axis=0, keepdims=True)
    exponent = jnp.floor(jnp.log2(jnp.maximum(largest, 2.0**-100)))
    steps = jnp.round(values * jnp.exp2(14.0 - exponent))
    steps = jnp.clip(steps, -32767.0, 32767.0)
    coded_ref[to, first : first + rows, :] = steps.astype(jnp.int32).astype(jnp.int16)
    return jnp.broadcast_to(exponent, (8, values.shape[1]))


def cube_kernel(table_ref, factor_ref, square_ref, got_ref, coded_ref, whole, total, *, scale):
    count = table_ref.shape[0]
    row = lax.axis_index("row")
    cols, rows, _ = got_ref.shape
    depth = rows // SLOTS
    for strip in range(cols):
        for place in range(SLOTS):
            start = place * TILE + strip * depth
            whole[start : start + depth, :] = got_ref[
                strip, place * depth : (place + 1) * depth, :
            ]
    total[...] = scale * jnp.dot(
        factor_ref[...], whole[...], preferred_element_type=jnp.float32
    )
    per_col = count // cols
    for to in range(cols):
        marks = []
        for index, source in enumerate((total, square_ref)):
            values = []
            for spot in range(per_col):
                place = table_ref[row, to * per_col + spot]
                start = pl.multiple_of(jnp.maximum(place, 0) * depth, depth)
                values.append(jnp.where(place >= 0, source[pl.ds(start, depth), :], 0.0))
            values = jnp.concatenate(values, axis=0)
            marks.append(code(values, coded_ref, to, index * per_col * depth))
        marks = jnp.concatenate(marks, axis=0)
        coded_ref[to, 2 * per_col * depth :, :] = marks.astype(jnp.int32).astype(jnp.int16)


def cube_strips(table, factor, square, got, scale):
    cols, rows, _ = got.shape
    depth = rows // SLOTS
    per_col = table.shape[0] // cols
    shape = jax.ShapeDtypeStruct((cols, 2 * per_col * depth + 16, TILE), jnp.int16)
    return call(
        functools.partial(cube_kernel, scale=scale),
        shape,
        (table, factor, square, got),
        scratch_shapes=[
            pltpu.VMEM((SLOTS * TILE, TILE), jnp.bfloat16),
            pltpu.VMEM((rows, TILE), jnp.float32),
        ],
    )


def home_kernel(got_ref, square_ref, cubed_ref, held):
    cols, rows, _ = got_ref.shape
    per_col = square_ref.shape[1] // TILE
    depth = TILE // cols
    sizes = []
    for strip in range(cols):
        marks = got_ref[strip, rows - 16 :, :].astype(jnp.int32).astype(jnp.float32)
        sizes.append(jnp.exp2(marks - 14.0))
    for index, out_ref in enumerate((cubed_ref, square_ref)):
        for spot in range(per_col):
            for strip in range(cols):
                start = (index * per_col + spot) * depth
                steps = got_ref[strip, start : start + depth, :].astype(jnp.int32)
                size = sizes[strip][index * 8 : index * 8 + 1, :]
                held[strip * depth : (strip + 1) * depth, :] = steps.astype(jnp.float32) * size
            out_ref[:, spot * TILE : (spot + 1) * TILE] = held[...].T


def home(got, shape):
    out = jax.ShapeDtypeStruct(shape, jnp.float32)
    return call(
        home_kernel,
        (out, out),
        (got,),
        tables=0,
        scratch_shapes=[pltpu.VMEM((TILE, TILE), jnp.float32)],
    )


def local(density, pattern, tile_perm):
    rows, columns = density.shape
    depth = rows // COL
    table = tables(pattern, tile_perm)
    strips = lax.all_to_all(density.reshape(COL, depth, columns), "col", 0, 0)
    packed, spread = pack(table, strips)
    across = to_other_y(packed)
    near = [jnp.concatenate([packed, to_other_core(packed)], 0)]
    far = [jnp.concatenate([across, to_other_core(across)], 0)]

    def both(blocks, step, y_flip):
        return [
            (blocks[step], (step, y_flip, 0)),
            (to_other_core(blocks[step]), (step, y_flip, 1)),
        ]

    near.append(along_z(near[0]))
    far.append(along_z(far[0]))
    near[1], spread = lax.optimization_barrier((near[1], spread))
    band = lax.all_to_all(spread, "col", 0, 0)
    near.append(along_z(near[1]))
    far.append(along_z(far[1]))
    near.append(along_z(near[2]))
    far.append(along_z(far[2]))
    factor = grow(
        table, None, [(near[0], (0, 0, 0)), (far[0], (0, 1, 0))] + both(near, 1, 0), depth
    )
    near[3], factor = lax.optimization_barrier((near[3], factor))
    near.append(along_z(near[3][:depth]))
    factor = grow(table, factor, both(far, 1, 1) + both(near, 2, 0), depth)
    near[4], far[3], factor = lax.optimization_barrier((near[4], far[3], factor))
    far.append(along_z(far[3][:depth]))
    factor = grow(table, factor, both(far, 2, 1) + both(near, 3, 0), depth)
    spread, square, factor = square_strips(
        table, factor, band, both(far, 3, 1) + both(near, 4, 0) + both(far, 4, 1)
    )
    got = lax.all_to_all(spread, "col", 0, 0)
    scale = (rows * lax.axis_size("row") / 2.0) ** (-0.25)
    coded = cube_strips(table, factor, square, got, scale)
    return home(lax.all_to_all(coded, "col", 0, 0), (rows, columns))


def solution(mesh):
    return jax.shard_map(
        local,
        mesh=mesh,
        in_specs=(P("row", "col"), P(), P()),
        out_specs=(P("row", "col"), P("row", "col")),
        check_vma=False,
    )
```

time: 295 us -> 127 us (0.43)
  waiting for transfers between devices: 251 us -> 18.1 us
  blocking collectives: 0 us -> 44.1 us
  starting transfers between devices: 0.12 us -> 41.3 us
  matrix products: 27 us -> 0 us
  Pallas kernels: 0 us -> 15.5 us
  between operations: 13.8 us -> 0.8 us
  local copies, waits for them, and re-layouts: 0.95 us -> 6.18 us
    all_gather x3 -> x0, waiting for transfers between devices: 250 us -> none  [the longest x1 140 us: local(): column = lax.all_gather(matrix, 'row', axis=0, tiled=True)]
    all_to_all x0 -> x2, blocking collectives: none -> 44.1 us  [the longest x1 26.5 us: local(): got = lax.all_to_all(spread, 'col', 0, 0)]
    ppermute x0 -> x19, starting transfers between devices: none -> 31.1 us  [move(): return lax.ppermute(block, BOTH, pairs(place))]
    dot_general x4 -> x0, matrix products: 27 us -> none  [the longest x1 12.7 us: local(): jnp.dot(lax.all_gather(matrix, 'col', axis=1, tiled=True), lower, preferr...]
    pallas_call x0 -> x8, Pallas kernels: none -> 15.5 us  [call(): pl.pallas_call(kernel, out_shape=out_shape, in_specs=[SMEM] * tables + [V...]
    all_to_all x0 -> x2, starting transfers between devices: none -> 10.2 us  [the longest x1 5.87 us: local(): strips = lax.all_to_all(density.reshape(COL, depth, columns), 'col', 0, 0)]
    ppermute x0 -> x19, waiting for transfers between devices: none -> 10.1 us  [move(): return lax.ppermute(block, BOTH, pairs(place))]
    all_to_all x0 -> x2, waiting for transfers between devices: none -> 8.06 us  [the longest x1 8.06 us: local(): strips = lax.all_to_all(density.reshape(COL, depth, columns), 'col', 0, 0)]
  transfers between devices with their start and end apart: 3 -> 21, of which waited for: 3 -> 7; matrix products, arithmetic and copies ran while one was open for 0% -> 1% of each run, Pallas kernels for 0% -> 4%
where the time goes in v2:
time: 127 us; the launch traced here: 126 us
  blocking collectives  44.1 us (35%)
  starting transfers between devices  41.3 us (33%)
  waiting for transfers between devices  18.1 us (14%)
  Pallas kernels  15.5 us (12%)
  local copies, waits for them, and re-layouts  6.18 us (5%)
    ppermute x19, starting transfers between devices, move(): return lax.ppermute(block, BOTH, pairs(place))  31.1 us
    all_to_all x1, blocking collectives, local(): got = lax.all_to_all(spread, 'col', 0, 0)  26.5 us
    all_to_all x1, blocking collectives, local(): return home(lax.all_to_all(coded, 'col', 0, 0), (rows, columns))  17.7 us
    pallas_call x8, Pallas kernels, call(): pl.pallas_call(kernel, out_shape=out_shape, in_specs=[SMEM] * tables + [V...  15.5 us
    ppermute x19, waiting for transfers between devices, move(): return lax.ppermute(block, BOTH, pairs(place))  10.1 us
    all_to_all x1, waiting for transfers between devices, local(): strips = lax.all_to_all(density.reshape(COL, depth, columns), 'col', 0, 0)  8.06 us
    all_to_all x1, starting transfers between devices, local(): strips = lax.all_to_all(density.reshape(COL, depth, columns), 'col', 0, 0)  5.87 us
    unnamed x20, local copies, waits for them, and re-layouts  5.39 us
  transfers between devices with their start and end apart: 21, of which 7 were waited for; matrix products, arithmetic and copies ran while one was open for 1% of the time, Pallas kernels for 4%

profile of v2, /device:TPU:1, one launch (start us, length us, event | category | flops | bytes accessed | tf_op | source)
XLA Modules:
  0.0 126.0 jit_solution(2724173839193966140)
XLA Ops:
  0.6 5.9 %all-to-all-start = ((bf16[8,32,1024]{2,1,0:T(8,128)(2,1)}), bf16[8,32,1024]{2,1,0:T(8,128)(2,1)S(1)}, u32[]{:S(2)}, u32[]{:S(2)}) async-start(bf16[8,32,1024]{2,1,0:T(8,128)(2,1)} %bitcast.2), calls=%async_computation | async-start | bytes 1048576 | tf_op jit(solution)/shard_map/all_to_all | solution.py:315
  8.6 8.1 %all-to-all-done.strips_ref = bf16[8,32,1024]{2,1,0:T(8,128)(2,1)S(1)} async-done(((bf16[8,32,1024]{2,1,0:T(8,128)(2,1)}), bf16[8,32,1024]{2,1,0:T(8,128)(2,1)S(1)}, u32[]{:S(2)}, u32[]{:S(2)}) %all-to-all-start) | async-done | bytes 524320 | tf_op jit(solution)/shard_map/all_to_all | solution.py:315
  16.7 2.2 %shard_map.51 = (bf16[32,3328]{1,0:T(8,128)(2,1)S(1)}, bf16[8,32,3328]{2,1,0:T(8,128)(2,1)}) custom-call(s32[32,64]{1,0:T(8,128)S(1)} %shard_map.50.table_ref, bf16[8,32,1024]{2,1,0:T(8,128)(2,1)S(1)} %all-to-all-done.strips_ref), custom_call_target="tpu_custom_call" | custom-call | tf_op jit(solution)/shard_map/pallas_call | solution.py:53
  18.9 2.6 %collective-permute-start.4 = (bf16[32,3328]{1,0:T(8,128)(2,1)S(1)}, bf16[32,3328]{1,0:T(8,128)(2,1)S(1)}, u32[]{:S(2)}, u32[]{:S(2)}) collective-permute-start(bf16[32,3328]{1,0:T(8,128)(2,1)S(1)} %get-tuple-element.14), channel_id=1, source_target_pairs={{0,16},{1,17},{2,18},{3,19},{4,20},{5,21},{6,22},{7,23},{8,24},{9,... | collective-permute-start | bytes 638984 | tf_op jit(solution)/shard_map/ppermute | solution.py:36
  21.5 1.1 collective-permute-start
  22.6 1.1 collective-permute-done
  23.7 5.7 %collective-permute-start.1 = (bf16[64,3328]{1,0:T(8,128)(2,1)S(1)}, bf16[64,3328]{1,0:T(8,128)(2,1)S(1)}, u32[]{:S(2)}, u32[]{:S(2)}) collective-permute-start(bf16[64,3328]{1,0:T(8,128)(2,1)S(1)} %constant_dynamic-update-slice_fusion.refs_0_), channel_id=1, source_target_pairs={{0,32},{1,33},{2,34},{3,35},{4,36},{5,37},{6,38},{7,39},{8,232},{9... | collective-permute-start | bytes 1277960 | tf_op jit(solution)/shard_map/ppermute | solution.py:36
  29.4 1.4 %collective-permute-done.5 = bf16[32,3328]{1,0:T(8,128)(2,1)S(1)} collective-permute-done((bf16[32,3328]{1,0:T(8,128)(2,1)S(1)}, bf16[32,3328]{1,0:T(8,128)(2,1)S(1)}, u32[]{:S(2)}, u32[]{:S(2)}) %collective-permute-start.5) | collective-permute-done | bytes 213024 | tf_op jit(solution)/shard_map/ppermute | solution.py:36
  30.9 3.9 %collective-permute-start.8 = (bf16[64,3328]{1,0:T(8,128)(2,1)S(1)}, bf16[64,3328]{1,0:T(8,128)(2,1)}, u32[]{:S(2)}, u32[]{:S(2)}) collective-permute-start(bf16[64,3328]{1,0:T(8,128)(2,1)S(1)} %constant_dynamic-update-slice_fusion.2.refs_1_), channel_id=1, source_target_pairs={{0,32},{1,33},{2,34},{3,35},{4,36},{5,37},{6,38},{7,39},{8,232},{9... | collective-permute-start | bytes 1277960 | tf_op jit(solution)/shard_map/ppermute | solution.py:36
  34.8 2.7 %collective-permute-start.2 = (bf16[64,3328]{1,0:T(8,128)(2,1)S(1)}, bf16[64,3328]{1,0:T(8,128)(2,1)}, u32[]{:S(2)}, u32[]{:S(2)}) collective-permute-start(bf16[64,3328]{1,0:T(8,128)(2,1)S(1)} %collective-permute-done.1.refs_2_), channel_id=1, source_target_pairs={{0,32},{1,33},{2,34},{3,35},{4,36},{5,37},{6,38},{7,39},{8,232},{9... | collective-permute-start | bytes 1277960 | tf_op jit(solution)/shard_map/ppermute | solution.py:36
  37.6 4.3 %all-to-all-start.1 = ((bf16[8,32,3328]{2,1,0:T(8,128)(2,1)}), bf16[8,32,3328]{2,1,0:T(8,128)(2,1)}, u32[]{:S(2)}, u32[]{:S(2)}) async-start(bf16[8,32,3328]{2,1,0:T(8,128)(2,1)} %get-tuple-element.20), calls=%async_computation.1 | async-start | bytes 3407872 | tf_op jit(solution)/shard_map/all_to_all | solution.py:330
  41.9 1.2 collective-permute-start.9
  43.1 1.3 %collective-permute-done.2.refs_2_ = bf16[64,3328]{1,0:T(8,128)(2,1)} collective-permute-done((bf16[64,3328]{1,0:T(8,128)(2,1)S(1)}, bf16[64,3328]{1,0:T(8,128)(2,1)}, u32[]{:S(2)}, u32[]{:S(2)}) %collective-permute-start.2) | collective-permute-done | bytes 426016 | tf_op jit(solution)/shard_map/ppermute | solution.py:36
  44.5 3.2 %collective-permute-start.3 = (bf16[64,3328]{1,0:T(8,128)(2,1)}, bf16[64,3328]{1,0:T(8,128)(2,1)S(1)}, u32[]{:S(2)}, u32[]{:S(2)}) collective-permute-start(bf16[64,3328]{1,0:T(8,128)(2,1)} %collective-permute-done.2.refs_2_), channel_id=1, source_target_pairs={{0,32},{1,33},{2,34},{3,35},{4,36},{5,37},{6,38},{7,39},{8,232},{9... | collective-permute-start | bytes 1277960 | tf_op jit(solution)/shard_map/ppermute | solution.py:36
  48.2 1.4 %collective-permute-done.9.refs_0_ = bf16[64,3328]{1,0:T(8,128)(2,1)S(1)} collective-permute-done((bf16[64,3328]{1,0:T(8,128)(2,1)}, bf16[64,3328]{1,0:T(8,128)(2,1)S(1)}, u32[]{:S(2)}, u32[]{:S(2)}) %collective-permute-start.9) | collective-permute-done | bytes 426016 | tf_op jit(solution)/shard_map/ppermute | solution.py:36
  49.6 3.0 %collective-permute-start.10 = (bf16[64,3328]{1,0:T(8,128)(2,1)S(1)}, bf16[64,3328]{1,0:T(8,128)(2,1)S(1)}, u32[]{:S(2)}, u32[]{:S(2)}) collective-permute-start(bf16[64,3328]{1,0:T(8,128)(2,1)S(1)} %collective-permute-done.9.refs_0_), channel_id=1, source_target_pairs={{0,32},{1,33},{2,34},{3,35},{4,36},{5,37},{6,38},{7,39},{8,232},{9... | collective-permute-start | bytes 1277960 | tf_op jit(solution)/shard_map/ppermute | solution.py:36
  52.6 1.0 copy-done.1
  53.6 1.0 copy-done.3
  54.6 1.0 copy-done.5
  55.6 2.5 %shard_map.52._ = bf16[416,3328]{1,0:T(8,128)(2,1)S(1)} custom-call(s32[32,64]{1,0:T(8,128)S(1)} %shard_map.50.table_ref, bf16[64,3328]{1,0:T(8,128)(2,1)S(1)} %copy-done.3, bf16[64,3328]{1,0:T(8,128)(2,1)S(1)} %copy-done.1, bf16[64,3328]{1,0:T(8,128)(2,1)S(1)} %copy-done.5, bf16[64,3328]{1,0:T(8,128)(2,1)S(1)} %collective-permute-done.6.refs_3_), custom_call_target="tpu_custom_call" | custom-call | tf_op jit(solution)/shard_map/pallas_call | solution.py:53
  59.4 1.4 %shard_map.53._ = bf16[416,3328]{1,0:T(8,128)(2,1)S(1)} custom-call(s32[32,64]{1,0:T(8,128)S(1)} %shard_map.50.table_ref, bf16[416,3328]{1,0:T(8,128)(2,1)S(1)} %shard_map.52._, bf16[64,3328]{1,0:T(8,128)(2,1)} %collective-permute-done.8.refs_0_, bf16[64,3328]{1,0:T(8,128)(2,1)S(1)} %collective-permute-done.11.refs_1_, ...), custom_call_target="tpu_custom_call", output_to_operand_aliasing={{}: (1, {})} | custom-call | tf_op jit(solution)/shard_map/pallas_call | solution.py:53
  60.8 2.4 %collective-permute-done.7.refs_2_ = bf16[32,3328]{1,0:T(8,128)(2,1)S(1)} collective-permute-done((bf16[32,3328]{1,0:T(8,128)(2,1)S(1)}, bf16[32,3328]{1,0:T(8,128)(2,1)S(1)}, u32[]{:S(2)}, u32[]{:S(2)}) %collective-permute-start.7) | collective-permute-done | bytes 213024 | tf_op jit(solution)/shard_map/ppermute | solution.py:36
  63.3 2.2 %collective-permute-start.17 = (bf16[32,3328]{1,0:T(8,128)(2,1)S(1)}, bf16[32,3328]{1,0:T(8,128)(2,1)}, u32[]{:S(2)}, u32[]{:S(2)}) collective-permute-start(bf16[32,3328]{1,0:T(8,128)(2,1)S(1)} %slice.7), channel_id=1, source_target_pairs={{0,32},{1,33},{2,34},{3,35},{4,36},{5,37},{6,38},{7,39},{8,232},{9... | collective-permute-start | bytes 638984 | tf_op jit(solution)/shard_map/ppermute | solution.py:36
  66.0 2.4 %collective-permute-done.17.refs_4_ = bf16[32,3328]{1,0:T(8,128)(2,1)} collective-permute-done((bf16[32,3328]{1,0:T(8,128)(2,1)S(1)}, bf16[32,3328]{1,0:T(8,128)(2,1)}, u32[]{:S(2)}, u32[]{:S(2)}) %collective-permute-start.17) | collective-permute-done | bytes 213024 | tf_op jit(solution)/shard_map/ppermute | solution.py:36
  68.3 3.1 %collective-permute-start.18 = (bf16[32,3328]{1,0:T(8,128)(2,1)}, bf16[32,3328]{1,0:T(8,128)(2,1)}, u32[]{:S(2)}, u32[]{:S(2)}) collective-permute-start(bf16[32,3328]{1,0:T(8,128)(2,1)} %collective-permute-done.17.refs_4_), channel_id=1, source_target_pairs={{0,8},{1,9},{2,10},{3,11},{4,12},{5,13},{6,14},{7,15},{8,0},{9,1},... | collective-permute-start | bytes 638984 | tf_op jit(solution)/shard_map/ppermute | solution.py:36
  71.4 1.0 shard_map.54._
  73.2 0.9 copy-done.7
  74.1 3.7 %shard_map.55 = (bf16[8,416,256]{2,1,0:T(8,128)(2,1)S(1)}, f32[416,256]{1,0:T(8,128)S(1)}, bf16[416,3328]{1,0:T(8,128)(2,1)S(1)}) custom-call(s32[32,64]{1,0:T(8,128)S(1)} %shard_map.50.table_ref, bf16[416,3328]{1,0:T(8,128)(2,1)S(1)} %shard_map.54._, bf16[8,32,3328]{2,1,0:T(8,128)(2,1)} %all-to-all-done.1.band_ref, ...), custom_call_target="tpu_custom_call", output_to_operand_aliasing={{2}: (1, {})} | custom-call | tf_op jit(solution)/shard_map/pallas_call | solution.py:53
  77.8 26.5 %all_to_all.20.got_ref = bf16[8,416,256]{2,1,0:T(8,128)(2,1)S(1)} all-to-all(bf16[8,416,256]{2,1,0:T(8,128)(2,1)S(1)} %get-tuple-element.25), channel_id=1, replica_groups=mesh['row'=32,'col'=8] {'col'}, dimensions={0} | all-to-all | bytes 3407872 | tf_op jit(solution)/shard_map/all_to_all | solution.py:347
  104.3 2.2 %shard_map.56 = s16[8,272,256]{2,1,0:T(8,128)(2,1)S(1)} custom-call(s32[32,64]{1,0:T(8,128)S(1)} %shard_map.50.table_ref, bf16[416,3328]{1,0:T(8,128)(2,1)S(1)} %get-tuple-element.23.factor_ref, f32[416,256]{1,0:T(8,128)S(1)} %get-tuple-element.24.square_ref, bf16[8,416,256]{2,1,0:T(8,128)(2,1)S(1)} %all_to_all.20.got_ref), custom_call_target="tpu_custom_call" | custom-call | tf_op jit(solution)/shard_map/pallas_call | solution.py:53
  106.5 17.7 %all_to_all.21.got_ref = s16[8,272,256]{2,1,0:T(8,128)(2,1)S(1)} all-to-all(s16[8,272,256]{2,1,0:T(8,128)(2,1)S(1)} %shard_map.56), channel_id=1, replica_groups=mesh['row'=32,'col'=8] {'col'}, dimensions={0} | all-to-all | bytes 2228224 | tf_op jit(solution)/shard_map/all_to_all | solution.py:350
  124.2 1.8 %shard_map.57 = (f32[256,1024]{1,0:T(8,128)}, f32[256,1024]{1,0:T(8,128)}) custom-call(s16[8,272,256]{2,1,0:T(8,128)(2,1)S(1)} %all_to_all.21.got_ref), custom_call_target="tpu_custom_call" | custom-call | tf_op jit(solution)/shard_map/pallas_call | solution.py:53
  (45 shorter events, 5.3 us)
Async XLA Ops:
  0.6 16.1 %all-to-all-start = ((bf16[8,32,1024]{2,1,0:T(8,128)(2,1)}), bf16[8,32,1024]{2,1,0:T(8,128)(2,1)S(1)}, u32[]{:S(2)}, u32[]{:S(2)}) async-start(bf16[8,32,1024]{2,1,0:T(8,128)(2,1)} %bitcast.2), calls=%async_computation | async-start | bytes 1048576 | tf_op jit(solution)/shard_map/all_to_all | solution.py:315
  7.2 0.7 copy-start.8
  18.9 10.5 %collective-permute-start.4 = (bf16[32,3328]{1,0:T(8,128)(2,1)S(1)}, bf16[32,3328]{1,0:T(8,128)(2,1)S(1)}, u32[]{:S(2)}, u32[]{:S(2)}) collective-permute-start(bf16[32,3328]{1,0:T(8,128)(2,1)S(1)} %get-tuple-element.14), channel_id=1, source_target_pairs={{0,16},{1,17},{2,18},{3,19},{4,20},{5,21},{6,22},{7,23},{8,24},{9,... | collective-permute-start | bytes 638984 | tf_op jit(solution)/shard_map/ppermute | solution.py:36
  21.5 2.2 %collective-permute-start = (bf16[32,3328]{1,0:T(8,128)(2,1)S(1)}, bf16[32,3328]{1,0:T(8,128)(2,1)S(1)}, u32[]{:S(2)}, u32[]{:S(2)}) collective-permute-start(bf16[32,3328]{1,0:T(8,128)(2,1)S(1)} %get-tuple-element.14), channel_id=1, source_target_pairs={{0,8},{1,9},{2,10},{3,11},{4,12},{5,13},{6,14},{7,15},{8,0},{9,1},... | collective-permute-start | bytes 638984 | tf_op jit(solution)/shard_map/ppermute | solution.py:36
  23.7 7.2 %copy-start.2 = (bf16[64,3328]{1,0:T(8,128)(2,1)}, bf16[64,3328]{1,0:T(8,128)(2,1)S(1)}, u32[]{:S(2)}) copy-start(bf16[64,3328]{1,0:T(8,128)(2,1)S(1)} %constant_dynamic-update-slice_fusion.refs_0_) | copy-start | bytes 1277956
  23.7 11.1 %collective-permute-start.1 = (bf16[64,3328]{1,0:T(8,128)(2,1)S(1)}, bf16[64,3328]{1,0:T(8,128)(2,1)S(1)}, u32[]{:S(2)}, u32[]{:S(2)}) collective-permute-start(bf16[64,3328]{1,0:T(8,128)(2,1)S(1)} %constant_dynamic-update-slice_fusion.refs_0_), channel_id=1, source_target_pairs={{0,32},{1,33},{2,34},{3,35},{4,36},{5,37},{6,38},{7,39},{8,232},{9... | collective-permute-start | bytes 1277960 | tf_op jit(solution)/shard_map/ppermute | solution.py:36
  29.4 1.5 %collective-permute-start.5 = (bf16[32,3328]{1,0:T(8,128)(2,1)S(1)}, bf16[32,3328]{1,0:T(8,128)(2,1)S(1)}, u32[]{:S(2)}, u32[]{:S(2)}) collective-permute-start(bf16[32,3328]{1,0:T(8,128)(2,1)S(1)} %collective-permute-done.4), channel_id=1, source_target_pairs={{0,8},{1,9},{2,10},{3,11},{4,12},{5,13},{6,14},{7,15},{8,0},{9,1},... | collective-permute-start | bytes 638984 | tf_op jit(solution)/shard_map/ppermute | solution.py:36
  30.9 6.7 %copy-start = (bf16[64,3328]{1,0:T(8,128)(2,1)}, bf16[64,3328]{1,0:T(8,128)(2,1)S(1)}, u32[]{:S(2)}) copy-start(bf16[64,3328]{1,0:T(8,128)(2,1)S(1)} %constant_dynamic-update-slice_fusion.2.refs_1_) | copy-start | bytes 1277956
  30.9 11.0 %collective-permute-start.8 = (bf16[64,3328]{1,0:T(8,128)(2,1)S(1)}, bf16[64,3328]{1,0:T(8,128)(2,1)}, u32[]{:S(2)}, u32[]{:S(2)}) collective-permute-start(bf16[64,3328]{1,0:T(8,128)(2,1)S(1)} %constant_dynamic-update-slice_fusion.2.refs_1_), channel_id=1, source_target_pairs={{0,32},{1,33},{2,34},{3,35},{4,36},{5,37},{6,38},{7,39},{8,232},{9... | collective-permute-start | bytes 1277960 | tf_op jit(solution)/shard_map/ppermute | solution.py:36
  34.8 8.3 %copy-start.4 = (bf16[64,3328]{1,0:T(8,128)(2,1)}, bf16[64,3328]{1,0:T(8,128)(2,1)S(1)}, u32[]{:S(2)}) copy-start(bf16[64,3328]{1,0:T(8,128)(2,1)S(1)} %collective-permute-done.1.refs_2_) | copy-start | bytes 1277956
  34.8 9.6 %collective-permute-start.2 = (bf16[64,3328]{1,0:T(8,128)(2,1)S(1)}, bf16[64,3328]{1,0:T(8,128)(2,1)}, u32[]{:S(2)}, u32[]{:S(2)}) collective-permute-start(bf16[64,3328]{1,0:T(8,128)(2,1)S(1)} %collective-permute-done.1.refs_2_), channel_id=1, source_target_pairs={{0,32},{1,33},{2,34},{3,35},{4,36},{5,37},{6,38},{7,39},{8,232},{9... | collective-permute-start | bytes 1277960 | tf_op jit(solution)/shard_map/ppermute | solution.py:36
  37.6 35.6 %all-to-all-start.1 = ((bf16[8,32,3328]{2,1,0:T(8,128)(2,1)}), bf16[8,32,3328]{2,1,0:T(8,128)(2,1)}, u32[]{:S(2)}, u32[]{:S(2)}) async-start(bf16[8,32,3328]{2,1,0:T(8,128)(2,1)} %get-tuple-element.20), calls=%async_computation.1 | async-start | bytes 3407872 | tf_op jit(solution)/shard_map/all_to_all | solution.py:330
  41.9 7.7 %collective-permute-start.9 = (bf16[64,3328]{1,0:T(8,128)(2,1)}, bf16[64,3328]{1,0:T(8,128)(2,1)S(1)}, u32[]{:S(2)}, u32[]{:S(2)}) collective-permute-start(bf16[64,3328]{1,0:T(8,128)(2,1)} %collective-permute-done.8.refs_0_), channel_id=1, source_target_pairs={{0,32},{1,33},{2,34},{3,35},{4,36},{5,37},{6,38},{7,39},{8,232},{9... | collective-permute-start | bytes 1277960 | tf_op jit(solution)/shard_map/ppermute | solution.py:36
  43.1 9.4 %collective-permute-start.6 = (bf16[64,3328]{1,0:T(8,128)(2,1)S(1)}, bf16[64,3328]{1,0:T(8,128)(2,1)S(1)}, u32[]{:S(2)}, u32[]{:S(2)}) collective-permute-start(bf16[64,3328]{1,0:T(8,128)(2,1)S(1)} %collective-permute-done.1.refs_2_), channel_id=1, source_target_pairs={{0,8},{1,9},{2,10},{3,11},{4,12},{5,13},{6,14},{7,15},{8,0},{9,1},... | collective-permute-start | bytes 1277960 | tf_op jit(solution)/shard_map/ppermute | solution.py:36
  44.5 13.6 %collective-permute-start.3 = (bf16[64,3328]{1,0:T(8,128)(2,1)}, bf16[64,3328]{1,0:T(8,128)(2,1)S(1)}, u32[]{:S(2)}, u32[]{:S(2)}) collective-permute-start(bf16[64,3328]{1,0:T(8,128)(2,1)} %collective-permute-done.2.refs_2_), channel_id=1, source_target_pairs={{0,32},{1,33},{2,34},{3,35},{4,36},{5,37},{6,38},{7,39},{8,232},{9... | collective-permute-start | bytes 1277960 | tf_op jit(solution)/shard_map/ppermute | solution.py:36
  47.7 11.2 %collective-permute-start.11 = (bf16[64,3328]{1,0:T(8,128)(2,1)}, bf16[64,3328]{1,0:T(8,128)(2,1)S(1)}, u32[]{:S(2)}, u32[]{:S(2)}) collective-permute-start(bf16[64,3328]{1,0:T(8,128)(2,1)} %collective-permute-done.8.refs_0_), channel_id=1, source_target_pairs={{0,8},{1,9},{2,10},{3,11},{4,12},{5,13},{6,14},{7,15},{8,0},{9,1},... | collective-permute-start | bytes 1277960 | tf_op jit(solution)/shard_map/ppermute | solution.py:36
  47.7 11.7 %collective-permute-start.12 = (bf16[64,3328]{1,0:T(8,128)(2,1)}, bf16[64,3328]{1,0:T(8,128)(2,1)S(1)}, u32[]{:S(2)}, u32[]{:S(2)}) collective-permute-start(bf16[64,3328]{1,0:T(8,128)(2,1)} %collective-permute-done.2.refs_2_), channel_id=1, source_target_pairs={{0,8},{1,9},{2,10},{3,11},{4,12},{5,13},{6,14},{7,15},{8,0},{9,1},... | collective-permute-start | bytes 1277960 | tf_op jit(solution)/shard_map/ppermute | solution.py:36
  49.6 13.7 %collective-permute-start.10 = (bf16[64,3328]{1,0:T(8,128)(2,1)S(1)}, bf16[64,3328]{1,0:T(8,128)(2,1)S(1)}, u32[]{:S(2)}, u32[]{:S(2)}) collective-permute-start(bf16[64,3328]{1,0:T(8,128)(2,1)S(1)} %collective-permute-done.9.refs_0_), channel_id=1, source_target_pairs={{0,32},{1,33},{2,34},{3,35},{4,36},{5,37},{6,38},{7,39},{8,232},{9... | collective-permute-start | bytes 1277960 | tf_op jit(solution)/shard_map/ppermute | solution.py:36
  52.6 1.0 copy-start.1
  53.6 1.0 copy-start.3
  54.6 1.0 copy-start.5
  58.1 5.2 %collective-permute-start.7 = (bf16[32,3328]{1,0:T(8,128)(2,1)S(1)}, bf16[32,3328]{1,0:T(8,128)(2,1)S(1)}, u32[]{:S(2)}, u32[]{:S(2)}) collective-permute-start(bf16[32,3328]{1,0:T(8,128)(2,1)S(1)} %slice.6), channel_id=1, source_target_pairs={{0,32},{1,33},{2,34},{3,35},{4,36},{5,37},{6,38},{7,39},{8,232},{9... | collective-permute-start | bytes 638984 | tf_op jit(solution)/shard_map/ppermute | solution.py:36
  58.9 12.6 %collective-permute-start.13 = (bf16[64,3328]{1,0:T(8,128)(2,1)S(1)}, bf16[64,3328]{1,0:T(8,128)(2,1)S(1)}, u32[]{:S(2)}, u32[]{:S(2)}) collective-permute-start(bf16[64,3328]{1,0:T(8,128)(2,1)S(1)} %collective-permute-done.9.refs_0_), channel_id=1, source_target_pairs={{0,8},{1,9},{2,10},{3,11},{4,12},{5,13},{6,14},{7,15},{8,0},{9,1},... | collective-permute-start | bytes 1277960 | tf_op jit(solution)/shard_map/ppermute | solution.py:36
  58.9 12.6 %collective-permute-start.14 = (bf16[64,3328]{1,0:T(8,128)(2,1)S(1)}, bf16[64,3328]{1,0:T(8,128)(2,1)S(1)}, u32[]{:S(2)}, u32[]{:S(2)}) collective-permute-start(bf16[64,3328]{1,0:T(8,128)(2,1)S(1)} %collective-permute-done.3.refs_2_), channel_id=1, source_target_pairs={{0,8},{1,9},{2,10},{3,11},{4,12},{5,13},{6,14},{7,15},{8,0},{9,1},... | collective-permute-start | bytes 1277960 | tf_op jit(solution)/shard_map/ppermute | solution.py:36
  63.3 5.1 %collective-permute-start.17 = (bf16[32,3328]{1,0:T(8,128)(2,1)S(1)}, bf16[32,3328]{1,0:T(8,128)(2,1)}, u32[]{:S(2)}, u32[]{:S(2)}) collective-permute-start(bf16[32,3328]{1,0:T(8,128)(2,1)S(1)} %slice.7), channel_id=1, source_target_pairs={{0,32},{1,33},{2,34},{3,35},{4,36},{5,37},{6,38},{7,39},{8,232},{9... | collective-permute-start | bytes 638984 | tf_op jit(solution)/shard_map/ppermute | solution.py:36
  65.5 7.7 %collective-permute-start.15 = (bf16[64,3328]{1,0:T(8,128)(2,1)S(1)}, bf16[64,3328]{1,0:T(8,128)(2,1)}, u32[]{:S(2)}, u32[]{:S(2)}) collective-permute-start(bf16[64,3328]{1,0:T(8,128)(2,1)S(1)} %collective-permute-done.10.refs_0_), channel_id=1, source_target_pairs={{0,8},{1,9},{2,10},{3,11},{4,12},{5,13},{6,14},{7,15},{8,0},{9,1},... | collective-permute-start | bytes 1277960 | tf_op jit(solution)/shard_map/ppermute | solution.py:36
  65.5 7.0 %collective-permute-start.16 = (bf16[32,3328]{1,0:T(8,128)(2,1)S(1)}, bf16[32,3328]{1,0:T(8,128)(2,1)S(1)}, u32[]{:S(2)}, u32[]{:S(2)}) collective-permute-start(bf16[32,3328]{1,0:T(8,128)(2,1)S(1)} %collective-permute-done.7.refs_2_), channel_id=1, source_target_pairs={{0,8},{1,9},{2,10},{3,11},{4,12},{5,13},{6,14},{7,15},{8,0},{9,1},... | collective-permute-start | bytes 638984 | tf_op jit(solution)/shard_map/ppermute | solution.py:36
  68.3 4.8 %collective-permute-start.18 = (bf16[32,3328]{1,0:T(8,128)(2,1)}, bf16[32,3328]{1,0:T(8,128)(2,1)}, u32[]{:S(2)}, u32[]{:S(2)}) collective-permute-start(bf16[32,3328]{1,0:T(8,128)(2,1)} %collective-permute-done.17.refs_4_), channel_id=1, source_target_pairs={{0,8},{1,9},{2,10},{3,11},{4,12},{5,13},{6,14},{7,15},{8,0},{9,1},... | collective-permute-start | bytes 638984 | tf_op jit(solution)/shard_map/ppermute | solution.py:36
  72.5 0.7 copy-start.6
  73.2 0.9 copy-start.7

commit v3 on v2

--- a/solution.py
+++ b/solution.py
@@ -14,7 +14,7 @@
 VMEM = pl.BlockSpec(memory_space=pltpu.VMEM)
 SMEM = pl.BlockSpec(memory_space=pltpu.SMEM)
 
-Z, Y_HI, CORE, COL = 8, 2, 2, 8
+Z, Y_HI, CORE, COL, X = 8, 2, 2, 8, 4
 
 
 def device(z, y_hi, core, col):
@@ -44,16 +44,26 @@
     return move(block, lambda z, y, core, col: (z, y + 1, core, col))
 
 
+def to_other_y_lo(block):
+    return move(block, lambda z, y, core, col: (z, y, core, (col + X) % COL))
+
+
+def along_x(block):
+    return move(
+        block,
+        lambda z, y, core, col: (z, y, core, col // X * X + (col + 1 - 2 * core) % X),
+    )
+
+
 def along_z(block, steps=1):
     return move(block, lambda z, y, core, col: (z + steps * (1 - 2 * core), y, core, col))
 
 
-def call(kernel, out_shape, operands, tables=1, loose=0, limit=16, **options):
-    held = len(operands) - tables - loose
+def call(kernel, out_shape, operands, tables=1, limit=16, **options):
     return pl.pallas_call(
         kernel,
         out_shape=out_shape,
-        in_specs=[SMEM] * tables + [VMEM] * held + [pl.BlockSpec(memory_space=pltpu.HBM)] * loose,
+        in_specs=[SMEM] * tables + [VMEM] * (len(operands) - tables),
         out_specs=jax.tree.map(lambda _: VMEM, out_shape),
         compiler_params=pltpu.CompilerParams(vmem_limit_bytes=limit * MIB),
         **options,
@@ -97,7 +107,7 @@
     return row // 4, (row // 2) % 2, row % 2
 
 
-def pack_kernel(table_ref, strips_ref, packed_ref, spread_ref):
+def pack_kernel(table_ref, strips_ref, packed_ref):
     count = table_ref.shape[0]
     row = lax.axis_index("row")
     per_col = strips_ref.shape[2] // TILE
@@ -106,99 +116,97 @@
         tile = table_ref[row, count + place]
         start = pl.multiple_of((tile % per_col) * TILE, TILE)
         block = strips_ref[tile // per_col, :, pl.ds(start, TILE)]
-        block = jnp.where(place < ones, block, jnp.zeros_like(block))
-        columns = slice(place * TILE, (place + 1) * TILE)
-        packed_ref[:, columns] = block
-        for col in range(COL):
-            spread_ref[col, :, columns] = block
+        packed_ref[:, place * TILE : (place + 1) * TILE] = jnp.where(
+            place < ones, block, jnp.zeros_like(block)
+        )
 
 
 def pack(table, strips):
-    _, depth, _ = strips.shape
-    width = SLOTS * TILE
-    shapes = (
-        jax.ShapeDtypeStruct((depth, width), strips.dtype),
-        jax.ShapeDtypeStruct((COL, depth, width), strips.dtype),
-    )
-    return call(pack_kernel, shapes, (table, strips), limit=8)
-
-
-def fill(table_ref, factor_ref, blocks, places, strips, arrived, fresh):
+    shape = jax.ShapeDtypeStruct((strips.shape[1], SLOTS * TILE), strips.dtype)
+    return call(pack_kernel, shape, (table, strips), limit=8)
+
+
+def fill(table_ref, factor_ref, blocks, places):
     count = table_ref.shape[0]
-    depth = strips.shape[1]
+    depth = factor_ref.shape[0] // SLOTS
     row = lax.axis_index("row")
     z, y_hi, core = place_of(row)
     ones = table_ref[row, count + SLOTS]
-    jobs = []
     for block, (step, y_flip, core_flip) in zip(blocks, places):
         passed_by = core ^ core_flip
         z_of = (z + Z + step * (2 * passed_by - 1)) % Z
         for half in range(block.shape[0] // depth):
             other = (z_of * Y_HI + (y_hi ^ y_flip)) * CORE + (passed_by ^ half)
-            index = len(jobs)
-            fetch = pltpu.make_async_copy(
-                block.at[pl.ds(half * depth, depth), :], strips.at[index], arrived.at[index]
-            )
-            jobs.append((table_ref[row, other], other, fetch))
-    for place, _, fetch in jobs:
-        pl.when(place >= 0)(fetch.start)
-    if fresh:
-        factor_ref[...] = jnp.zeros_like(factor_ref)
-    for index, (place, other, fetch) in enumerate(jobs):
-
-        @pl.when(place >= 0)
-        def _(index=index, place=place, other=other, fetch=fetch):
-            fetch.wait()
-            start = pl.multiple_of(place * depth, depth)
-
-            def copy(inner, _):
-                slot = table_ref[other, table_ref[row, count + inner]]
-
-                @pl.when(slot >= 0)
-                def _():
-                    factor_ref[
-                        pl.ds(start, depth), pl.ds(pl.multiple_of(inner * TILE, TILE), TILE)
-                    ] = strips[index, :, pl.ds(pl.multiple_of(slot * TILE, TILE), TILE)]
-
-                return 0
-
-            lax.fori_loop(0, ones, copy, 0)
-
-
-def fill_scratch(blocks, depth):
-    jobs = sum(block.shape[0] // depth for block in blocks)
-    return [
-        pltpu.VMEM((jobs, depth, blocks[0].shape[1]), blocks[0].dtype),
-        pltpu.SemaphoreType.DMA((jobs,)),
-    ]
+            place = table_ref[row, other]
+
+            @pl.when(place >= 0)
+            def _(block=block, half=half, other=other, place=place):
+                start = pl.multiple_of(place * depth, depth)
+
+                def copy(inner, _):
+                    slot = table_ref[other, table_ref[row, count + inner]]
+
+                    @pl.when(slot >= 0)
+                    def _():
+                        factor_ref[
+                            pl.ds(start, depth), pl.ds(pl.multiple_of(inner * TILE, TILE), TILE)
+                        ] = block[
+                            half * depth : (half + 1) * depth,
+                            pl.ds(pl.multiple_of(slot * TILE, TILE), TILE),
+                        ]
+
+                    return 0
+
+                lax.fori_loop(0, ones, copy, 0)
 
 
 def first_kernel(table_ref, *refs, places):
-    fill(table_ref, refs[-3], refs[:-3], places, refs[-2], refs[-1], True)
+    refs[-1][...] = jnp.zeros_like(refs[-1])
+    fill(table_ref, refs[-1], refs[:-1], places)
 
 
 def next_kernel(table_ref, _, *refs, places):
-    fill(table_ref, refs[-3], refs[:-3], places, refs[-2], refs[-1], False)
+    fill(table_ref, refs[-1], refs[:-1], places)
 
 
 def grow(table, factor, arrived, depth):
     blocks, places = zip(*arrived)
     width = blocks[0].shape[1]
     shape = jax.ShapeDtypeStruct((SLOTS * depth, width), blocks[0].dtype)
-    options = dict(loose=len(blocks), limit=12, scratch_shapes=fill_scratch(blocks, depth))
     if factor is None:
         kernel = functools.partial(first_kernel, places=places)
-        return call(kernel, shape, (table, *blocks), **options)
+        return call(kernel, shape, (table, *blocks), limit=8)
     kernel = functools.partial(next_kernel, places=places)
-    return call(kernel, shape, (table, factor, *blocks), input_output_aliases={1: 0}, **options)
+    return call(kernel, shape, (table, factor, *blocks), limit=8, input_output_aliases={1: 0})
+
+
+def join_kernel(own_ref, other_ref, band_ref):
+    depth = own_ref.shape[0] // X
+    col = lax.axis_index("col")
+    y_lo, x = col // X, col % X
+    step = 1 - 2 * place_of(lax.axis_index("row"))[2]
+    for ref, y_of in ((own_ref, y_lo), (other_ref, 1 - y_lo)):
+        for index, x_step in enumerate((0, -step, step, 2)):
+            strip = y_of * X + (x + X + x_step) % X
+            band_ref[pl.ds(pl.multiple_of(strip * depth, depth), depth), :] = ref[
+                index * depth : (index + 1) * depth, :
+            ]
+
+
+def join(own, other):
+    rows, width = own.shape
+    shape = jax.ShapeDtypeStruct((2 * rows, width), own.dtype)
+    return call(join_kernel, shape, (own, other), tables=0, limit=8)
 
 
 def square_kernel(table_ref, _, band_ref, *refs, places):
-    blocks, (spread_ref, square_ref, factor_ref, strips, arrived) = refs[:-5], refs[-5:]
-    fill(table_ref, factor_ref, blocks, places, strips, arrived, False)
-    band = band_ref[...].reshape(TILE, band_ref.shape[2])
+    blocks, (spread_ref, square_ref, factor_ref) = refs[:-3], refs[-3:]
+    fill(table_ref, factor_ref, blocks, places)
     square = lax.dot_general(
-        factor_ref[...], band, (((1,), (1,)), ((), ())), preferred_element_type=jnp.float32
+        factor_ref[...],
+        band_ref[...],
+        (((1,), (1,)), ((), ())),
+        preferred_element_type=jnp.float32,
     )
     square_ref[...] = square
     half = square.astype(jnp.bfloat16)
@@ -218,9 +226,7 @@
         functools.partial(square_kernel, places=places),
         shapes,
         (table, factor, band, *blocks),
-        loose=len(blocks),
         input_output_aliases={1: 2},
-        scratch_shapes=fill_scratch(blocks, band.shape[1]),
     )
 
 
@@ -313,36 +319,53 @@
     depth = rows // COL
     table = tables(pattern, tile_perm)
     strips = lax.all_to_all(density.reshape(COL, depth, columns), "col", 0, 0)
-    packed, spread = pack(table, strips)
+    packed = pack(table, strips)
     across = to_other_y(packed)
     near = [jnp.concatenate([packed, to_other_core(packed)], 0)]
     far = [jnp.concatenate([across, to_other_core(across)], 0)]
 
-    def both(blocks, step, y_flip):
-        return [
-            (blocks[step], (step, y_flip, 0)),
-            (to_other_core(blocks[step]), (step, y_flip, 1)),
-        ]
-
     near.append(along_z(near[0]))
     far.append(along_z(far[0]))
-    near[1], spread = lax.optimization_barrier((near[1], spread))
-    band = lax.all_to_all(spread, "col", 0, 0)
+    next_x = along_x(near[0])
+    own = jnp.concatenate(
+        [packed, next_x[:depth], to_other_core(next_x[depth:]), along_x(next_x[:depth])], 0
+    )
+    other = to_other_y_lo(own)
     near.append(along_z(near[1]))
     far.append(along_z(far[1]))
+    near_swapped, far_swapped = [None], [None]
+
+    def swap(block, swapped, hold):
+        hold, arrived = lax.optimization_barrier((hold, to_other_core(block)))
+        swapped.append(arrived)
+        return hold
+
+    near[2] = swap(near[1], near_swapped, near[2])
     near.append(along_z(near[2]))
+    far[2] = swap(far[1], far_swapped, far[2])
     far.append(along_z(far[2]))
-    factor = grow(
-        table, None, [(near[0], (0, 0, 0)), (far[0], (0, 1, 0))] + both(near, 1, 0), depth
-    )
+    near[3] = swap(near[2], near_swapped, near[3])
+
+    def both(step, y_flip):
+        direct, swapped = (far, far_swapped) if y_flip else (near, near_swapped)
+        return [(direct[step], (step, y_flip, 0)), (swapped[step], (step, y_flip, 1))]
+
+    factor = grow(table, None, [(near[0], (0, 0, 0)), (far[0], (0, 1, 0))] + both(1, 0), depth)
     near[3], factor = lax.optimization_barrier((near[3], factor))
     near.append(along_z(near[3][:depth]))
-    factor = grow(table, factor, both(far, 1, 1) + both(near, 2, 0), depth)
-    near[4], far[3], factor = lax.optimization_barrier((near[4], far[3], factor))
+    far[3] = swap(far[2], far_swapped, far[3])
+    near[4], far[3] = lax.optimization_barrier((near[4], far[3]))
     far.append(along_z(far[3][:depth]))
-    factor = grow(table, factor, both(far, 2, 1) + both(near, 3, 0), depth)
+    factor = grow(table, factor, both(1, 1) + both(2, 0), depth)
+    for step in (3, 4):
+        near_swapped.append(to_other_core(near[step]))
+    far_swapped.append(to_other_core(far[3]))
+    factor = grow(table, factor, both(2, 1) + both(3, 0), depth)
+    band = join(own, other)
+    far[4], factor, band = lax.optimization_barrier((far[4], factor, band))
+    far_swapped.append(to_other_core(far[4]))
     spread, square, factor = square_strips(
-        table, factor, band, both(far, 3, 1) + both(near, 4, 0) + both(far, 4, 1)
+        table, factor, band, both(3, 1) + both(4, 0) + both(4, 1)
     )
     got = lax.all_to_all(spread, "col", 0, 0)
     scale = (rows * lax.axis_size("row") / 2.0) ** (-0.25)

time: 127 us -> 120 us (0.945)
  local copies, waits for them, and re-layouts: 6.18 us -> 1.54 us
  Pallas kernels: 15.5 us -> 12 us
  starting transfers between devices: 41.3 us -> 43.5 us
  blocking collectives: 44.1 us -> 42.3 us
    ppermute x19 -> x23, starting transfers between devices: 31.1 us -> 37.6 us  [move(): return lax.ppermute(block, BOTH, pairs(place))]
    unnamed x20 -> x3, local copies, waits for them, and re-layouts: 5.39 us -> 0.73 us
    all_to_all x1 -> x0, starting transfers between devices: 4.3 us -> none  [local(): band = lax.all_to_all(spread, 'col', 0, 0)]
    pallas_call x8 -> x9, Pallas kernels: 15.5 us -> 12 us  [call(): pl.pallas_call(kernel, out_shape=out_shape, in_specs=[SMEM] * tables + [V...]
    all_to_all x1, blocking collectives: 26.5 us -> 25 us  [local(): got = lax.all_to_all(spread, 'col', 0, 0)]
    ppermute x19 -> x23, waiting for transfers between devices: 10.1 us -> 11.1 us  [move(): return lax.ppermute(block, BOTH, pairs(place))]
  transfers between devices with their start and end apart: 21 -> 24, of which waited for: 7 -> 9; matrix products, arithmetic and copies ran while one was open for 1% -> 1% of each run, Pallas kernels for 4% -> 4%
where the time goes in v3:
time: 120 us; the launch traced here: 119 us
  starting transfers between devices  43.5 us (36%)
  blocking collectives  42.3 us (35%)
  waiting for transfers between devices  19.2 us (16%)
  Pallas kernels  12 us (10%)
  local copies, waits for them, and re-layouts  1.54 us (1%)
    ppermute x23, starting transfers between devices, move(): return lax.ppermute(block, BOTH, pairs(place))  37.6 us
    all_to_all x1, blocking collectives, local(): got = lax.all_to_all(spread, 'col', 0, 0)  25 us
    all_to_all x1, blocking collectives, local(): return home(lax.all_to_all(coded, 'col', 0, 0), (rows, columns))  17.3 us
    pallas_call x9, Pallas kernels, call(): pl.pallas_call(kernel, out_shape=out_shape, in_specs=[SMEM] * tables + [V...  12 us
    ppermute x23, waiting for transfers between devices, move(): return lax.ppermute(block, BOTH, pairs(place))  11.1 us
    all_to_all x1, waiting for transfers between devices, local(): strips = lax.all_to_all(density.reshape(COL, depth, columns), 'col', 0, 0)  8.06 us
    all_to_all x1, starting transfers between devices, local(): strips = lax.all_to_all(density.reshape(COL, depth, columns), 'col', 0, 0)  5.87 us
  transfers between devices with their start and end apart: 24, of which 9 were waited for; matrix products, arithmetic and copies ran while one was open for 1% of the time, Pallas kernels for 4%

profile of v3, /device:TPU:1, one launch (start us, length us, event | category | flops | bytes accessed | tf_op | source)
XLA Modules:
  0.0 119.4 jit_solution(13413558075682240094)
XLA Ops:
  0.6 5.9 %all-to-all-start = ((bf16[8,32,1024]{2,1,0:T(8,128)(2,1)}), bf16[8,32,1024]{2,1,0:T(8,128)(2,1)S(1)}, u32[]{:S(2)}, u32[]{:S(2)}) async-start(bf16[8,32,1024]{2,1,0:T(8,128)(2,1)} %bitcast.2), calls=%async_computation | async-start | bytes 1048576 | tf_op jit(solution)/shard_map/all_to_all | solution.py:321
  8.6 8.1 %all-to-all-done.strips_ref = bf16[8,32,1024]{2,1,0:T(8,128)(2,1)S(1)} async-done(((bf16[8,32,1024]{2,1,0:T(8,128)(2,1)}), bf16[8,32,1024]{2,1,0:T(8,128)(2,1)S(1)}, u32[]{:S(2)}, u32[]{:S(2)}) %all-to-all-start) | async-done | bytes 524320 | tf_op jit(solution)/shard_map/all_to_all | solution.py:321
  17.6 0.9 collective-permute-start
  18.6 2.6 %collective-permute-start.6 = (bf16[32,3328]{1,0:T(8,128)(2,1)S(1)}, bf16[32,3328]{1,0:T(8,128)(2,1)S(1)}, u32[]{:S(2)}, u32[]{:S(2)}) collective-permute-start(bf16[32,3328]{1,0:T(8,128)(2,1)S(1)} %shard_map.51), channel_id=1, source_target_pairs={{0,16},{1,17},{2,18},{3,19},{4,20},{5,21},{6,22},{7,23},{8,24},{9,... | collective-permute-start | bytes 638984 | tf_op jit(solution)/shard_map/ppermute | solution.py:36
  21.9 5.6 %collective-permute-start.1 = (bf16[64,3328]{1,0:T(8,128)(2,1)S(1)}, bf16[64,3328]{1,0:T(8,128)(2,1)S(1)}, u32[]{:S(2)}, u32[]{:S(2)}) collective-permute-start(bf16[64,3328]{1,0:T(8,128)(2,1)S(1)} %pad_maximum_fusion.1.refs_0_), channel_id=1, source_target_pairs={{0,32},{1,33},{2,34},{3,35},{4,36},{5,37},{6,38},{7,39},{8,232},{9... | collective-permute-start | bytes 1277960 | tf_op jit(solution)/shard_map/ppermute | solution.py:36
  27.8 1.2 %collective-permute-done.7 = bf16[32,3328]{1,0:T(8,128)(2,1)S(1)} collective-permute-done((bf16[32,3328]{1,0:T(8,128)(2,1)S(1)}, bf16[32,3328]{1,0:T(8,128)(2,1)S(1)}, u32[]{:S(2)}, u32[]{:S(2)}) %collective-permute-start.7) | collective-permute-done | bytes 213024 | tf_op jit(solution)/shard_map/ppermute | solution.py:36
  29.0 5.5 %collective-permute-start.9 = (bf16[64,3328]{1,0:T(8,128)(2,1)S(1)}, bf16[64,3328]{1,0:T(8,128)(2,1)S(1)}, u32[]{:S(2)}, u32[]{:S(2)}) collective-permute-start(bf16[64,3328]{1,0:T(8,128)(2,1)S(1)} %constant_dynamic-update-slice_fusion.refs_1_), channel_id=1, source_target_pairs={{0,32},{1,33},{2,34},{3,35},{4,36},{5,37},{6,38},{7,39},{8,232},{9... | collective-permute-start | bytes 1277960 | tf_op jit(solution)/shard_map/ppermute | solution.py:36
  34.5 1.7 %collective-permute-start.2 = (bf16[64,3328]{1,0:T(8,128)(2,1)S(1)}, bf16[64,3328]{1,0:T(8,128)(2,1)S(1)}, u32[]{:S(2)}, u32[]{:S(2)}) collective-permute-start(bf16[64,3328]{1,0:T(8,128)(2,1)S(1)} %collective-permute-done.1.refs_2_), channel_id=1, source_target_pairs={{0,32},{1,33},{2,34},{3,35},{4,36},{5,37},{6,38},{7,39},{8,232},{9... | collective-permute-start | bytes 1277960 | tf_op jit(solution)/shard_map/ppermute | solution.py:36
  36.4 2.2 %collective-permute-start.18 = (bf16[32,3328]{1,0:T(8,128)(2,1)S(1)}, bf16[32,3328]{1,0:T(8,128)(2,1)S(1)}, u32[]{:S(2)}, u32[]{:S(2)}) collective-permute-start(bf16[32,3328]{1,0:T(8,128)(2,1)S(1)} %get-tuple-element.39), channel_id=1, source_target_pairs={{0,1},{1,2},{2,3},{3,0},{4,5},{5,6},{6,7},{7,4},{8,11},{9,8},{10,9... | collective-permute-start | bytes 638984 | tf_op jit(solution)/shard_map/ppermute | solution.py:36
  38.5 1.0 collective-permute-done.9.refs_0_
  39.6 1.7 %collective-permute-start.11 = (bf16[64,3328]{1,0:T(8,128)(2,1)S(1)}, bf16[64,3328]{1,0:T(8,128)(2,1)S(1)}, u32[]{:S(2)}, u32[]{:S(2)}) collective-permute-start(bf16[64,3328]{1,0:T(8,128)(2,1)S(1)} %collective-permute-done.9.refs_0_), channel_id=1, source_target_pairs={{0,8},{1,9},{2,10},{3,11},{4,12},{5,13},{6,14},{7,15},{8,0},{9,1},... | collective-permute-start | bytes 1277960 | tf_op jit(solution)/shard_map/ppermute | solution.py:36
  41.3 1.7 %collective-permute-start.10 = (bf16[64,3328]{1,0:T(8,128)(2,1)S(1)}, bf16[64,3328]{1,0:T(8,128)(2,1)S(1)}, u32[]{:S(2)}, u32[]{:S(2)}) collective-permute-start(bf16[64,3328]{1,0:T(8,128)(2,1)S(1)} %collective-permute-done.9.refs_0_), channel_id=1, source_target_pairs={{0,32},{1,33},{2,34},{3,35},{4,36},{5,37},{6,38},{7,39},{8,232},{9... | collective-permute-start | bytes 1277960 | tf_op jit(solution)/shard_map/ppermute | solution.py:36
  43.0 1.1 collective-permute-done.2.refs_2_
  44.1 1.7 %collective-permute-start.5 = (bf16[64,3328]{1,0:T(8,128)(2,1)S(1)}, bf16[64,3328]{1,0:T(8,128)(2,1)S(1)}, u32[]{:S(2)}, u32[]{:S(2)}) collective-permute-start(bf16[64,3328]{1,0:T(8,128)(2,1)S(1)} %collective-permute-done.2.refs_2_), channel_id=1, source_target_pairs={{0,8},{1,9},{2,10},{3,11},{4,12},{5,13},{6,14},{7,15},{8,0},{9,1},... | collective-permute-start | bytes 1277960 | tf_op jit(solution)/shard_map/ppermute | solution.py:36
  45.8 1.7 %collective-permute-start.4 = (bf16[64,3328]{1,0:T(8,128)(2,1)S(1)}, bf16[64,3328]{1,0:T(8,128)(2,1)S(1)}, u32[]{:S(2)}, u32[]{:S(2)}) collective-permute-start(bf16[64,3328]{1,0:T(8,128)(2,1)S(1)} %collective-permute-done.2.refs_2_), channel_id=1, source_target_pairs={{0,32},{1,33},{2,34},{3,35},{4,36},{5,37},{6,38},{7,39},{8,232},{9... | collective-permute-start | bytes 1277960 | tf_op jit(solution)/shard_map/ppermute | solution.py:36
  48.7 1.9 %collective-permute-start.13 = (bf16[64,3328]{1,0:T(8,128)(2,1)S(1)}, bf16[64,3328]{1,0:T(8,128)(2,1)S(1)}, u32[]{:S(2)}, u32[]{:S(2)}) collective-permute-start(bf16[64,3328]{1,0:T(8,128)(2,1)S(1)} %collective-permute-done.10.refs_0_), channel_id=1, source_target_pairs={{0,8},{1,9},{2,10},{3,11},{4,12},{5,13},{6,14},{7,15},{8,0},{9,1},... | collective-permute-start | bytes 1277960 | tf_op jit(solution)/shard_map/ppermute | solution.py:36
  50.6 1.5 %collective-permute-start.12 = (bf16[64,3328]{1,0:T(8,128)(2,1)S(1)}, bf16[64,3328]{1,0:T(8,128)(2,1)S(1)}, u32[]{:S(2)}, u32[]{:S(2)}) collective-permute-start(bf16[64,3328]{1,0:T(8,128)(2,1)S(1)} %collective-permute-done.10.refs_0_), channel_id=1, source_target_pairs={{0,32},{1,33},{2,34},{3,35},{4,36},{5,37},{6,38},{7,39},{8,232},{9... | collective-permute-start | bytes 1277960 | tf_op jit(solution)/shard_map/ppermute | solution.py:36
  52.1 1.7 %shard_map.52._ = bf16[416,3328]{1,0:T(8,128)(2,1)S(1)} custom-call(s32[32,64]{1,0:T(8,128)S(1)} %shard_map.50.table_ref, bf16[64,3328]{1,0:T(8,128)(2,1)S(1)} %pad_maximum_fusion.1.refs_0_, bf16[64,3328]{1,0:T(8,128)(2,1)S(1)} %constant_dynamic-update-slice_fusion.refs_1_, bf16[64,3328]{1,0:T(8,128)(2,1)S(1)} %collective-permute-done.1.refs_2_, ...), custom_call_target="tpu_custom_call" | custom-call | tf_op jit(solution)/shard_map/pallas_call | solution.py:63
  53.9 2.6 %collective-permute-start.8 = (bf16[32,3328]{1,0:T(8,128)(2,1)S(1)}, bf16[32,3328]{1,0:T(8,128)(2,1)S(1)}, u32[]{:S(2)}, u32[]{:S(2)}) collective-permute-start(bf16[32,3328]{1,0:T(8,128)(2,1)S(1)} %slice.13), channel_id=1, source_target_pairs={{0,32},{1,33},{2,34},{3,35},{4,36},{5,37},{6,38},{7,39},{8,232},{9... | collective-permute-start | bytes 638984 | tf_op jit(solution)/shard_map/ppermute | solution.py:36
  56.5 1.4 %collective-permute-done.12.refs_0_ = bf16[64,3328]{1,0:T(8,128)(2,1)S(1)} collective-permute-done((bf16[64,3328]{1,0:T(8,128)(2,1)S(1)}, bf16[64,3328]{1,0:T(8,128)(2,1)S(1)}, u32[]{:S(2)}, u32[]{:S(2)}) %collective-permute-start.12) | collective-permute-done | bytes 426016 | tf_op jit(solution)/shard_map/ppermute | solution.py:36
  57.9 2.3 %collective-permute-done.8.refs_2_ = bf16[32,3328]{1,0:T(8,128)(2,1)S(1)} collective-permute-done((bf16[32,3328]{1,0:T(8,128)(2,1)S(1)}, bf16[32,3328]{1,0:T(8,128)(2,1)S(1)}, u32[]{:S(2)}, u32[]{:S(2)}) %collective-permute-start.8) | collective-permute-done | bytes 213024 | tf_op jit(solution)/shard_map/ppermute | solution.py:36
  60.2 3.1 %collective-permute-start.14 = (bf16[32,3328]{1,0:T(8,128)(2,1)S(1)}, bf16[32,3328]{1,0:T(8,128)(2,1)S(1)}, u32[]{:S(2)}, u32[]{:S(2)}) collective-permute-start(bf16[32,3328]{1,0:T(8,128)(2,1)S(1)} %slice.14), channel_id=1, source_target_pairs={{0,32},{1,33},{2,34},{3,35},{4,36},{5,37},{6,38},{7,39},{8,232},{9... | collective-permute-start | bytes 638984 | tf_op jit(solution)/shard_map/ppermute | solution.py:36
  63.3 1.1 shard_map.53._
  65.2 2.3 %collective-permute-done.19.other_ref = bf16[128,3328]{1,0:T(8,128)(2,1)S(1)} collective-permute-done((bf16[128,3328]{1,0:T(8,128)(2,1)S(1)}, bf16[128,3328]{1,0:T(8,128)(2,1)S(1)}, u32[]{:S(2)}, u32[]{:S(2)}) %collective-permute-start.19) | collective-permute-done | bytes 852000 | tf_op jit(solution)/shard_map/ppermute | solution.py:36
  67.6 0.9 shard_map.54._
  68.6 0.9 collective-permute-start.22
  69.5 1.1 collective-permute-done.22.refs_5_
  70.6 2.4 %shard_map.56 = (bf16[8,416,256]{2,1,0:T(8,128)(2,1)S(1)}, f32[416,256]{1,0:T(8,128)S(1)}, bf16[416,3328]{1,0:T(8,128)(2,1)S(1)}) custom-call(s32[32,64]{1,0:T(8,128)S(1)} %shard_map.50.table_ref, bf16[416,3328]{1,0:T(8,128)(2,1)S(1)} %shard_map.54._, bf16[256,3328]{1,0:T(8,128)(2,1)S(1)} %shard_map.55.band_ref, ...), custom_call_target="tpu_custom_call", output_to_operand_aliasing={{2}: (1, {})} | custom-call | tf_op jit(solution)/shard_map/pallas_call | solution.py:63
  73.0 25.0 %all_to_all.15.got_ref = bf16[8,416,256]{2,1,0:T(8,128)(2,1)S(1)} all-to-all(bf16[8,416,256]{2,1,0:T(8,128)(2,1)S(1)} %get-tuple-element.37), channel_id=1, replica_groups=mesh['row'=32,'col'=8] {'col'}, dimensions={0} | all-to-all | bytes 3407872 | tf_op jit(solution)/shard_map/all_to_all | solution.py:370
  98.0 2.2 %shard_map.57 = s16[8,272,256]{2,1,0:T(8,128)(2,1)S(1)} custom-call(s32[32,64]{1,0:T(8,128)S(1)} %shard_map.50.table_ref, bf16[416,3328]{1,0:T(8,128)(2,1)S(1)} %get-tuple-element.35.factor_ref, f32[416,256]{1,0:T(8,128)S(1)} %get-tuple-element.36.square_ref, bf16[8,416,256]{2,1,0:T(8,128)(2,1)S(1)} %all_to_all.15.got_ref), custom_call_target="tpu_custom_call" | custom-call | tf_op jit(solution)/shard_map/pallas_call | solution.py:63
  100.2 17.3 %all_to_all.16.got_ref = s16[8,272,256]{2,1,0:T(8,128)(2,1)S(1)} all-to-all(s16[8,272,256]{2,1,0:T(8,128)(2,1)S(1)} %shard_map.57), channel_id=1, replica_groups=mesh['row'=32,'col'=8] {'col'}, dimensions={0} | all-to-all | bytes 2228224 | tf_op jit(solution)/shard_map/all_to_all | solution.py:373
  117.5 1.8 %shard_map.58 = (f32[256,1024]{1,0:T(8,128)}, f32[256,1024]{1,0:T(8,128)}) custom-call(s16[8,272,256]{2,1,0:T(8,128)(2,1)S(1)} %all_to_all.16.got_ref), custom_call_target="tpu_custom_call" | custom-call | tf_op jit(solution)/shard_map/pallas_call | solution.py:63
  (37 shorter events, 6.2 us)
Async XLA Ops:
  0.6 16.1 %all-to-all-start = ((bf16[8,32,1024]{2,1,0:T(8,128)(2,1)}), bf16[8,32,1024]{2,1,0:T(8,128)(2,1)S(1)}, u32[]{:S(2)}, u32[]{:S(2)}) async-start(bf16[8,32,1024]{2,1,0:T(8,128)(2,1)} %bitcast.2), calls=%async_computation | async-start | bytes 1048576 | tf_op jit(solution)/shard_map/all_to_all | solution.py:321
  7.2 0.7 copy-start
  17.6 3.6 %collective-permute-start = (bf16[32,3328]{1,0:T(8,128)(2,1)S(1)}, bf16[32,3328]{1,0:T(8,128)(2,1)S(1)}, u32[]{:S(2)}, u32[]{:S(2)}) collective-permute-start(bf16[32,3328]{1,0:T(8,128)(2,1)S(1)} %shard_map.51), channel_id=1, source_target_pairs={{0,8},{1,9},{2,10},{3,11},{4,12},{5,13},{6,14},{7,15},{8,0},{9,1},... | collective-permute-start | bytes 638984 | tf_op jit(solution)/shard_map/ppermute | solution.py:36
  18.6 9.0 %collective-permute-start.6 = (bf16[32,3328]{1,0:T(8,128)(2,1)S(1)}, bf16[32,3328]{1,0:T(8,128)(2,1)S(1)}, u32[]{:S(2)}, u32[]{:S(2)}) collective-permute-start(bf16[32,3328]{1,0:T(8,128)(2,1)S(1)} %shard_map.51), channel_id=1, source_target_pairs={{0,16},{1,17},{2,18},{3,19},{4,20},{5,21},{6,22},{7,23},{8,24},{9,... | collective-permute-start | bytes 638984 | tf_op jit(solution)/shard_map/ppermute | solution.py:36
  21.2 15.0 %collective-permute-start.16 = (bf16[64,3328]{1,0:T(8,128)(2,1)S(1)}, bf16[64,3328]{1,0:T(8,128)(2,1)S(1)}, u32[]{:S(2)}, u32[]{:S(2)}) collective-permute-start(bf16[64,3328]{1,0:T(8,128)(2,1)S(1)} %pad_maximum_fusion.1.refs_0_), channel_id=1, source_target_pairs={{0,1},{1,2},{2,3},{3,0},{4,5},{5,6},{6,7},{7,4},{8,11},{9,8},{10,9... | collective-permute-start | bytes 1277960 | tf_op jit(solution)/shard_map/ppermute | solution.py:36
  21.9 12.6 %collective-permute-start.1 = (bf16[64,3328]{1,0:T(8,128)(2,1)S(1)}, bf16[64,3328]{1,0:T(8,128)(2,1)S(1)}, u32[]{:S(2)}, u32[]{:S(2)}) collective-permute-start(bf16[64,3328]{1,0:T(8,128)(2,1)S(1)} %pad_maximum_fusion.1.refs_0_), channel_id=1, source_target_pairs={{0,32},{1,33},{2,34},{3,35},{4,36},{5,37},{6,38},{7,39},{8,232},{9... | collective-permute-start | bytes 1277960 | tf_op jit(solution)/shard_map/ppermute | solution.py:36
  27.5 1.5 %collective-permute-start.7 = (bf16[32,3328]{1,0:T(8,128)(2,1)S(1)}, bf16[32,3328]{1,0:T(8,128)(2,1)S(1)}, u32[]{:S(2)}, u32[]{:S(2)}) collective-permute-start(bf16[32,3328]{1,0:T(8,128)(2,1)S(1)} %collective-permute-done.6), channel_id=1, source_target_pairs={{0,8},{1,9},{2,10},{3,11},{4,12},{5,13},{6,14},{7,15},{8,0},{9,1},... | collective-permute-start | bytes 638984 | tf_op jit(solution)/shard_map/ppermute | solution.py:36
  29.0 10.6 %collective-permute-start.9 = (bf16[64,3328]{1,0:T(8,128)(2,1)S(1)}, bf16[64,3328]{1,0:T(8,128)(2,1)S(1)}, u32[]{:S(2)}, u32[]{:S(2)}) collective-permute-start(bf16[64,3328]{1,0:T(8,128)(2,1)S(1)} %constant_dynamic-update-slice_fusion.refs_1_), channel_id=1, source_target_pairs={{0,32},{1,33},{2,34},{3,35},{4,36},{5,37},{6,38},{7,39},{8,232},{9... | collective-permute-start | bytes 1277960 | tf_op jit(solution)/shard_map/ppermute | solution.py:36
  34.5 6.8 %collective-permute-start.3 = (bf16[64,3328]{1,0:T(8,128)(2,1)S(1)}, bf16[64,3328]{1,0:T(8,128)(2,1)S(1)}, u32[]{:S(2)}, u32[]{:S(2)}) collective-permute-start(bf16[64,3328]{1,0:T(8,128)(2,1)S(1)} %collective-permute-done.1.refs_2_), channel_id=1, source_target_pairs={{0,8},{1,9},{2,10},{3,11},{4,12},{5,13},{6,14},{7,15},{8,0},{9,1},... | collective-permute-start | bytes 1277960 | tf_op jit(solution)/shard_map/ppermute | solution.py:36
  34.5 9.6 %collective-permute-start.2 = (bf16[64,3328]{1,0:T(8,128)(2,1)S(1)}, bf16[64,3328]{1,0:T(8,128)(2,1)S(1)}, u32[]{:S(2)}, u32[]{:S(2)}) collective-permute-start(bf16[64,3328]{1,0:T(8,128)(2,1)S(1)} %collective-permute-done.1.refs_2_), channel_id=1, source_target_pairs={{0,32},{1,33},{2,34},{3,35},{4,36},{5,37},{6,38},{7,39},{8,232},{9... | collective-permute-start | bytes 1277960 | tf_op jit(solution)/shard_map/ppermute | solution.py:36
  36.3 9.6 %collective-permute-start.17 = (bf16[32,3328]{1,0:T(8,128)(2,1)S(1)}, bf16[32,3328]{1,0:T(8,128)(2,1)S(1)}, u32[]{:S(2)}, u32[]{:S(2)}) collective-permute-start(bf16[32,3328]{1,0:T(8,128)(2,1)S(1)} %get-tuple-element.38), channel_id=1, source_target_pairs={{0,8},{1,9},{2,10},{3,11},{4,12},{5,13},{6,14},{7,15},{8,0},{9,1},... | collective-permute-start | bytes 638984 | tf_op jit(solution)/shard_map/ppermute | solution.py:36
  36.4 11.2 %collective-permute-start.18 = (bf16[32,3328]{1,0:T(8,128)(2,1)S(1)}, bf16[32,3328]{1,0:T(8,128)(2,1)S(1)}, u32[]{:S(2)}, u32[]{:S(2)}) collective-permute-start(bf16[32,3328]{1,0:T(8,128)(2,1)S(1)} %get-tuple-element.39), channel_id=1, source_target_pairs={{0,1},{1,2},{2,3},{3,0},{4,5},{5,6},{6,7},{7,4},{8,11},{9,8},{10,9... | collective-permute-start | bytes 638984 | tf_op jit(solution)/shard_map/ppermute | solution.py:36
  39.6 8.4 %collective-permute-start.11 = (bf16[64,3328]{1,0:T(8,128)(2,1)S(1)}, bf16[64,3328]{1,0:T(8,128)(2,1)S(1)}, u32[]{:S(2)}, u32[]{:S(2)}) collective-permute-start(bf16[64,3328]{1,0:T(8,128)(2,1)S(1)} %collective-permute-done.9.refs_0_), channel_id=1, source_target_pairs={{0,8},{1,9},{2,10},{3,11},{4,12},{5,13},{6,14},{7,15},{8,0},{9,1},... | collective-permute-start | bytes 1277960 | tf_op jit(solution)/shard_map/ppermute | solution.py:36
  41.3 7.4 %collective-permute-start.10 = (bf16[64,3328]{1,0:T(8,128)(2,1)S(1)}, bf16[64,3328]{1,0:T(8,128)(2,1)S(1)}, u32[]{:S(2)}, u32[]{:S(2)}) collective-permute-start(bf16[64,3328]{1,0:T(8,128)(2,1)S(1)} %collective-permute-done.9.refs_0_), channel_id=1, source_target_pairs={{0,32},{1,33},{2,34},{3,35},{4,36},{5,37},{6,38},{7,39},{8,232},{9... | collective-permute-start | bytes 1277960 | tf_op jit(solution)/shard_map/ppermute | solution.py:36
  44.1 9.7 %collective-permute-start.5 = (bf16[64,3328]{1,0:T(8,128)(2,1)S(1)}, bf16[64,3328]{1,0:T(8,128)(2,1)S(1)}, u32[]{:S(2)}, u32[]{:S(2)}) collective-permute-start(bf16[64,3328]{1,0:T(8,128)(2,1)S(1)} %collective-permute-done.2.refs_2_), channel_id=1, source_target_pairs={{0,8},{1,9},{2,10},{3,11},{4,12},{5,13},{6,14},{7,15},{8,0},{9,1},... | collective-permute-start | bytes 1277960 | tf_op jit(solution)/shard_map/ppermute | solution.py:36
  45.8 8.1 %collective-permute-start.4 = (bf16[64,3328]{1,0:T(8,128)(2,1)S(1)}, bf16[64,3328]{1,0:T(8,128)(2,1)S(1)}, u32[]{:S(2)}, u32[]{:S(2)}) collective-permute-start(bf16[64,3328]{1,0:T(8,128)(2,1)S(1)} %collective-permute-done.2.refs_2_), channel_id=1, source_target_pairs={{0,32},{1,33},{2,34},{3,35},{4,36},{5,37},{6,38},{7,39},{8,232},{9... | collective-permute-start | bytes 1277960 | tf_op jit(solution)/shard_map/ppermute | solution.py:36
  47.6 19.8 %collective-permute-start.19 = (bf16[128,3328]{1,0:T(8,128)(2,1)S(1)}, bf16[128,3328]{1,0:T(8,128)(2,1)S(1)}, u32[]{:S(2)}, u32[]{:S(2)}) collective-permute-start(bf16[128,3328]{1,0:T(8,128)(2,1)S(1)} %pad_maximum_fusion.own_ref), channel_id=1, source_target_pairs={{0,4},{1,5},{2,6},{3,7},{4,0},{5,1},{6,2},{7,3},{8,12},{9,13},{10,... | collective-permute-start | bytes 2555912 | tf_op jit(solution)/shard_map/ppermute | solution.py:36
  48.7 7.8 %collective-permute-start.13 = (bf16[64,3328]{1,0:T(8,128)(2,1)S(1)}, bf16[64,3328]{1,0:T(8,128)(2,1)S(1)}, u32[]{:S(2)}, u32[]{:S(2)}) collective-permute-start(bf16[64,3328]{1,0:T(8,128)(2,1)S(1)} %collective-permute-done.10.refs_0_), channel_id=1, source_target_pairs={{0,8},{1,9},{2,10},{3,11},{4,12},{5,13},{6,14},{7,15},{8,0},{9,1},... | collective-permute-start | bytes 1277960 | tf_op jit(solution)/shard_map/ppermute | solution.py:36
  50.6 7.3 %collective-permute-start.12 = (bf16[64,3328]{1,0:T(8,128)(2,1)S(1)}, bf16[64,3328]{1,0:T(8,128)(2,1)S(1)}, u32[]{:S(2)}, u32[]{:S(2)}) collective-permute-start(bf16[64,3328]{1,0:T(8,128)(2,1)S(1)} %collective-permute-done.10.refs_0_), channel_id=1, source_target_pairs={{0,32},{1,33},{2,34},{3,35},{4,36},{5,37},{6,38},{7,39},{8,232},{9... | collective-permute-start | bytes 1277960 | tf_op jit(solution)/shard_map/ppermute | solution.py:36
  53.9 6.3 %collective-permute-start.8 = (bf16[32,3328]{1,0:T(8,128)(2,1)S(1)}, bf16[32,3328]{1,0:T(8,128)(2,1)S(1)}, u32[]{:S(2)}, u32[]{:S(2)}) collective-permute-start(bf16[32,3328]{1,0:T(8,128)(2,1)S(1)} %slice.13), channel_id=1, source_target_pairs={{0,32},{1,33},{2,34},{3,35},{4,36},{5,37},{6,38},{7,39},{8,232},{9... | collective-permute-start | bytes 638984 | tf_op jit(solution)/shard_map/ppermute | solution.py:36
  56.5 11.1 %collective-permute-start.15 = (bf16[64,3328]{1,0:T(8,128)(2,1)S(1)}, bf16[64,3328]{1,0:T(8,128)(2,1)S(1)}, u32[]{:S(2)}, u32[]{:S(2)}) collective-permute-start(bf16[64,3328]{1,0:T(8,128)(2,1)S(1)} %collective-permute-done.4.refs_2_), channel_id=1, source_target_pairs={{0,8},{1,9},{2,10},{3,11},{4,12},{5,13},{6,14},{7,15},{8,0},{9,1},... | collective-permute-start | bytes 1277960 | tf_op jit(solution)/shard_map/ppermute | solution.py:36
  60.2 8.4 %collective-permute-start.14 = (bf16[32,3328]{1,0:T(8,128)(2,1)S(1)}, bf16[32,3328]{1,0:T(8,128)(2,1)S(1)}, u32[]{:S(2)}, u32[]{:S(2)}) collective-permute-start(bf16[32,3328]{1,0:T(8,128)(2,1)S(1)} %slice.14), channel_id=1, source_target_pairs={{0,32},{1,33},{2,34},{3,35},{4,36},{5,37},{6,38},{7,39},{8,232},{9... | collective-permute-start | bytes 638984 | tf_op jit(solution)/shard_map/ppermute | solution.py:36
  63.3 6.2 %collective-permute-start.20 = (bf16[64,3328]{1,0:T(8,128)(2,1)S(1)}, bf16[64,3328]{1,0:T(8,128)(2,1)S(1)}, u32[]{:S(2)}, u32[]{:S(2)}) collective-permute-start(bf16[64,3328]{1,0:T(8,128)(2,1)S(1)} %collective-permute-done.12.refs_0_), channel_id=1, source_target_pairs={{0,8},{1,9},{2,10},{3,11},{4,12},{5,13},{6,14},{7,15},{8,0},{9,1},... | collective-permute-start | bytes 1277960 | tf_op jit(solution)/shard_map/ppermute | solution.py:36
  64.4 5.0 %collective-permute-start.21 = (bf16[32,3328]{1,0:T(8,128)(2,1)S(1)}, bf16[32,3328]{1,0:T(8,128)(2,1)S(1)}, u32[]{:S(2)}, u32[]{:S(2)}) collective-permute-start(bf16[32,3328]{1,0:T(8,128)(2,1)S(1)} %collective-permute-done.8.refs_2_), channel_id=1, source_target_pairs={{0,8},{1,9},{2,10},{3,11},{4,12},{5,13},{6,14},{7,15},{8,0},{9,1},... | collective-permute-start | bytes 638984 | tf_op jit(solution)/shard_map/ppermute | solution.py:36
  68.6 2.0 %collective-permute-start.22 = (bf16[32,3328]{1,0:T(8,128)(2,1)S(1)}, bf16[32,3328]{1,0:T(8,128)(2,1)S(1)}, u32[]{:S(2)}, u32[]{:S(2)}) collective-permute-start(bf16[32,3328]{1,0:T(8,128)(2,1)S(1)} %collective-permute-done.14.refs_4_), channel_id=1, source_target_pairs={{0,8},{1,9},{2,10},{3,11},{4,12},{5,13},{6,14},{7,15},{8,0},{9,1},... | collective-permute-start | bytes 638984 | tf_op jit(solution)/shard_map/ppermute | solution.py:36

commit v4 on v3

--- a/solution.py
+++ b/solution.py
@@ -180,27 +180,58 @@
     return call(kernel, shape, (table, factor, *blocks), limit=8, input_output_aliases={1: 0})
 
 
-def join_kernel(own_ref, other_ref, band_ref):
-    depth = own_ref.shape[0] // X
+def join_kernel(own_ref, far_own_ref, other_ref, far_other_ref, band_ref):
+    depth = own_ref.shape[0] // 2
     col = lax.axis_index("col")
     y_lo, x = col // X, col % X
     step = 1 - 2 * place_of(lax.axis_index("row"))[2]
-    for ref, y_of in ((own_ref, y_lo), (other_ref, 1 - y_lo)):
-        for index, x_step in enumerate((0, -step, step, 2)):
+    for ref, y_of, x_steps in (
+        (own_ref, y_lo, (0, -step)),
+        (far_own_ref, y_lo, (step, 2)),
+        (other_ref, 1 - y_lo, (0, -step)),
+        (far_other_ref, 1 - y_lo, (step, 2)),
+    ):
+        for index, x_step in enumerate(x_steps):
             strip = y_of * X + (x + X + x_step) % X
             band_ref[pl.ds(pl.multiple_of(strip * depth, depth), depth), :] = ref[
                 index * depth : (index + 1) * depth, :
             ]
 
 
-def join(own, other):
-    rows, width = own.shape
-    shape = jax.ShapeDtypeStruct((2 * rows, width), own.dtype)
-    return call(join_kernel, shape, (own, other), tables=0, limit=8)
+def join(*pieces):
+    rows, width = pieces[0].shape
+    shape = jax.ShapeDtypeStruct((4 * rows, width), pieces[0].dtype)
+    return call(join_kernel, shape, pieces, tables=0, limit=8)
+
+
+MARKS = 16
+
+
+def code(strips):
+    steps, marks = [], []
+    for values in strips:
+        largest = jnp.max(jnp.abs(values), axis=0, keepdims=True)
+        exponent = jnp.floor(jnp.log2(jnp.maximum(largest, 2.0**-100)))
+        scaled = jnp.round(values * jnp.exp2(14.0 - exponent))
+        steps.append(jnp.clip(scaled, -32767.0, 32767.0))
+        marks.append(exponent)
+    marks += [jnp.zeros_like(marks[0])] * (MARKS - len(marks))
+    coded = jnp.concatenate(steps + marks, axis=0)
+    return coded.astype(jnp.int32).astype(jnp.int16)
+
+
+def steps_of(coded_ref, strip):
+    first = coded_ref.shape[1] - MARKS
+    marks = coded_ref[strip, first:, :].astype(jnp.int32).astype(jnp.float32)
+    return jnp.exp2(marks - 14.0)
+
+
+def decode(steps, step):
+    return steps.astype(jnp.int32).astype(jnp.float32) * step
 
 
 def square_kernel(table_ref, _, band_ref, *refs, places):
-    blocks, (spread_ref, square_ref, factor_ref) = refs[:-3], refs[-3:]
+    blocks, (spread_ref, factor_ref) = refs[:-2], refs[-2:]
     fill(table_ref, factor_ref, blocks, places)
     square = lax.dot_general(
         factor_ref[...],
@@ -208,110 +239,102 @@
         (((1,), (1,)), ((), ())),
         preferred_element_type=jnp.float32,
     )
-    square_ref[...] = square
-    half = square.astype(jnp.bfloat16)
+    depth = square.shape[0] // SLOTS
+    coded = code([square[place * depth : (place + 1) * depth] for place in range(SLOTS)])
     for col in range(COL):
-        spread_ref[col] = half
+        spread_ref[col] = coded
 
 
 def square_strips(table, factor, band, arrived):
     blocks, places = zip(*arrived)
-    rows = factor.shape[0]
     shapes = (
-        jax.ShapeDtypeStruct((COL, rows, TILE), jnp.bfloat16),
-        jax.ShapeDtypeStruct((rows, TILE), jnp.float32),
+        jax.ShapeDtypeStruct((COL, factor.shape[0] + MARKS, TILE), jnp.int16),
         jax.ShapeDtypeStruct(factor.shape, factor.dtype),
     )
     return call(
         functools.partial(square_kernel, places=places),
         shapes,
         (table, factor, band, *blocks),
-        input_output_aliases={1: 2},
-    )
-
-
-def code(values, coded_ref, to, first):
-    rows = values.shape[0]
-    largest = jnp.max(jnp.abs(values), axis=0, keepdims=True)
-    exponent = jnp.floor(jnp.log2(jnp.maximum(largest, 2.0**-100)))
-    steps = jnp.round(values * jnp.exp2(14.0 - exponent))
-    steps = jnp.clip(steps, -32767.0, 32767.0)
-    coded_ref[to, first : first + rows, :] = steps.astype(jnp.int32).astype(jnp.int16)
-    return jnp.broadcast_to(exponent, (8, values.shape[1]))
-
-
-def cube_kernel(table_ref, factor_ref, square_ref, got_ref, coded_ref, whole, total, *, scale):
+        input_output_aliases={1: 1},
+    )
+
+
+def cube_kernel(table_ref, factor_ref, got_ref, coded_ref, whole, total, *, scale):
     count = table_ref.shape[0]
     row = lax.axis_index("row")
     cols, rows, _ = got_ref.shape
-    depth = rows // SLOTS
+    depth = (rows - MARKS) // SLOTS
     for strip in range(cols):
+        sizes = steps_of(got_ref, strip)
         for place in range(SLOTS):
             start = place * TILE + strip * depth
-            whole[start : start + depth, :] = got_ref[
-                strip, place * depth : (place + 1) * depth, :
-            ]
+            steps = got_ref[strip, place * depth : (place + 1) * depth, :]
+            square = decode(steps, sizes[place : place + 1])
+            whole[start : start + depth, :] = square.astype(jnp.bfloat16)
     total[...] = scale * jnp.dot(
         factor_ref[...], whole[...], preferred_element_type=jnp.float32
     )
     per_col = count // cols
     for to in range(cols):
-        marks = []
-        for index, source in enumerate((total, square_ref)):
-            values = []
-            for spot in range(per_col):
-                place = table_ref[row, to * per_col + spot]
-                start = pl.multiple_of(jnp.maximum(place, 0) * depth, depth)
-                values.append(jnp.where(place >= 0, source[pl.ds(start, depth), :], 0.0))
-            values = jnp.concatenate(values, axis=0)
-            marks.append(code(values, coded_ref, to, index * per_col * depth))
-        marks = jnp.concatenate(marks, axis=0)
-        coded_ref[to, 2 * per_col * depth :, :] = marks.astype(jnp.int32).astype(jnp.int16)
-
-
-def cube_strips(table, factor, square, got, scale):
+        values = []
+        for spot in range(per_col):
+            place = table_ref[row, to * per_col + spot]
+            start = pl.multiple_of(jnp.maximum(place, 0) * depth, depth)
+            values.append(jnp.where(place >= 0, total[pl.ds(start, depth), :], 0.0))
+        coded_ref[to] = code(values)
+
+
+def cube_strips(table, factor, got, scale):
     cols, rows, _ = got.shape
-    depth = rows // SLOTS
+    depth = (rows - MARKS) // SLOTS
     per_col = table.shape[0] // cols
-    shape = jax.ShapeDtypeStruct((cols, 2 * per_col * depth + 16, TILE), jnp.int16)
+    shape = jax.ShapeDtypeStruct((cols, per_col * depth + MARKS, TILE), jnp.int16)
     return call(
         functools.partial(cube_kernel, scale=scale),
         shape,
-        (table, factor, square, got),
+        (table, factor, got),
         scratch_shapes=[
             pltpu.VMEM((SLOTS * TILE, TILE), jnp.bfloat16),
-            pltpu.VMEM((rows, TILE), jnp.float32),
+            pltpu.VMEM((SLOTS * depth, TILE), jnp.float32),
         ],
     )
 
 
-def home_kernel(got_ref, square_ref, cubed_ref, held):
+def square_home_kernel(table_ref, got_ref, square_ref, held):
+    row, col = lax.axis_index("row"), lax.axis_index("col")
     cols, rows, _ = got_ref.shape
+    depth = (rows - MARKS) // SLOTS
     per_col = square_ref.shape[1] // TILE
+    sizes = [steps_of(got_ref, strip) for strip in range(cols)]
+    index = lax.broadcasted_iota(jnp.int32, sizes[0].shape, 0)
+    for spot in range(per_col):
+        place = table_ref[row, col * per_col + spot]
+        start = pl.multiple_of(jnp.maximum(place, 0) * depth, depth)
+        for strip in range(cols):
+            size = jnp.sum(jnp.where(index == place, sizes[strip], 0.0), axis=0, keepdims=True)
+            held[strip * depth : (strip + 1) * depth, :] = decode(
+                got_ref[strip, pl.ds(start, depth), :], size
+            )
+        square_ref[:, spot * TILE : (spot + 1) * TILE] = held[...].T
+
+
+def cube_home_kernel(got_ref, cubed_ref, held):
+    cols = got_ref.shape[0]
     depth = TILE // cols
-    sizes = []
-    for strip in range(cols):
-        marks = got_ref[strip, rows - 16 :, :].astype(jnp.int32).astype(jnp.float32)
-        sizes.append(jnp.exp2(marks - 14.0))
-    for index, out_ref in enumerate((cubed_ref, square_ref)):
-        for spot in range(per_col):
-            for strip in range(cols):
-                start = (index * per_col + spot) * depth
-                steps = got_ref[strip, start : start + depth, :].astype(jnp.int32)
-                size = sizes[strip][index * 8 : index * 8 + 1, :]
-                held[strip * depth : (strip + 1) * depth, :] = steps.astype(jnp.float32) * size
-            out_ref[:, spot * TILE : (spot + 1) * TILE] = held[...].T
-
-
-def home(got, shape):
+    sizes = [steps_of(got_ref, strip) for strip in range(cols)]
+    for spot in range(cubed_ref.shape[1] // TILE):
+        for strip in range(cols):
+            steps = got_ref[strip, spot * depth : (spot + 1) * depth, :]
+            held[strip * depth : (strip + 1) * depth, :] = decode(
+                steps, sizes[strip][spot : spot + 1]
+            )
+        cubed_ref[:, spot * TILE : (spot + 1) * TILE] = held[...].T
+
+
+def home(kernel, operands, tables, shape):
     out = jax.ShapeDtypeStruct(shape, jnp.float32)
-    return call(
-        home_kernel,
-        (out, out),
-        (got,),
-        tables=0,
-        scratch_shapes=[pltpu.VMEM((TILE, TILE), jnp.float32)],
-    )
+    scratch = [pltpu.VMEM((TILE, TILE), jnp.float32)]
+    return call(kernel, out, operands, tables=tables, scratch_shapes=scratch)
 
 
 def local(density, pattern, tile_perm):
@@ -327,10 +350,10 @@
     near.append(along_z(near[0]))
     far.append(along_z(far[0]))
     next_x = along_x(near[0])
-    own = jnp.concatenate(
-        [packed, next_x[:depth], to_other_core(next_x[depth:]), along_x(next_x[:depth])], 0
-    )
+    own = jnp.concatenate([packed, next_x[:depth]], 0)
     other = to_other_y_lo(own)
+    far_own = jnp.concatenate([to_other_core(next_x[depth:]), along_x(next_x[:depth])], 0)
+    far_other = to_other_y_lo(far_own)
     near.append(along_z(near[1]))
     far.append(along_z(far[1]))
     near_swapped, far_swapped = [None], [None]
@@ -343,6 +366,7 @@
     near[2] = swap(near[1], near_swapped, near[2])
     near.append(along_z(near[2]))
     far[2] = swap(far[1], far_swapped, far[2])
+    far[2], other = lax.optimization_barrier((far[2], other))
     far.append(along_z(far[2]))
     near[3] = swap(near[2], near_swapped, near[3])
 
@@ -354,23 +378,24 @@
     near[3], factor = lax.optimization_barrier((near[3], factor))
     near.append(along_z(near[3][:depth]))
     far[3] = swap(far[2], far_swapped, far[3])
-    near[4], far[3] = lax.optimization_barrier((near[4], far[3]))
     far.append(along_z(far[3][:depth]))
     factor = grow(table, factor, both(1, 1) + both(2, 0), depth)
     for step in (3, 4):
         near_swapped.append(to_other_core(near[step]))
     far_swapped.append(to_other_core(far[3]))
     factor = grow(table, factor, both(2, 1) + both(3, 0), depth)
-    band = join(own, other)
+    band = join(own, far_own, other, far_other)
     far[4], factor, band = lax.optimization_barrier((far[4], factor, band))
     far_swapped.append(to_other_core(far[4]))
-    spread, square, factor = square_strips(
+    spread, factor = square_strips(
         table, factor, band, both(3, 1) + both(4, 0) + both(4, 1)
     )
     got = lax.all_to_all(spread, "col", 0, 0)
     scale = (rows * lax.axis_size("row") / 2.0) ** (-0.25)
-    coded = cube_strips(table, factor, square, got, scale)
-    return home(lax.all_to_all(coded, "col", 0, 0), (rows, columns))
+    coded = cube_strips(table, factor, got, scale)
+    square = home(square_home_kernel, (table, got), 1, (rows, columns))
+    cubed = home(cube_home_kernel, (lax.all_to_all(coded, "col", 0, 0),), 0, (rows, columns))
+    return square, cubed
 
 
 def solution(mesh):

time: 120 us -> 115 us (0.958)
  blocking collectives: 42.3 us -> 25.2 us
  waiting for transfers between devices: 19.2 us -> 27.3 us
  Pallas kernels: 12 us -> 14.1 us
  starting transfers between devices: 43.5 us -> 45.5 us
    all_to_all x1 -> x0, blocking collectives: 17.3 us -> none  [local(): return home(lax.all_to_all(coded, 'col', 0, 0), (rows, columns))]
    all_to_all x0 -> x1, waiting for transfers between devices: none -> 8.62 us  [local(): lax.all_to_all(coded, 'col', 0, 0)]
    all_to_all x0 -> x1, starting transfers between devices: none -> 3.54 us  [local(): lax.all_to_all(coded, 'col', 0, 0)]
    pallas_call x9 -> x10, Pallas kernels: 12 us -> 14.1 us  [call(): pl.pallas_call(kernel, out_shape=out_shape, in_specs=[SMEM] * tables + [V...]
    ppermute x23 -> x24, starting transfers between devices: 37.6 us -> 36.1 us  [move(): return lax.ppermute(block, BOTH, pairs(place))]
    ppermute x23 -> x24, waiting for transfers between devices: 11.1 us -> 10.6 us  [move(): return lax.ppermute(block, BOTH, pairs(place))]
  transfers between devices with their start and end apart: 24 -> 26, of which waited for: 9 -> 9; matrix products, arithmetic and copies ran while one was open for 1% -> 1% of each run, Pallas kernels for 4% -> 6%
where the time goes in v4:
time: 115 us
  starting transfers between devices  45.5 us (40%)
  waiting for transfers between devices  27.3 us (24%)
  blocking collectives  25.2 us (22%)
  Pallas kernels  14.1 us (12%)
  local copies, waits for them, and re-layouts  1.57 us (1%)
    ppermute x24, starting transfers between devices, move(): return lax.ppermute(block, BOTH, pairs(place))  36.1 us
    all_to_all x1, blocking collectives, local(): got = lax.all_to_all(spread, 'col', 0, 0)  25.2 us
    pallas_call x10, Pallas kernels, call(): pl.pallas_call(kernel, out_shape=out_shape, in_specs=[SMEM] * tables + [V...  14.1 us
    ppermute x24, waiting for transfers between devices, move(): return lax.ppermute(block, BOTH, pairs(place))  10.6 us
    all_to_all x1, waiting for transfers between devices, local(): lax.all_to_all(coded, 'col', 0, 0)  8.62 us
    all_to_all x1, waiting for transfers between devices, local(): strips = lax.all_to_all(density.reshape(COL, depth, columns), 'col', 0, 0)  8.06 us
    all_to_all x1, starting transfers between devices, local(): strips = lax.all_to_all(density.reshape(COL, depth, columns), 'col', 0, 0)  5.87 us
    all_to_all x1, starting transfers between devices, local(): lax.all_to_all(coded, 'col', 0, 0)  3.54 us
  transfers between devices with their start and end apart: 26, of which 9 were waited for; matrix products, arithmetic and copies ran while one was open for 1% of the time, Pallas kernels for 6%

profile of v4, /device:TPU:1, one launch (start us, length us, event | category | flops | bytes accessed | tf_op | source)
XLA Modules:
  0.0 114.6 jit_solution(11187332828099712194)
XLA Ops:
  0.6 5.9 %all-to-all-start = ((bf16[8,32,1024]{2,1,0:T(8,128)(2,1)}), bf16[8,32,1024]{2,1,0:T(8,128)(2,1)S(1)}, u32[]{:S(2)}, u32[]{:S(2)}) async-start(bf16[8,32,1024]{2,1,0:T(8,128)(2,1)} %bitcast.2), calls=%async_computation | async-start | bytes 1048576 | tf_op jit(solution)/shard_map/all_to_all | solution.py:344
  8.6 8.1 %all-to-all-done.strips_ref = bf16[8,32,1024]{2,1,0:T(8,128)(2,1)S(1)} async-done(((bf16[8,32,1024]{2,1,0:T(8,128)(2,1)}), bf16[8,32,1024]{2,1,0:T(8,128)(2,1)S(1)}, u32[]{:S(2)}, u32[]{:S(2)}) %all-to-all-start) | async-done | bytes 524320 | tf_op jit(solution)/shard_map/all_to_all | solution.py:344
  18.6 2.6 %collective-permute-start = (bf16[32,3328]{1,0:T(8,128)(2,1)S(1)}, bf16[32,3328]{1,0:T(8,128)(2,1)S(1)}, u32[]{:S(2)}, u32[]{:S(2)}) collective-permute-start(bf16[32,3328]{1,0:T(8,128)(2,1)S(1)} %shard_map.51), channel_id=1, source_target_pairs={{0,16},{1,17},{2,18},{3,19},{4,20},{5,21},{6,22},{7,23},{8,24},{9,... | collective-permute-start | bytes 638984 | tf_op jit(solution)/shard_map/ppermute | solution.py:36
  21.9 5.6 %collective-permute-start.11 = (bf16[64,3328]{1,0:T(8,128)(2,1)S(1)}, bf16[64,3328]{1,0:T(8,128)(2,1)S(1)}, u32[]{:S(2)}, u32[]{:S(2)}) collective-permute-start(bf16[64,3328]{1,0:T(8,128)(2,1)S(1)} %pad_maximum_fusion.refs_0_), channel_id=1, source_target_pairs={{0,32},{1,33},{2,34},{3,35},{4,36},{5,37},{6,38},{7,39},{8,232},{9... | collective-permute-start | bytes 1277960 | tf_op jit(solution)/shard_map/ppermute | solution.py:36
  27.8 1.2 %collective-permute-done.1 = bf16[32,3328]{1,0:T(8,128)(2,1)S(1)} collective-permute-done((bf16[32,3328]{1,0:T(8,128)(2,1)S(1)}, bf16[32,3328]{1,0:T(8,128)(2,1)S(1)}, u32[]{:S(2)}, u32[]{:S(2)}) %collective-permute-start.1) | collective-permute-done | bytes 213024 | tf_op jit(solution)/shard_map/ppermute | solution.py:36
  29.0 5.5 %collective-permute-start.2 = (bf16[64,3328]{1,0:T(8,128)(2,1)S(1)}, bf16[64,3328]{1,0:T(8,128)(2,1)S(1)}, u32[]{:S(2)}, u32[]{:S(2)}) collective-permute-start(bf16[64,3328]{1,0:T(8,128)(2,1)S(1)} %constant_dynamic-update-slice_fusion.refs_1_), channel_id=1, source_target_pairs={{0,32},{1,33},{2,34},{3,35},{4,36},{5,37},{6,38},{7,39},{8,232},{9... | collective-permute-start | bytes 1277960 | tf_op jit(solution)/shard_map/ppermute | solution.py:36
  34.7 2.0 %collective-permute-start.12 = (bf16[64,3328]{1,0:T(8,128)(2,1)S(1)}, bf16[64,3328]{1,0:T(8,128)(2,1)S(1)}, u32[]{:S(2)}, u32[]{:S(2)}) collective-permute-start(bf16[64,3328]{1,0:T(8,128)(2,1)S(1)} %collective-permute-done.11.refs_2_), channel_id=1, source_target_pairs={{0,32},{1,33},{2,34},{3,35},{4,36},{5,37},{6,38},{7,39},{8,232},{9... | collective-permute-start | bytes 1277960 | tf_op jit(solution)/shard_map/ppermute | solution.py:36
  37.0 2.5 %collective-permute-done.2.refs_0_ = bf16[64,3328]{1,0:T(8,128)(2,1)S(1)} collective-permute-done((bf16[64,3328]{1,0:T(8,128)(2,1)S(1)}, bf16[64,3328]{1,0:T(8,128)(2,1)S(1)}, u32[]{:S(2)}, u32[]{:S(2)}) %collective-permute-start.2) | collective-permute-done | bytes 426016 | tf_op jit(solution)/shard_map/ppermute | solution.py:36
  39.6 1.7 %collective-permute-start.13 = (bf16[64,3328]{1,0:T(8,128)(2,1)S(1)}, bf16[64,3328]{1,0:T(8,128)(2,1)S(1)}, u32[]{:S(2)}, u32[]{:S(2)}) collective-permute-start(bf16[64,3328]{1,0:T(8,128)(2,1)S(1)} %collective-permute-done.11.refs_2_), channel_id=1, source_target_pairs={{0,8},{1,9},{2,10},{3,11},{4,12},{5,13},{6,14},{7,15},{8,0},{9,1},... | collective-permute-start | bytes 1277960 | tf_op jit(solution)/shard_map/ppermute | solution.py:36
  41.3 1.7 %collective-permute-start.3 = (bf16[64,3328]{1,0:T(8,128)(2,1)S(1)}, bf16[64,3328]{1,0:T(8,128)(2,1)S(1)}, u32[]{:S(2)}, u32[]{:S(2)}) collective-permute-start(bf16[64,3328]{1,0:T(8,128)(2,1)S(1)} %collective-permute-done.2.refs_0_), channel_id=1, source_target_pairs={{0,32},{1,33},{2,34},{3,35},{4,36},{5,37},{6,38},{7,39},{8,232},{9... | collective-permute-start | bytes 1277960 | tf_op jit(solution)/shard_map/ppermute | solution.py:36
  43.0 1.1 collective-permute-done.12.refs_2_
  44.1 1.7 %collective-permute-start.4 = (bf16[64,3328]{1,0:T(8,128)(2,1)S(1)}, bf16[64,3328]{1,0:T(8,128)(2,1)S(1)}, u32[]{:S(2)}, u32[]{:S(2)}) collective-permute-start(bf16[64,3328]{1,0:T(8,128)(2,1)S(1)} %collective-permute-done.2.refs_0_), channel_id=1, source_target_pairs={{0,8},{1,9},{2,10},{3,11},{4,12},{5,13},{6,14},{7,15},{8,0},{9,1},... | collective-permute-start | bytes 1277960 | tf_op jit(solution)/shard_map/ppermute | solution.py:36
  45.9 1.8 %collective-permute-start.14 = (bf16[64,3328]{1,0:T(8,128)(2,1)S(1)}, bf16[64,3328]{1,0:T(8,128)(2,1)S(1)}, u32[]{:S(2)}, u32[]{:S(2)}) collective-permute-start(bf16[64,3328]{1,0:T(8,128)(2,1)S(1)} %collective-permute-done.12.refs_2_), channel_id=1, source_target_pairs={{0,32},{1,33},{2,34},{3,35},{4,36},{5,37},{6,38},{7,39},{8,232},{9... | collective-permute-start | bytes 1277960 | tf_op jit(solution)/shard_map/ppermute | solution.py:36
  47.7 1.0 collective-permute-done.3.refs_0_
  48.7 1.9 %collective-permute-start.15 = (bf16[64,3328]{1,0:T(8,128)(2,1)S(1)}, bf16[64,3328]{1,0:T(8,128)(2,1)S(1)}, u32[]{:S(2)}, u32[]{:S(2)}) collective-permute-start(bf16[64,3328]{1,0:T(8,128)(2,1)S(1)} %collective-permute-done.12.refs_2_), channel_id=1, source_target_pairs={{0,8},{1,9},{2,10},{3,11},{4,12},{5,13},{6,14},{7,15},{8,0},{9,1},... | collective-permute-start | bytes 1277960 | tf_op jit(solution)/shard_map/ppermute | solution.py:36
  50.6 1.5 %collective-permute-start.8 = (bf16[64,3328]{1,0:T(8,128)(2,1)S(1)}, bf16[64,3328]{1,0:T(8,128)(2,1)S(1)}, u32[]{:S(2)}, u32[]{:S(2)}) collective-permute-start(bf16[64,3328]{1,0:T(8,128)(2,1)S(1)} %collective-permute-done.3.refs_0_), channel_id=1, source_target_pairs={{0,32},{1,33},{2,34},{3,35},{4,36},{5,37},{6,38},{7,39},{8,232},{9... | collective-permute-start | bytes 1277960 | tf_op jit(solution)/shard_map/ppermute | solution.py:36
  52.7 1.7 %shard_map.52._ = bf16[416,3328]{1,0:T(8,128)(2,1)S(1)} custom-call(s32[32,64]{1,0:T(8,128)S(1)} %shard_map.50.table_ref, bf16[64,3328]{1,0:T(8,128)(2,1)S(1)} %pad_maximum_fusion.refs_0_, bf16[64,3328]{1,0:T(8,128)(2,1)S(1)} %constant_dynamic-update-slice_fusion.refs_1_, bf16[64,3328]{1,0:T(8,128)(2,1)S(1)} %collective-permute-done.11.refs_2_, ...), custom_call_target="tpu_custom_call" | custom-call | tf_op jit(solution)/shard_map/pallas_call | solution.py:63
  55.3 1.5 %collective-permute-start.21 = (bf16[32,3328]{1,0:T(8,128)(2,1)S(1)}, bf16[32,3328]{1,0:T(8,128)(2,1)S(1)}, u32[]{:S(2)}, u32[]{:S(2)}) collective-permute-start(bf16[32,3328]{1,0:T(8,128)(2,1)S(1)} %slice.16), channel_id=1, source_target_pairs={{0,32},{1,33},{2,34},{3,35},{4,36},{5,37},{6,38},{7,39},{8,232},{9... | collective-permute-start | bytes 638984 | tf_op jit(solution)/shard_map/ppermute | solution.py:36
  56.8 1.1 collective-permute-done.8.refs_0_
  57.9 3.1 %collective-permute-start.10 = (bf16[32,3328]{1,0:T(8,128)(2,1)S(1)}, bf16[32,3328]{1,0:T(8,128)(2,1)S(1)}, u32[]{:S(2)}, u32[]{:S(2)}) collective-permute-start(bf16[32,3328]{1,0:T(8,128)(2,1)S(1)} %slice.14), channel_id=1, source_target_pairs={{0,32},{1,33},{2,34},{3,35},{4,36},{5,37},{6,38},{7,39},{8,232},{9... | collective-permute-start | bytes 638984 | tf_op jit(solution)/shard_map/ppermute | solution.py:36
  61.1 2.3 %collective-permute-done.19.far_other_ref = bf16[64,3328]{1,0:T(8,128)(2,1)S(1)} collective-permute-done((bf16[64,3328]{1,0:T(8,128)(2,1)S(1)}, bf16[64,3328]{1,0:T(8,128)(2,1)S(1)}, u32[]{:S(2)}, u32[]{:S(2)}) %collective-permute-start.19) | collective-permute-done | bytes 426016 | tf_op jit(solution)/shard_map/ppermute | solution.py:36
  63.5 1.1 shard_map.53._
  64.6 1.5 %collective-permute-start.22 = (bf16[32,3328]{1,0:T(8,128)(2,1)S(1)}, bf16[32,3328]{1,0:T(8,128)(2,1)S(1)}, u32[]{:S(2)}, u32[]{:S(2)}) collective-permute-start(bf16[32,3328]{1,0:T(8,128)(2,1)S(1)} %collective-permute-done.21.refs_2_), channel_id=1, source_target_pairs={{0,8},{1,9},{2,10},{3,11},{4,12},{5,13},{6,14},{7,15},{8,0},{9,1},... | collective-permute-start | bytes 638984 | tf_op jit(solution)/shard_map/ppermute | solution.py:36
  66.0 1.1 shard_map.54._
  67.4 1.3 %collective-permute-done.23.refs_5_ = bf16[32,3328]{1,0:T(8,128)(2,1)S(1)} collective-permute-done((bf16[32,3328]{1,0:T(8,128)(2,1)S(1)}, bf16[32,3328]{1,0:T(8,128)(2,1)S(1)}, u32[]{:S(2)}, u32[]{:S(2)}) %collective-permute-start.23) | collective-permute-done | bytes 213024 | tf_op jit(solution)/shard_map/ppermute | solution.py:36
  68.7 2.1 %shard_map.56 = (s16[8,432,256]{2,1,0:T(8,128)(2,1)S(1)}, bf16[416,3328]{1,0:T(8,128)(2,1)S(1)}) custom-call(s32[32,64]{1,0:T(8,128)S(1)} %shard_map.50.table_ref, bf16[416,3328]{1,0:T(8,128)(2,1)S(1)} %shard_map.54._, bf16[256,3328]{1,0:T(8,128)(2,1)S(1)} %shard_map.55.band_ref, ...), custom_call_target="tpu_custom_call", output_to_operand_aliasing={{1}: (1, {})} | custom-call | tf_op jit(solution)/shard_map/pallas_call | solution.py:63
  70.9 25.2 %all_to_all.15.got_ref = s16[8,432,256]{2,1,0:T(8,128)(2,1)S(1)} all-to-all(s16[8,432,256]{2,1,0:T(8,128)(2,1)S(1)} %get-tuple-element.34), channel_id=1, replica_groups=mesh['row'=32,'col'=8] {'col'}, dimensions={0} | all-to-all | bytes 3538944 | tf_op jit(solution)/shard_map/all_to_all | solution.py:393
  96.1 2.9 %shard_map.58 = s16[8,144,256]{2,1,0:T(8,128)(2,1)} custom-call(s32[32,64]{1,0:T(8,128)S(1)} %shard_map.50.table_ref, bf16[416,3328]{1,0:T(8,128)(2,1)S(1)} %get-tuple-element.35.factor_ref, s16[8,432,256]{2,1,0:T(8,128)(2,1)S(1)} %all_to_all.15.got_ref), custom_call_target="tpu_custom_call" | custom-call | tf_op jit(solution)/shard_map/pallas_call | solution.py:63
  98.9 3.5 %all-to-all-start.2 = ((s16[8,144,256]{2,1,0:T(8,128)(2,1)}), s16[8,144,256]{2,1,0:T(8,128)(2,1)S(1)}, u32[]{:S(2)}, u32[]{:S(2)}) async-start(s16[8,144,256]{2,1,0:T(8,128)(2,1)} %shard_map.58), calls=%async_computation.2 | async-start | bytes 1179648 | tf_op jit(solution)/shard_map/all_to_all | solution.py:397
  102.5 2.1 %shard_map.57 = f32[256,1024]{1,0:T(8,128)} custom-call(s32[32,64]{1,0:T(8,128)S(1)} %shard_map.50.table_ref, s16[8,432,256]{2,1,0:T(8,128)(2,1)S(1)} %all_to_all.15.got_ref), custom_call_target="tpu_custom_call" | custom-call | tf_op jit(solution)/shard_map/pallas_call | solution.py:63
  104.6 8.6 %all-to-all-done.2.got_ref = s16[8,144,256]{2,1,0:T(8,128)(2,1)S(1)} async-done(((s16[8,144,256]{2,1,0:T(8,128)(2,1)}), s16[8,144,256]{2,1,0:T(8,128)(2,1)S(1)}, u32[]{:S(2)}, u32[]{:S(2)}) %all-to-all-start.2) | async-done | bytes 589856 | tf_op jit(solution)/shard_map/all_to_all | solution.py:397
  113.2 1.3 %shard_map.59 = f32[256,1024]{1,0:T(8,128)} custom-call(s16[8,144,256]{2,1,0:T(8,128)(2,1)S(1)} %all-to-all-done.2.got_ref), custom_call_target="tpu_custom_call" | custom-call | tf_op jit(solution)/shard_map/pallas_call | solution.py:63
  (43 shorter events, 7.3 us)
Async XLA Ops:
  0.6 16.1 %all-to-all-start = ((bf16[8,32,1024]{2,1,0:T(8,128)(2,1)}), bf16[8,32,1024]{2,1,0:T(8,128)(2,1)S(1)}, u32[]{:S(2)}, u32[]{:S(2)}) async-start(bf16[8,32,1024]{2,1,0:T(8,128)(2,1)} %bitcast.2), calls=%async_computation | async-start | bytes 1048576 | tf_op jit(solution)/shard_map/all_to_all | solution.py:344
  7.2 0.7 copy-start
  17.6 3.6 %collective-permute-start.5 = (bf16[32,3328]{1,0:T(8,128)(2,1)S(1)}, bf16[32,3328]{1,0:T(8,128)(2,1)S(1)}, u32[]{:S(2)}, u32[]{:S(2)}) collective-permute-start(bf16[32,3328]{1,0:T(8,128)(2,1)S(1)} %shard_map.51), channel_id=1, source_target_pairs={{0,8},{1,9},{2,10},{3,11},{4,12},{5,13},{6,14},{7,15},{8,0},{9,1},... | collective-permute-start | bytes 638984 | tf_op jit(solution)/shard_map/ppermute | solution.py:36
  18.6 9.0 %collective-permute-start = (bf16[32,3328]{1,0:T(8,128)(2,1)S(1)}, bf16[32,3328]{1,0:T(8,128)(2,1)S(1)}, u32[]{:S(2)}, u32[]{:S(2)}) collective-permute-start(bf16[32,3328]{1,0:T(8,128)(2,1)S(1)} %shard_map.51), channel_id=1, source_target_pairs={{0,16},{1,17},{2,18},{3,19},{4,20},{5,21},{6,22},{7,23},{8,24},{9,... | collective-permute-start | bytes 638984 | tf_op jit(solution)/shard_map/ppermute | solution.py:36
  21.2 13.3 %collective-permute-start.6 = (bf16[64,3328]{1,0:T(8,128)(2,1)S(1)}, bf16[64,3328]{1,0:T(8,128)(2,1)S(1)}, u32[]{:S(2)}, u32[]{:S(2)}) collective-permute-start(bf16[64,3328]{1,0:T(8,128)(2,1)S(1)} %pad_maximum_fusion.refs_0_), channel_id=1, source_target_pairs={{0,1},{1,2},{2,3},{3,0},{4,5},{5,6},{6,7},{7,4},{8,11},{9,8},{10,9... | collective-permute-start | bytes 1277960 | tf_op jit(solution)/shard_map/ppermute | solution.py:36
  21.9 12.7 %collective-permute-start.11 = (bf16[64,3328]{1,0:T(8,128)(2,1)S(1)}, bf16[64,3328]{1,0:T(8,128)(2,1)S(1)}, u32[]{:S(2)}, u32[]{:S(2)}) collective-permute-start(bf16[64,3328]{1,0:T(8,128)(2,1)S(1)} %pad_maximum_fusion.refs_0_), channel_id=1, source_target_pairs={{0,32},{1,33},{2,34},{3,35},{4,36},{5,37},{6,38},{7,39},{8,232},{9... | collective-permute-start | bytes 1277960 | tf_op jit(solution)/shard_map/ppermute | solution.py:36
  27.5 1.5 %collective-permute-start.1 = (bf16[32,3328]{1,0:T(8,128)(2,1)S(1)}, bf16[32,3328]{1,0:T(8,128)(2,1)S(1)}, u32[]{:S(2)}, u32[]{:S(2)}) collective-permute-start(bf16[32,3328]{1,0:T(8,128)(2,1)S(1)} %collective-permute-done), channel_id=1, source_target_pairs={{0,8},{1,9},{2,10},{3,11},{4,12},{5,13},{6,14},{7,15},{8,0},{9,1},... | collective-permute-start | bytes 638984 | tf_op jit(solution)/shard_map/ppermute | solution.py:36
  29.0 10.6 %collective-permute-start.2 = (bf16[64,3328]{1,0:T(8,128)(2,1)S(1)}, bf16[64,3328]{1,0:T(8,128)(2,1)S(1)}, u32[]{:S(2)}, u32[]{:S(2)}) collective-permute-start(bf16[64,3328]{1,0:T(8,128)(2,1)S(1)} %constant_dynamic-update-slice_fusion.refs_1_), channel_id=1, source_target_pairs={{0,32},{1,33},{2,34},{3,35},{4,36},{5,37},{6,38},{7,39},{8,232},{9... | collective-permute-start | bytes 1277960 | tf_op jit(solution)/shard_map/ppermute | solution.py:36
  34.5 6.7 %collective-permute-start.17 = (bf16[32,3328]{1,0:T(8,128)(2,1)S(1)}, bf16[32,3328]{1,0:T(8,128)(2,1)S(1)}, u32[]{:S(2)}, u32[]{:S(2)}) collective-permute-start(bf16[32,3328]{1,0:T(8,128)(2,1)S(1)} %get-tuple-element.36), channel_id=1, source_target_pairs={{0,8},{1,9},{2,10},{3,11},{4,12},{5,13},{6,14},{7,15},{8,0},{9,1},... | collective-permute-start | bytes 638984 | tf_op jit(solution)/shard_map/ppermute | solution.py:36
  34.7 9.5 %collective-permute-start.12 = (bf16[64,3328]{1,0:T(8,128)(2,1)S(1)}, bf16[64,3328]{1,0:T(8,128)(2,1)S(1)}, u32[]{:S(2)}, u32[]{:S(2)}) collective-permute-start(bf16[64,3328]{1,0:T(8,128)(2,1)S(1)} %collective-permute-done.11.refs_2_), channel_id=1, source_target_pairs={{0,32},{1,33},{2,34},{3,35},{4,36},{5,37},{6,38},{7,39},{8,232},{9... | collective-permute-start | bytes 1277960 | tf_op jit(solution)/shard_map/ppermute | solution.py:36
  36.7 15.4 %collective-permute-start.18 = (bf16[32,3328]{1,0:T(8,128)(2,1)S(1)}, bf16[32,3328]{1,0:T(8,128)(2,1)S(1)}, u32[]{:S(2)}, u32[]{:S(2)}) collective-permute-start(bf16[32,3328]{1,0:T(8,128)(2,1)S(1)} %get-tuple-element.37), channel_id=1, source_target_pairs={{0,1},{1,2},{2,3},{3,0},{4,5},{5,6},{6,7},{7,4},{8,11},{9,8},{10,9... | collective-permute-start | bytes 638984 | tf_op jit(solution)/shard_map/ppermute | solution.py:36
  36.8 13.8 %collective-permute-start.7 = (bf16[64,3328]{1,0:T(8,128)(2,1)S(1)}, bf16[64,3328]{1,0:T(8,128)(2,1)S(1)}, u32[]{:S(2)}, u32[]{:S(2)}) collective-permute-start(bf16[64,3328]{1,0:T(8,128)(2,1)S(1)} %pad_maximum_fusion.1.own_ref), channel_id=1, source_target_pairs={{0,4},{1,5},{2,6},{3,7},{4,0},{5,1},{6,2},{7,3},{8,12},{9,13},{10,... | collective-permute-start | bytes 1277960 | tf_op jit(solution)/shard_map/ppermute | solution.py:36
  39.6 6.3 %collective-permute-start.13 = (bf16[64,3328]{1,0:T(8,128)(2,1)S(1)}, bf16[64,3328]{1,0:T(8,128)(2,1)S(1)}, u32[]{:S(2)}, u32[]{:S(2)}) collective-permute-start(bf16[64,3328]{1,0:T(8,128)(2,1)S(1)} %collective-permute-done.11.refs_2_), channel_id=1, source_target_pairs={{0,8},{1,9},{2,10},{3,11},{4,12},{5,13},{6,14},{7,15},{8,0},{9,1},... | collective-permute-start | bytes 1277960 | tf_op jit(solution)/shard_map/ppermute | solution.py:36
  41.3 7.4 %collective-permute-start.3 = (bf16[64,3328]{1,0:T(8,128)(2,1)S(1)}, bf16[64,3328]{1,0:T(8,128)(2,1)S(1)}, u32[]{:S(2)}, u32[]{:S(2)}) collective-permute-start(bf16[64,3328]{1,0:T(8,128)(2,1)S(1)} %collective-permute-done.2.refs_0_), channel_id=1, source_target_pairs={{0,32},{1,33},{2,34},{3,35},{4,36},{5,37},{6,38},{7,39},{8,232},{9... | collective-permute-start | bytes 1277960 | tf_op jit(solution)/shard_map/ppermute | solution.py:36
  44.1 6.5 %collective-permute-start.4 = (bf16[64,3328]{1,0:T(8,128)(2,1)S(1)}, bf16[64,3328]{1,0:T(8,128)(2,1)S(1)}, u32[]{:S(2)}, u32[]{:S(2)}) collective-permute-start(bf16[64,3328]{1,0:T(8,128)(2,1)S(1)} %collective-permute-done.2.refs_0_), channel_id=1, source_target_pairs={{0,8},{1,9},{2,10},{3,11},{4,12},{5,13},{6,14},{7,15},{8,0},{9,1},... | collective-permute-start | bytes 1277960 | tf_op jit(solution)/shard_map/ppermute | solution.py:36
  45.9 8.6 %collective-permute-start.14 = (bf16[64,3328]{1,0:T(8,128)(2,1)S(1)}, bf16[64,3328]{1,0:T(8,128)(2,1)S(1)}, u32[]{:S(2)}, u32[]{:S(2)}) collective-permute-start(bf16[64,3328]{1,0:T(8,128)(2,1)S(1)} %collective-permute-done.12.refs_2_), channel_id=1, source_target_pairs={{0,32},{1,33},{2,34},{3,35},{4,36},{5,37},{6,38},{7,39},{8,232},{9... | collective-permute-start | bytes 1277960 | tf_op jit(solution)/shard_map/ppermute | solution.py:36
  48.7 5.7 %collective-permute-start.15 = (bf16[64,3328]{1,0:T(8,128)(2,1)S(1)}, bf16[64,3328]{1,0:T(8,128)(2,1)S(1)}, u32[]{:S(2)}, u32[]{:S(2)}) collective-permute-start(bf16[64,3328]{1,0:T(8,128)(2,1)S(1)} %collective-permute-done.12.refs_2_), channel_id=1, source_target_pairs={{0,8},{1,9},{2,10},{3,11},{4,12},{5,13},{6,14},{7,15},{8,0},{9,1},... | collective-permute-start | bytes 1277960 | tf_op jit(solution)/shard_map/ppermute | solution.py:36
  50.6 7.3 %collective-permute-start.8 = (bf16[64,3328]{1,0:T(8,128)(2,1)S(1)}, bf16[64,3328]{1,0:T(8,128)(2,1)S(1)}, u32[]{:S(2)}, u32[]{:S(2)}) collective-permute-start(bf16[64,3328]{1,0:T(8,128)(2,1)S(1)} %collective-permute-done.3.refs_0_), channel_id=1, source_target_pairs={{0,32},{1,33},{2,34},{3,35},{4,36},{5,37},{6,38},{7,39},{8,232},{9... | collective-permute-start | bytes 1277960 | tf_op jit(solution)/shard_map/ppermute | solution.py:36
  52.2 5.8 %collective-permute-start.9 = (bf16[64,3328]{1,0:T(8,128)(2,1)S(1)}, bf16[64,3328]{1,0:T(8,128)(2,1)S(1)}, u32[]{:S(2)}, u32[]{:S(2)}) collective-permute-start(bf16[64,3328]{1,0:T(8,128)(2,1)S(1)} %collective-permute-done.3.refs_0_), channel_id=1, source_target_pairs={{0,8},{1,9},{2,10},{3,11},{4,12},{5,13},{6,14},{7,15},{8,0},{9,1},... | collective-permute-start | bytes 1277960 | tf_op jit(solution)/shard_map/ppermute | solution.py:36
  52.2 11.1 %collective-permute-start.19 = (bf16[64,3328]{1,0:T(8,128)(2,1)S(1)}, bf16[64,3328]{1,0:T(8,128)(2,1)S(1)}, u32[]{:S(2)}, u32[]{:S(2)}) collective-permute-start(bf16[64,3328]{1,0:T(8,128)(2,1)S(1)} %constant_dynamic-update-slice_fusion.2.far_own_ref), channel_id=1, source_target_pairs={{0,4},{1,5},{2,6},{3,7},{4,0},{5,1},{6,2},{7,3},{8,12},{9,13},{10,... | collective-permute-start | bytes 1277960 | tf_op jit(solution)/shard_map/ppermute | solution.py:36
  54.5 11.6 %collective-permute-start.16 = (bf16[64,3328]{1,0:T(8,128)(2,1)S(1)}, bf16[64,3328]{1,0:T(8,128)(2,1)S(1)}, u32[]{:S(2)}, u32[]{:S(2)}) collective-permute-start(bf16[64,3328]{1,0:T(8,128)(2,1)S(1)} %collective-permute-done.14.refs_2_), channel_id=1, source_target_pairs={{0,8},{1,9},{2,10},{3,11},{4,12},{5,13},{6,14},{7,15},{8,0},{9,1},... | collective-permute-start | bytes 1277960 | tf_op jit(solution)/shard_map/ppermute | solution.py:36
  55.3 9.3 %collective-permute-start.21 = (bf16[32,3328]{1,0:T(8,128)(2,1)S(1)}, bf16[32,3328]{1,0:T(8,128)(2,1)S(1)}, u32[]{:S(2)}, u32[]{:S(2)}) collective-permute-start(bf16[32,3328]{1,0:T(8,128)(2,1)S(1)} %slice.16), channel_id=1, source_target_pairs={{0,32},{1,33},{2,34},{3,35},{4,36},{5,37},{6,38},{7,39},{8,232},{9... | collective-permute-start | bytes 638984 | tf_op jit(solution)/shard_map/ppermute | solution.py:36
  57.9 9.2 %collective-permute-start.10 = (bf16[32,3328]{1,0:T(8,128)(2,1)S(1)}, bf16[32,3328]{1,0:T(8,128)(2,1)S(1)}, u32[]{:S(2)}, u32[]{:S(2)}) collective-permute-start(bf16[32,3328]{1,0:T(8,128)(2,1)S(1)} %slice.14), channel_id=1, source_target_pairs={{0,32},{1,33},{2,34},{3,35},{4,36},{5,37},{6,38},{7,39},{8,232},{9... | collective-permute-start | bytes 638984 | tf_op jit(solution)/shard_map/ppermute | solution.py:36
  61.1 7.6 %collective-permute-start.20 = (bf16[64,3328]{1,0:T(8,128)(2,1)S(1)}, bf16[64,3328]{1,0:T(8,128)(2,1)S(1)}, u32[]{:S(2)}, u32[]{:S(2)}) collective-permute-start(bf16[64,3328]{1,0:T(8,128)(2,1)S(1)} %collective-permute-done.8.refs_0_), channel_id=1, source_target_pairs={{0,8},{1,9},{2,10},{3,11},{4,12},{5,13},{6,14},{7,15},{8,0},{9,1},... | collective-permute-start | bytes 1277960 | tf_op jit(solution)/shard_map/ppermute | solution.py:36
  64.6 2.8 %collective-permute-start.22 = (bf16[32,3328]{1,0:T(8,128)(2,1)S(1)}, bf16[32,3328]{1,0:T(8,128)(2,1)S(1)}, u32[]{:S(2)}, u32[]{:S(2)}) collective-permute-start(bf16[32,3328]{1,0:T(8,128)(2,1)S(1)} %collective-permute-done.21.refs_2_), channel_id=1, source_target_pairs={{0,8},{1,9},{2,10},{3,11},{4,12},{5,13},{6,14},{7,15},{8,0},{9,1},... | collective-permute-start | bytes 638984 | tf_op jit(solution)/shard_map/ppermute | solution.py:36
  67.2 1.6 %collective-permute-start.23 = (bf16[32,3328]{1,0:T(8,128)(2,1)S(1)}, bf16[32,3328]{1,0:T(8,128)(2,1)S(1)}, u32[]{:S(2)}, u32[]{:S(2)}) collective-permute-start(bf16[32,3328]{1,0:T(8,128)(2,1)S(1)} %collective-permute-done.10.refs_4_), channel_id=1, source_target_pairs={{0,8},{1,9},{2,10},{3,11},{4,12},{5,13},{6,14},{7,15},{8,0},{9,1},... | collective-permute-start | bytes 638984 | tf_op jit(solution)/shard_map/ppermute | solution.py:36
  98.9 14.3 %all-to-all-start.2 = ((s16[8,144,256]{2,1,0:T(8,128)(2,1)}), s16[8,144,256]{2,1,0:T(8,128)(2,1)S(1)}, u32[]{:S(2)}, u32[]{:S(2)}) async-start(s16[8,144,256]{2,1,0:T(8,128)(2,1)} %shard_map.58), calls=%async_computation.2 | async-start | bytes 1179648 | tf_op jit(solution)/shard_map/all_to_all | solution.py:397

commit v5 on v4

--- a/solution.py
+++ b/solution.py
@@ -216,8 +216,11 @@
         steps.append(jnp.clip(scaled, -32767.0, 32767.0))
         marks.append(exponent)
     marks += [jnp.zeros_like(marks[0])] * (MARKS - len(marks))
-    coded = jnp.concatenate(steps + marks, axis=0)
-    return coded.astype(jnp.int32).astype(jnp.int16)
+    return jnp.concatenate(steps, axis=0), jnp.concatenate(marks, axis=0)
+
+
+def to_16_bits(values):
+    return values.astype(jnp.int32).astype(jnp.int16)
 
 
 def steps_of(coded_ref, strip):
@@ -241,6 +244,7 @@
     )
     depth = square.shape[0] // SLOTS
     coded = code([square[place * depth : (place + 1) * depth] for place in range(SLOTS)])
+    coded = to_16_bits(jnp.concatenate(coded, axis=0))
     for col in range(COL):
         spread_ref[col] = coded
 
@@ -259,7 +263,7 @@
     )
 
 
-def cube_kernel(table_ref, factor_ref, got_ref, coded_ref, whole, total, *, scale):
+def cube_kernel(table_ref, factor_ref, got_ref, coded_ref, whole, held, held_marks, *, scale):
     count = table_ref.shape[0]
     row = lax.axis_index("row")
     cols, rows, _ = got_ref.shape
@@ -271,17 +275,23 @@
             steps = got_ref[strip, place * depth : (place + 1) * depth, :]
             square = decode(steps, sizes[place : place + 1])
             whole[start : start + depth, :] = square.astype(jnp.bfloat16)
-    total[...] = scale * jnp.dot(
-        factor_ref[...], whole[...], preferred_element_type=jnp.float32
-    )
+    total = scale * jnp.dot(factor_ref[...], whole[...], preferred_element_type=jnp.float32)
+    steps, marks = code([total[place * depth : (place + 1) * depth] for place in range(SLOTS)])
+    held[...] = to_16_bits(steps)
+    held_marks[...] = marks
     per_col = count // cols
     for to in range(cols):
-        values = []
+        marks = []
         for spot in range(per_col):
             place = table_ref[row, to * per_col + spot]
-            start = pl.multiple_of(jnp.maximum(place, 0) * depth, depth)
-            values.append(jnp.where(place >= 0, total[pl.ds(start, depth), :], 0.0))
-        coded_ref[to] = code(values)
+            first = jnp.maximum(place, 0)
+            block = held[pl.ds(pl.multiple_of(first * depth, depth), depth), :]
+            coded_ref[to, spot * depth : (spot + 1) * depth, :] = jnp.where(
+                place >= 0, block, jnp.zeros_like(block)
+            )
+            marks.append(held_marks[pl.ds(first, 1), :])
+        marks += [jnp.zeros_like(marks[0])] * (MARKS - per_col)
+        coded_ref[to, per_col * depth :, :] = to_16_bits(jnp.concatenate(marks, axis=0))
 
 
 def cube_strips(table, factor, got, scale):
@@ -295,7 +305,8 @@
         (table, factor, got),
         scratch_shapes=[
             pltpu.VMEM((SLOTS * TILE, TILE), jnp.bfloat16),
-            pltpu.VMEM((SLOTS * depth, TILE), jnp.float32),
+            pltpu.VMEM((SLOTS * depth, TILE), jnp.int16),
+            pltpu.VMEM((MARKS, TILE), jnp.float32),
         ],
     )
 
@@ -347,15 +358,15 @@
     near = [jnp.concatenate([packed, to_other_core(packed)], 0)]
     far = [jnp.concatenate([across, to_other_core(across)], 0)]
 
+    far.append(along_z(far[0]))
     near.append(along_z(near[0]))
-    far.append(along_z(far[0]))
     next_x = along_x(near[0])
     own = jnp.concatenate([packed, next_x[:depth]], 0)
     other = to_other_y_lo(own)
     far_own = jnp.concatenate([to_other_core(next_x[depth:]), along_x(next_x[:depth])], 0)
     far_other = to_other_y_lo(far_own)
+    far.append(along_z(far[1]))
     near.append(along_z(near[1]))
-    far.append(along_z(far[1]))
     near_swapped, far_swapped = [None], [None]
 
     def swap(block, swapped, hold):
@@ -377,13 +388,12 @@
     factor = grow(table, None, [(near[0], (0, 0, 0)), (far[0], (0, 1, 0))] + both(1, 0), depth)
     near[3], factor = lax.optimization_barrier((near[3], factor))
     near.append(along_z(near[3][:depth]))
-    far[3] = swap(far[2], far_swapped, far[3])
+    far_swapped.append(to_other_core(far[2]))
     far.append(along_z(far[3][:depth]))
-    factor = grow(table, factor, both(1, 1) + both(2, 0), depth)
     for step in (3, 4):
         near_swapped.append(to_other_core(near[step]))
     far_swapped.append(to_other_core(far[3]))
-    factor = grow(table, factor, both(2, 1) + both(3, 0), depth)
+    factor = grow(table, factor, both(1, 1) + both(2, 0) + both(2, 1) + both(3, 0), depth)
     band = join(own, far_own, other, far_other)
     far[4], factor, band = lax.optimization_barrier((far[4], factor, band))
     far_swapped.append(to_other_core(far[4]))

time: 115 us -> 114 us (level)
    pallas_call x10 -> x9, Pallas kernels: 14.1 us -> 13.6 us  [call(): pl.pallas_call(kernel, out_shape=out_shape, in_specs=[SMEM] * tables + [V...]
where the time goes in v5:
time: 114 us
  starting transfers between devices  46.3 us (41%)
  waiting for transfers between devices  26.7 us (23%)
  blocking collectives  25.4 us (22%)
  Pallas kernels  13.6 us (12%)
  local copies, waits for them, and re-layouts  1.57 us (1%)
    ppermute x24, starting transfers between devices, move(): return lax.ppermute(block, BOTH, pairs(place))  36.9 us
    all_to_all x1, blocking collectives, local(): got = lax.all_to_all(spread, 'col', 0, 0)  25.4 us
    pallas_call x9, Pallas kernels, call(): pl.pallas_call(kernel, out_shape=out_shape, in_specs=[SMEM] * tables + [V...  13.6 us
    ppermute x24, waiting for transfers between devices, move(): return lax.ppermute(block, BOTH, pairs(place))  9.95 us
    all_to_all x1, waiting for transfers between devices, local(): lax.all_to_all(coded, 'col', 0, 0)  8.69 us
    all_to_all x1, waiting for transfers between devices, local(): strips = lax.all_to_all(density.reshape(COL, depth, columns), 'col', 0, 0)  8.06 us
    all_to_all x1, starting transfers between devices, local(): strips = lax.all_to_all(density.reshape(COL, depth, columns), 'col', 0, 0)  5.87 us
    all_to_all x1, starting transfers between devices, local(): lax.all_to_all(coded, 'col', 0, 0)  3.54 us
  transfers between devices with their start and end apart: 26, of which 9 were waited for; matrix products, arithmetic and copies ran while one was open for 1% of the time, Pallas kernels for 6%

profile of v5, /device:TPU:1, one launch (start us, length us, event | category | flops | bytes accessed | tf_op | source)
XLA Modules:
  0.0 114.4 jit_solution(12590675079046825902)
XLA Ops:
  0.6 5.9 %all-to-all-start = ((bf16[8,32,1024]{2,1,0:T(8,128)(2,1)}), bf16[8,32,1024]{2,1,0:T(8,128)(2,1)S(1)}, u32[]{:S(2)}, u32[]{:S(2)}) async-start(bf16[8,32,1024]{2,1,0:T(8,128)(2,1)} %bitcast.2), calls=%async_computation | async-start | bytes 1048576 | tf_op jit(solution)/shard_map/all_to_all | solution.py:355
  8.6 8.1 %all-to-all-done.strips_ref = bf16[8,32,1024]{2,1,0:T(8,128)(2,1)S(1)} async-done(((bf16[8,32,1024]{2,1,0:T(8,128)(2,1)}), bf16[8,32,1024]{2,1,0:T(8,128)(2,1)S(1)}, u32[]{:S(2)}, u32[]{:S(2)}) %all-to-all-start) | async-done | bytes 524320 | tf_op jit(solution)/shard_map/all_to_all | solution.py:355
  17.6 0.9 collective-permute-start.5
  18.6 2.6 %collective-permute-start = (bf16[32,3328]{1,0:T(8,128)(2,1)S(1)}, bf16[32,3328]{1,0:T(8,128)(2,1)S(1)}, u32[]{:S(2)}, u32[]{:S(2)}) collective-permute-start(bf16[32,3328]{1,0:T(8,128)(2,1)S(1)} %shard_map.51), channel_id=1, source_target_pairs={{0,16},{1,17},{2,18},{3,19},{4,20},{5,21},{6,22},{7,23},{8,24},{9,... | collective-permute-start | bytes 638984 | tf_op jit(solution)/shard_map/ppermute | solution.py:36
  21.9 5.6 %collective-permute-start.10 = (bf16[64,3328]{1,0:T(8,128)(2,1)S(1)}, bf16[64,3328]{1,0:T(8,128)(2,1)S(1)}, u32[]{:S(2)}, u32[]{:S(2)}) collective-permute-start(bf16[64,3328]{1,0:T(8,128)(2,1)S(1)} %pad_maximum_fusion.refs_0_), channel_id=1, source_target_pairs={{0,32},{1,33},{2,34},{3,35},{4,36},{5,37},{6,38},{7,39},{8,232},{9... | collective-permute-start | bytes 1277960 | tf_op jit(solution)/shard_map/ppermute | solution.py:36
  27.8 1.2 %collective-permute-done.1 = bf16[32,3328]{1,0:T(8,128)(2,1)S(1)} collective-permute-done((bf16[32,3328]{1,0:T(8,128)(2,1)S(1)}, bf16[32,3328]{1,0:T(8,128)(2,1)S(1)}, u32[]{:S(2)}, u32[]{:S(2)}) %collective-permute-start.1) | collective-permute-done | bytes 213024 | tf_op jit(solution)/shard_map/ppermute | solution.py:36
  29.0 5.5 %collective-permute-start.2 = (bf16[64,3328]{1,0:T(8,128)(2,1)S(1)}, bf16[64,3328]{1,0:T(8,128)(2,1)S(1)}, u32[]{:S(2)}, u32[]{:S(2)}) collective-permute-start(bf16[64,3328]{1,0:T(8,128)(2,1)S(1)} %constant_dynamic-update-slice_fusion.refs_1_), channel_id=1, source_target_pairs={{0,32},{1,33},{2,34},{3,35},{4,36},{5,37},{6,38},{7,39},{8,232},{9... | collective-permute-start | bytes 1277960 | tf_op jit(solution)/shard_map/ppermute | solution.py:36
  34.7 2.1 %collective-permute-start.11 = (bf16[64,3328]{1,0:T(8,128)(2,1)S(1)}, bf16[64,3328]{1,0:T(8,128)(2,1)S(1)}, u32[]{:S(2)}, u32[]{:S(2)}) collective-permute-start(bf16[64,3328]{1,0:T(8,128)(2,1)S(1)} %collective-permute-done.10.refs_2_), channel_id=1, source_target_pairs={{0,32},{1,33},{2,34},{3,35},{4,36},{5,37},{6,38},{7,39},{8,232},{9... | collective-permute-start | bytes 1277960 | tf_op jit(solution)/shard_map/ppermute | solution.py:36
  37.0 2.5 %collective-permute-done.2.refs_0_ = bf16[64,3328]{1,0:T(8,128)(2,1)S(1)} collective-permute-done((bf16[64,3328]{1,0:T(8,128)(2,1)S(1)}, bf16[64,3328]{1,0:T(8,128)(2,1)S(1)}, u32[]{:S(2)}, u32[]{:S(2)}) %collective-permute-start.2) | collective-permute-done | bytes 426016 | tf_op jit(solution)/shard_map/ppermute | solution.py:36
  39.6 1.7 %collective-permute-start.12 = (bf16[64,3328]{1,0:T(8,128)(2,1)S(1)}, bf16[64,3328]{1,0:T(8,128)(2,1)S(1)}, u32[]{:S(2)}, u32[]{:S(2)}) collective-permute-start(bf16[64,3328]{1,0:T(8,128)(2,1)S(1)} %collective-permute-done.10.refs_2_), channel_id=1, source_target_pairs={{0,8},{1,9},{2,10},{3,11},{4,12},{5,13},{6,14},{7,15},{8,0},{9,1},... | collective-permute-start | bytes 1277960 | tf_op jit(solution)/shard_map/ppermute | solution.py:36
  41.3 1.7 %collective-permute-start.3 = (bf16[64,3328]{1,0:T(8,128)(2,1)S(1)}, bf16[64,3328]{1,0:T(8,128)(2,1)S(1)}, u32[]{:S(2)}, u32[]{:S(2)}) collective-permute-start(bf16[64,3328]{1,0:T(8,128)(2,1)S(1)} %collective-permute-done.2.refs_0_), channel_id=1, source_target_pairs={{0,32},{1,33},{2,34},{3,35},{4,36},{5,37},{6,38},{7,39},{8,232},{9... | collective-permute-start | bytes 1277960 | tf_op jit(solution)/shard_map/ppermute | solution.py:36
  43.0 1.1 collective-permute-done.11.refs_2_
  44.1 1.7 %collective-permute-start.4 = (bf16[64,3328]{1,0:T(8,128)(2,1)S(1)}, bf16[64,3328]{1,0:T(8,128)(2,1)S(1)}, u32[]{:S(2)}, u32[]{:S(2)}) collective-permute-start(bf16[64,3328]{1,0:T(8,128)(2,1)S(1)} %collective-permute-done.2.refs_0_), channel_id=1, source_target_pairs={{0,8},{1,9},{2,10},{3,11},{4,12},{5,13},{6,14},{7,15},{8,0},{9,1},... | collective-permute-start | bytes 1277960 | tf_op jit(solution)/shard_map/ppermute | solution.py:36
  45.9 1.8 %collective-permute-start.13 = (bf16[64,3328]{1,0:T(8,128)(2,1)S(1)}, bf16[64,3328]{1,0:T(8,128)(2,1)S(1)}, u32[]{:S(2)}, u32[]{:S(2)}) collective-permute-start(bf16[64,3328]{1,0:T(8,128)(2,1)S(1)} %collective-permute-done.11.refs_2_), channel_id=1, source_target_pairs={{0,32},{1,33},{2,34},{3,35},{4,36},{5,37},{6,38},{7,39},{8,232},{9... | collective-permute-start | bytes 1277960 | tf_op jit(solution)/shard_map/ppermute | solution.py:36
  47.7 1.0 collective-permute-done.3.refs_4_
  48.7 1.9 %collective-permute-start.14 = (bf16[64,3328]{1,0:T(8,128)(2,1)S(1)}, bf16[64,3328]{1,0:T(8,128)(2,1)S(1)}, u32[]{:S(2)}, u32[]{:S(2)}) collective-permute-start(bf16[64,3328]{1,0:T(8,128)(2,1)S(1)} %collective-permute-done.11.refs_2_), channel_id=1, source_target_pairs={{0,8},{1,9},{2,10},{3,11},{4,12},{5,13},{6,14},{7,15},{8,0},{9,1},... | collective-permute-start | bytes 1277960 | tf_op jit(solution)/shard_map/ppermute | solution.py:36
  50.6 1.5 %collective-permute-start.8 = (bf16[64,3328]{1,0:T(8,128)(2,1)S(1)}, bf16[64,3328]{1,0:T(8,128)(2,1)S(1)}, u32[]{:S(2)}, u32[]{:S(2)}) collective-permute-start(bf16[64,3328]{1,0:T(8,128)(2,1)S(1)} %collective-permute-done.3.refs_4_), channel_id=1, source_target_pairs={{0,32},{1,33},{2,34},{3,35},{4,36},{5,37},{6,38},{7,39},{8,232},{9... | collective-permute-start | bytes 1277960 | tf_op jit(solution)/shard_map/ppermute | solution.py:36
  52.5 2.0 %shard_map.52._ = bf16[416,3328]{1,0:T(8,128)(2,1)S(1)} custom-call(s32[32,64]{1,0:T(8,128)S(1)} %shard_map.50.table_ref, bf16[64,3328]{1,0:T(8,128)(2,1)S(1)} %pad_maximum_fusion.refs_0_, bf16[64,3328]{1,0:T(8,128)(2,1)S(1)} %constant_dynamic-update-slice_fusion.refs_1_, bf16[64,3328]{1,0:T(8,128)(2,1)S(1)} %collective-permute-done.10.refs_2_, ...), custom_call_target="tpu_custom_call" | custom-call | tf_op jit(solution)/shard_map/pallas_call | solution.py:63
  55.3 1.5 %collective-permute-start.21 = (bf16[32,3328]{1,0:T(8,128)(2,1)S(1)}, bf16[32,3328]{1,0:T(8,128)(2,1)S(1)}, u32[]{:S(2)}, u32[]{:S(2)}) collective-permute-start(bf16[32,3328]{1,0:T(8,128)(2,1)S(1)} %slice.16), channel_id=1, source_target_pairs={{0,32},{1,33},{2,34},{3,35},{4,36},{5,37},{6,38},{7,39},{8,232},{9... | collective-permute-start | bytes 638984 | tf_op jit(solution)/shard_map/ppermute | solution.py:36
  56.8 1.1 collective-permute-done.8.refs_0_
  57.9 3.1 %collective-permute-start.9 = (bf16[32,3328]{1,0:T(8,128)(2,1)S(1)}, bf16[32,3328]{1,0:T(8,128)(2,1)S(1)}, u32[]{:S(2)}, u32[]{:S(2)}) collective-permute-start(bf16[32,3328]{1,0:T(8,128)(2,1)S(1)} %slice.18), channel_id=1, source_target_pairs={{0,32},{1,33},{2,34},{3,35},{4,36},{5,37},{6,38},{7,39},{8,232},{9... | collective-permute-start | bytes 638984 | tf_op jit(solution)/shard_map/ppermute | solution.py:36
  61.1 1.8 %collective-permute-done.19.far_other_ref = bf16[64,3328]{1,0:T(8,128)(2,1)S(1)} collective-permute-done((bf16[64,3328]{1,0:T(8,128)(2,1)S(1)}, bf16[64,3328]{1,0:T(8,128)(2,1)S(1)}, u32[]{:S(2)}, u32[]{:S(2)}) %collective-permute-start.19) | collective-permute-done | bytes 426016 | tf_op jit(solution)/shard_map/ppermute | solution.py:36
  63.6 1.4 %shard_map.53._ = bf16[416,3328]{1,0:T(8,128)(2,1)S(1)} custom-call(s32[32,64]{1,0:T(8,128)S(1)} %shard_map.50.table_ref, bf16[416,3328]{1,0:T(8,128)(2,1)S(1)} %shard_map.52._, bf16[64,3328]{1,0:T(8,128)(2,1)S(1)} %collective-permute-done.2.refs_0_, bf16[64,3328]{1,0:T(8,128)(2,1)S(1)} %collective-permute-done.4.refs_1_, ...), custom_call_target="tpu_custom_call", output_to_operand_aliasing={{}: (1, {})} | custom-call | tf_op jit(solution)/shard_map/pallas_call | solution.py:63
  65.0 2.2 %collective-permute-start.23 = (bf16[32,3328]{1,0:T(8,128)(2,1)S(1)}, bf16[32,3328]{1,0:T(8,128)(2,1)S(1)}, u32[]{:S(2)}, u32[]{:S(2)}) collective-permute-start(bf16[32,3328]{1,0:T(8,128)(2,1)S(1)} %collective-permute-done.9.refs_4_), channel_id=1, source_target_pairs={{0,8},{1,9},{2,10},{3,11},{4,12},{5,13},{6,14},{7,15},{8,0},{9,1},... | collective-permute-start | bytes 638984 | tf_op jit(solution)/shard_map/ppermute | solution.py:36
  67.2 1.1 collective-permute-done.23.refs_5_
  68.3 2.3 %shard_map.55 = (s16[8,432,256]{2,1,0:T(8,128)(2,1)S(1)}, bf16[416,3328]{1,0:T(8,128)(2,1)S(1)}) custom-call(s32[32,64]{1,0:T(8,128)S(1)} %shard_map.50.table_ref, bf16[416,3328]{1,0:T(8,128)(2,1)S(1)} %shard_map.53._, bf16[256,3328]{1,0:T(8,128)(2,1)S(1)} %shard_map.54.band_ref, ...), custom_call_target="tpu_custom_call", output_to_operand_aliasing={{1}: (1, {})} | custom-call | tf_op jit(solution)/shard_map/pallas_call | solution.py:63
  70.6 25.4 %all_to_all.15.got_ref = s16[8,432,256]{2,1,0:T(8,128)(2,1)S(1)} all-to-all(s16[8,432,256]{2,1,0:T(8,128)(2,1)S(1)} %get-tuple-element.30), channel_id=1, replica_groups=mesh['row'=32,'col'=8] {'col'}, dimensions={0} | all-to-all | bytes 3538944 | tf_op jit(solution)/shard_map/all_to_all | solution.py:403
  96.1 2.7 %shard_map.57 = s16[8,144,256]{2,1,0:T(8,128)(2,1)} custom-call(s32[32,64]{1,0:T(8,128)S(1)} %shard_map.50.table_ref, bf16[416,3328]{1,0:T(8,128)(2,1)S(1)} %get-tuple-element.31.factor_ref, s16[8,432,256]{2,1,0:T(8,128)(2,1)S(1)} %all_to_all.15.got_ref), custom_call_target="tpu_custom_call" | custom-call | tf_op jit(solution)/shard_map/pallas_call | solution.py:63
  98.8 3.5 %all-to-all-start.2 = ((s16[8,144,256]{2,1,0:T(8,128)(2,1)}), s16[8,144,256]{2,1,0:T(8,128)(2,1)S(1)}, u32[]{:S(2)}, u32[]{:S(2)}) async-start(s16[8,144,256]{2,1,0:T(8,128)(2,1)} %shard_map.57), calls=%async_computation.2 | async-start | bytes 1179648 | tf_op jit(solution)/shard_map/all_to_all | solution.py:407
  102.3 2.1 %shard_map.56 = f32[256,1024]{1,0:T(8,128)} custom-call(s32[32,64]{1,0:T(8,128)S(1)} %shard_map.50.table_ref, s16[8,432,256]{2,1,0:T(8,128)(2,1)S(1)} %all_to_all.15.got_ref), custom_call_target="tpu_custom_call" | custom-call | tf_op jit(solution)/shard_map/pallas_call | solution.py:63
  104.4 8.7 %all-to-all-done.2.got_ref = s16[8,144,256]{2,1,0:T(8,128)(2,1)S(1)} async-done(((s16[8,144,256]{2,1,0:T(8,128)(2,1)}), s16[8,144,256]{2,1,0:T(8,128)(2,1)S(1)}, u32[]{:S(2)}, u32[]{:S(2)}) %all-to-all-start.2) | async-done | bytes 589856 | tf_op jit(solution)/shard_map/all_to_all | solution.py:407
  113.1 1.3 %shard_map.58 = f32[256,1024]{1,0:T(8,128)} custom-call(s16[8,144,256]{2,1,0:T(8,128)(2,1)S(1)} %all-to-all-done.2.got_ref), custom_call_target="tpu_custom_call" | custom-call | tf_op jit(solution)/shard_map/pallas_call | solution.py:63
  (42 shorter events, 6.4 us)
Async XLA Ops:
  0.6 16.1 %all-to-all-start = ((bf16[8,32,1024]{2,1,0:T(8,128)(2,1)}), bf16[8,32,1024]{2,1,0:T(8,128)(2,1)S(1)}, u32[]{:S(2)}, u32[]{:S(2)}) async-start(bf16[8,32,1024]{2,1,0:T(8,128)(2,1)} %bitcast.2), calls=%async_computation | async-start | bytes 1048576 | tf_op jit(solution)/shard_map/all_to_all | solution.py:355
  7.2 0.7 copy-start
  17.6 3.6 %collective-permute-start.5 = (bf16[32,3328]{1,0:T(8,128)(2,1)S(1)}, bf16[32,3328]{1,0:T(8,128)(2,1)S(1)}, u32[]{:S(2)}, u32[]{:S(2)}) collective-permute-start(bf16[32,3328]{1,0:T(8,128)(2,1)S(1)} %shard_map.51), channel_id=1, source_target_pairs={{0,8},{1,9},{2,10},{3,11},{4,12},{5,13},{6,14},{7,15},{8,0},{9,1},... | collective-permute-start | bytes 638984 | tf_op jit(solution)/shard_map/ppermute | solution.py:36
  18.6 9.0 %collective-permute-start = (bf16[32,3328]{1,0:T(8,128)(2,1)S(1)}, bf16[32,3328]{1,0:T(8,128)(2,1)S(1)}, u32[]{:S(2)}, u32[]{:S(2)}) collective-permute-start(bf16[32,3328]{1,0:T(8,128)(2,1)S(1)} %shard_map.51), channel_id=1, source_target_pairs={{0,16},{1,17},{2,18},{3,19},{4,20},{5,21},{6,22},{7,23},{8,24},{9,... | collective-permute-start | bytes 638984 | tf_op jit(solution)/shard_map/ppermute | solution.py:36
  21.2 13.3 %collective-permute-start.6 = (bf16[64,3328]{1,0:T(8,128)(2,1)S(1)}, bf16[64,3328]{1,0:T(8,128)(2,1)S(1)}, u32[]{:S(2)}, u32[]{:S(2)}) collective-permute-start(bf16[64,3328]{1,0:T(8,128)(2,1)S(1)} %pad_maximum_fusion.refs_0_), channel_id=1, source_target_pairs={{0,1},{1,2},{2,3},{3,0},{4,5},{5,6},{6,7},{7,4},{8,11},{9,8},{10,9... | collective-permute-start | bytes 1277960 | tf_op jit(solution)/shard_map/ppermute | solution.py:36
  21.9 12.7 %collective-permute-start.10 = (bf16[64,3328]{1,0:T(8,128)(2,1)S(1)}, bf16[64,3328]{1,0:T(8,128)(2,1)S(1)}, u32[]{:S(2)}, u32[]{:S(2)}) collective-permute-start(bf16[64,3328]{1,0:T(8,128)(2,1)S(1)} %pad_maximum_fusion.refs_0_), channel_id=1, source_target_pairs={{0,32},{1,33},{2,34},{3,35},{4,36},{5,37},{6,38},{7,39},{8,232},{9... | collective-permute-start | bytes 1277960 | tf_op jit(solution)/shard_map/ppermute | solution.py:36
  27.5 1.5 %collective-permute-start.1 = (bf16[32,3328]{1,0:T(8,128)(2,1)S(1)}, bf16[32,3328]{1,0:T(8,128)(2,1)S(1)}, u32[]{:S(2)}, u32[]{:S(2)}) collective-permute-start(bf16[32,3328]{1,0:T(8,128)(2,1)S(1)} %collective-permute-done), channel_id=1, source_target_pairs={{0,8},{1,9},{2,10},{3,11},{4,12},{5,13},{6,14},{7,15},{8,0},{9,1},... | collective-permute-start | bytes 638984 | tf_op jit(solution)/shard_map/ppermute | solution.py:36
  29.0 10.6 %collective-permute-start.2 = (bf16[64,3328]{1,0:T(8,128)(2,1)S(1)}, bf16[64,3328]{1,0:T(8,128)(2,1)S(1)}, u32[]{:S(2)}, u32[]{:S(2)}) collective-permute-start(bf16[64,3328]{1,0:T(8,128)(2,1)S(1)} %constant_dynamic-update-slice_fusion.refs_1_), channel_id=1, source_target_pairs={{0,32},{1,33},{2,34},{3,35},{4,36},{5,37},{6,38},{7,39},{8,232},{9... | collective-permute-start | bytes 1277960 | tf_op jit(solution)/shard_map/ppermute | solution.py:36
  34.5 6.7 %collective-permute-start.17 = (bf16[32,3328]{1,0:T(8,128)(2,1)S(1)}, bf16[32,3328]{1,0:T(8,128)(2,1)S(1)}, u32[]{:S(2)}, u32[]{:S(2)}) collective-permute-start(bf16[32,3328]{1,0:T(8,128)(2,1)S(1)} %get-tuple-element.32), channel_id=1, source_target_pairs={{0,8},{1,9},{2,10},{3,11},{4,12},{5,13},{6,14},{7,15},{8,0},{9,1},... | collective-permute-start | bytes 638984 | tf_op jit(solution)/shard_map/ppermute | solution.py:36
  34.7 9.5 %collective-permute-start.11 = (bf16[64,3328]{1,0:T(8,128)(2,1)S(1)}, bf16[64,3328]{1,0:T(8,128)(2,1)S(1)}, u32[]{:S(2)}, u32[]{:S(2)}) collective-permute-start(bf16[64,3328]{1,0:T(8,128)(2,1)S(1)} %collective-permute-done.10.refs_2_), channel_id=1, source_target_pairs={{0,32},{1,33},{2,34},{3,35},{4,36},{5,37},{6,38},{7,39},{8,232},{9... | collective-permute-start | bytes 1277960 | tf_op jit(solution)/shard_map/ppermute | solution.py:36
  36.7 15.4 %collective-permute-start.18 = (bf16[32,3328]{1,0:T(8,128)(2,1)S(1)}, bf16[32,3328]{1,0:T(8,128)(2,1)S(1)}, u32[]{:S(2)}, u32[]{:S(2)}) collective-permute-start(bf16[32,3328]{1,0:T(8,128)(2,1)S(1)} %get-tuple-element.33), channel_id=1, source_target_pairs={{0,1},{1,2},{2,3},{3,0},{4,5},{5,6},{6,7},{7,4},{8,11},{9,8},{10,9... | collective-permute-start | bytes 638984 | tf_op jit(solution)/shard_map/ppermute | solution.py:36
  36.8 13.8 %collective-permute-start.7 = (bf16[64,3328]{1,0:T(8,128)(2,1)S(1)}, bf16[64,3328]{1,0:T(8,128)(2,1)S(1)}, u32[]{:S(2)}, u32[]{:S(2)}) collective-permute-start(bf16[64,3328]{1,0:T(8,128)(2,1)S(1)} %pad_maximum_fusion.1.own_ref), channel_id=1, source_target_pairs={{0,4},{1,5},{2,6},{3,7},{4,0},{5,1},{6,2},{7,3},{8,12},{9,13},{10,... | collective-permute-start | bytes 1277960 | tf_op jit(solution)/shard_map/ppermute | solution.py:36
  39.6 6.3 %collective-permute-start.12 = (bf16[64,3328]{1,0:T(8,128)(2,1)S(1)}, bf16[64,3328]{1,0:T(8,128)(2,1)S(1)}, u32[]{:S(2)}, u32[]{:S(2)}) collective-permute-start(bf16[64,3328]{1,0:T(8,128)(2,1)S(1)} %collective-permute-done.10.refs_2_), channel_id=1, source_target_pairs={{0,8},{1,9},{2,10},{3,11},{4,12},{5,13},{6,14},{7,15},{8,0},{9,1},... | collective-permute-start | bytes 1277960 | tf_op jit(solution)/shard_map/ppermute | solution.py:36
  41.3 7.4 %collective-permute-start.3 = (bf16[64,3328]{1,0:T(8,128)(2,1)S(1)}, bf16[64,3328]{1,0:T(8,128)(2,1)S(1)}, u32[]{:S(2)}, u32[]{:S(2)}) collective-permute-start(bf16[64,3328]{1,0:T(8,128)(2,1)S(1)} %collective-permute-done.2.refs_0_), channel_id=1, source_target_pairs={{0,32},{1,33},{2,34},{3,35},{4,36},{5,37},{6,38},{7,39},{8,232},{9... | collective-permute-start | bytes 1277960 | tf_op jit(solution)/shard_map/ppermute | solution.py:36
  44.1 6.5 %collective-permute-start.4 = (bf16[64,3328]{1,0:T(8,128)(2,1)S(1)}, bf16[64,3328]{1,0:T(8,128)(2,1)S(1)}, u32[]{:S(2)}, u32[]{:S(2)}) collective-permute-start(bf16[64,3328]{1,0:T(8,128)(2,1)S(1)} %collective-permute-done.2.refs_0_), channel_id=1, source_target_pairs={{0,8},{1,9},{2,10},{3,11},{4,12},{5,13},{6,14},{7,15},{8,0},{9,1},... | collective-permute-start | bytes 1277960 | tf_op jit(solution)/shard_map/ppermute | solution.py:36
  45.9 8.8 %collective-permute-start.13 = (bf16[64,3328]{1,0:T(8,128)(2,1)S(1)}, bf16[64,3328]{1,0:T(8,128)(2,1)S(1)}, u32[]{:S(2)}, u32[]{:S(2)}) collective-permute-start(bf16[64,3328]{1,0:T(8,128)(2,1)S(1)} %collective-permute-done.11.refs_2_), channel_id=1, source_target_pairs={{0,32},{1,33},{2,34},{3,35},{4,36},{5,37},{6,38},{7,39},{8,232},{9... | collective-permute-start | bytes 1277960 | tf_op jit(solution)/shard_map/ppermute | solution.py:36
  48.7 5.9 %collective-permute-start.14 = (bf16[64,3328]{1,0:T(8,128)(2,1)S(1)}, bf16[64,3328]{1,0:T(8,128)(2,1)S(1)}, u32[]{:S(2)}, u32[]{:S(2)}) collective-permute-start(bf16[64,3328]{1,0:T(8,128)(2,1)S(1)} %collective-permute-done.11.refs_2_), channel_id=1, source_target_pairs={{0,8},{1,9},{2,10},{3,11},{4,12},{5,13},{6,14},{7,15},{8,0},{9,1},... | collective-permute-start | bytes 1277960 | tf_op jit(solution)/shard_map/ppermute | solution.py:36
  50.6 7.3 %collective-permute-start.8 = (bf16[64,3328]{1,0:T(8,128)(2,1)S(1)}, bf16[64,3328]{1,0:T(8,128)(2,1)S(1)}, u32[]{:S(2)}, u32[]{:S(2)}) collective-permute-start(bf16[64,3328]{1,0:T(8,128)(2,1)S(1)} %collective-permute-done.3.refs_4_), channel_id=1, source_target_pairs={{0,32},{1,33},{2,34},{3,35},{4,36},{5,37},{6,38},{7,39},{8,232},{9... | collective-permute-start | bytes 1277960 | tf_op jit(solution)/shard_map/ppermute | solution.py:36
  52.2 10.7 %collective-permute-start.19 = (bf16[64,3328]{1,0:T(8,128)(2,1)S(1)}, bf16[64,3328]{1,0:T(8,128)(2,1)S(1)}, u32[]{:S(2)}, u32[]{:S(2)}) collective-permute-start(bf16[64,3328]{1,0:T(8,128)(2,1)S(1)} %constant_dynamic-update-slice_fusion.2.far_own_ref), channel_id=1, source_target_pairs={{0,4},{1,5},{2,6},{3,7},{4,0},{5,1},{6,2},{7,3},{8,12},{9,13},{10,... | collective-permute-start | bytes 1277960 | tf_op jit(solution)/shard_map/ppermute | solution.py:36
  54.5 9.1 %collective-permute-start.15 = (bf16[64,3328]{1,0:T(8,128)(2,1)S(1)}, bf16[64,3328]{1,0:T(8,128)(2,1)S(1)}, u32[]{:S(2)}, u32[]{:S(2)}) collective-permute-start(bf16[64,3328]{1,0:T(8,128)(2,1)S(1)} %collective-permute-done.3.refs_4_), channel_id=1, source_target_pairs={{0,8},{1,9},{2,10},{3,11},{4,12},{5,13},{6,14},{7,15},{8,0},{9,1},... | collective-permute-start | bytes 1277960 | tf_op jit(solution)/shard_map/ppermute | solution.py:36
  54.6 9.0 %collective-permute-start.16 = (bf16[64,3328]{1,0:T(8,128)(2,1)S(1)}, bf16[64,3328]{1,0:T(8,128)(2,1)S(1)}, u32[]{:S(2)}, u32[]{:S(2)}) collective-permute-start(bf16[64,3328]{1,0:T(8,128)(2,1)S(1)} %collective-permute-done.13.refs_6_), channel_id=1, source_target_pairs={{0,8},{1,9},{2,10},{3,11},{4,12},{5,13},{6,14},{7,15},{8,0},{9,1},... | collective-permute-start | bytes 1277960 | tf_op jit(solution)/shard_map/ppermute | solution.py:36
  55.3 7.7 %collective-permute-start.21 = (bf16[32,3328]{1,0:T(8,128)(2,1)S(1)}, bf16[32,3328]{1,0:T(8,128)(2,1)S(1)}, u32[]{:S(2)}, u32[]{:S(2)}) collective-permute-start(bf16[32,3328]{1,0:T(8,128)(2,1)S(1)} %slice.16), channel_id=1, source_target_pairs={{0,32},{1,33},{2,34},{3,35},{4,36},{5,37},{6,38},{7,39},{8,232},{9... | collective-permute-start | bytes 638984 | tf_op jit(solution)/shard_map/ppermute | solution.py:36
  57.9 7.1 %collective-permute-start.9 = (bf16[32,3328]{1,0:T(8,128)(2,1)S(1)}, bf16[32,3328]{1,0:T(8,128)(2,1)S(1)}, u32[]{:S(2)}, u32[]{:S(2)}) collective-permute-start(bf16[32,3328]{1,0:T(8,128)(2,1)S(1)} %slice.18), channel_id=1, source_target_pairs={{0,32},{1,33},{2,34},{3,35},{4,36},{5,37},{6,38},{7,39},{8,232},{9... | collective-permute-start | bytes 638984 | tf_op jit(solution)/shard_map/ppermute | solution.py:36
  62.8 5.4 %collective-permute-start.20 = (bf16[64,3328]{1,0:T(8,128)(2,1)S(1)}, bf16[64,3328]{1,0:T(8,128)(2,1)S(1)}, u32[]{:S(2)}, u32[]{:S(2)}) collective-permute-start(bf16[64,3328]{1,0:T(8,128)(2,1)S(1)} %collective-permute-done.8.refs_0_), channel_id=1, source_target_pairs={{0,8},{1,9},{2,10},{3,11},{4,12},{5,13},{6,14},{7,15},{8,0},{9,1},... | collective-permute-start | bytes 1277960 | tf_op jit(solution)/shard_map/ppermute | solution.py:36
  63.0 4.2 %collective-permute-start.22 = (bf16[32,3328]{1,0:T(8,128)(2,1)S(1)}, bf16[32,3328]{1,0:T(8,128)(2,1)S(1)}, u32[]{:S(2)}, u32[]{:S(2)}) collective-permute-start(bf16[32,3328]{1,0:T(8,128)(2,1)S(1)} %collective-permute-done.21.refs_2_), channel_id=1, source_target_pairs={{0,8},{1,9},{2,10},{3,11},{4,12},{5,13},{6,14},{7,15},{8,0},{9,1},... | collective-permute-start | bytes 638984 | tf_op jit(solution)/shard_map/ppermute | solution.py:36
  65.0 3.3 %collective-permute-start.23 = (bf16[32,3328]{1,0:T(8,128)(2,1)S(1)}, bf16[32,3328]{1,0:T(8,128)(2,1)S(1)}, u32[]{:S(2)}, u32[]{:S(2)}) collective-permute-start(bf16[32,3328]{1,0:T(8,128)(2,1)S(1)} %collective-permute-done.9.refs_4_), channel_id=1, source_target_pairs={{0,8},{1,9},{2,10},{3,11},{4,12},{5,13},{6,14},{7,15},{8,0},{9,1},... | collective-permute-start | bytes 638984 | tf_op jit(solution)/shard_map/ppermute | solution.py:36
  98.8 14.4 %all-to-all-start.2 = ((s16[8,144,256]{2,1,0:T(8,128)(2,1)}), s16[8,144,256]{2,1,0:T(8,128)(2,1)S(1)}, u32[]{:S(2)}, u32[]{:S(2)}) async-start(s16[8,144,256]{2,1,0:T(8,128)(2,1)} %shard_map.57), calls=%async_computation.2 | async-start | bytes 1179648 | tf_op jit(solution)/shard_map/all_to_all | solution.py:407

commit v6 on v5

--- a/solution.py
+++ b/solution.py
@@ -263,19 +263,25 @@
     )
 
 
-def cube_kernel(table_ref, factor_ref, got_ref, coded_ref, whole, held, held_marks, *, scale):
+def cube_kernel(table_ref, factor_ref, got_ref, coded_ref, held, held_marks, *, scale):
     count = table_ref.shape[0]
     row = lax.axis_index("row")
     cols, rows, _ = got_ref.shape
     depth = (rows - MARKS) // SLOTS
-    for strip in range(cols):
-        sizes = steps_of(got_ref, strip)
-        for place in range(SLOTS):
-            start = place * TILE + strip * depth
+    sizes = [steps_of(got_ref, strip) for strip in range(cols)]
+    total = jnp.zeros((SLOTS * depth, got_ref.shape[2]), jnp.float32)
+    for place in range(SLOTS):
+        tile = []
+        for strip in range(cols):
             steps = got_ref[strip, place * depth : (place + 1) * depth, :]
-            square = decode(steps, sizes[place : place + 1])
-            whole[start : start + depth, :] = square.astype(jnp.bfloat16)
-    total = scale * jnp.dot(factor_ref[...], whole[...], preferred_element_type=jnp.float32)
+            square = decode(steps, sizes[strip][place : place + 1])
+            tile.append(square.astype(jnp.bfloat16))
+        total += jnp.dot(
+            factor_ref[:, place * TILE : (place + 1) * TILE],
+            jnp.concatenate(tile, axis=0),
+            preferred_element_type=jnp.float32,
+        )
+    total *= scale
     steps, marks = code([total[place * depth : (place + 1) * depth] for place in range(SLOTS)])
     held[...] = to_16_bits(steps)
     held_marks[...] = marks
@@ -304,7 +310,6 @@
         shape,
         (table, factor, got),
         scratch_shapes=[
-            pltpu.VMEM((SLOTS * TILE, TILE), jnp.bfloat16),
             pltpu.VMEM((SLOTS * depth, TILE), jnp.int16),
             pltpu.VMEM((MARKS, TILE), jnp.float32),
         ],

time: 114 us -> 115 us (level); the launches traced: 114 us -> 113 us
  transfers between devices with their start and end apart: 26 -> 26, of which waited for: 9 -> 9; matrix products, arithmetic and copies ran while one was open for 1% -> 1% of each run, Pallas kernels for 6% -> 5%
where the time goes in v6:
time: 115 us; the launch traced here: 113 us
  starting transfers between devices  46.8 us (41%)
  waiting for transfers between devices  25.9 us (23%)
  blocking collectives  24.7 us (21%)
  Pallas kernels  13 us (11%)
  local copies, waits for them, and re-layouts  1.57 us (1%)
    ppermute x24, starting transfers between devices, move(): return lax.ppermute(block, BOTH, pairs(place))  37.4 us
    all_to_all x1, blocking collectives, local(): got = lax.all_to_all(spread, 'col', 0, 0)  24.7 us
    pallas_call x9, Pallas kernels, call(): pl.pallas_call(kernel, out_shape=out_shape, in_specs=[SMEM] * tables + [V...  13 us
    ppermute x24, waiting for transfers between devices, move(): return lax.ppermute(block, BOTH, pairs(place))  9.95 us
    all_to_all x1, waiting for transfers between devices, local(): strips = lax.all_to_all(density.reshape(COL, depth, columns), 'col', 0, 0)  8.06 us
    all_to_all x1, waiting for transfers between devices, local(): lax.all_to_all(coded, 'col', 0, 0)  7.9 us
    all_to_all x1, starting transfers between devices, local(): strips = lax.all_to_all(density.reshape(COL, depth, columns), 'col', 0, 0)  5.87 us
    all_to_all x1, starting transfers between devices, local(): lax.all_to_all(coded, 'col', 0, 0)  3.54 us
  transfers between devices with their start and end apart: 26, of which 9 were waited for; matrix products, arithmetic and copies ran while one was open for 1% of the time, Pallas kernels for 5%

profile of v6, /device:TPU:1, one launch (start us, length us, event | category | flops | bytes accessed | tf_op | source)
XLA Modules:
  0.0 112.9 jit_solution(5680077925486241997)
XLA Ops:
  0.6 5.9 %all-to-all-start = ((bf16[8,32,1024]{2,1,0:T(8,128)(2,1)}), bf16[8,32,1024]{2,1,0:T(8,128)(2,1)S(1)}, u32[]{:S(2)}, u32[]{:S(2)}) async-start(bf16[8,32,1024]{2,1,0:T(8,128)(2,1)} %bitcast.2), calls=%async_computation | async-start | bytes 1048576 | tf_op jit(solution)/shard_map/all_to_all | solution.py:360
  8.6 8.1 %all-to-all-done.strips_ref = bf16[8,32,1024]{2,1,0:T(8,128)(2,1)S(1)} async-done(((bf16[8,32,1024]{2,1,0:T(8,128)(2,1)}), bf16[8,32,1024]{2,1,0:T(8,128)(2,1)S(1)}, u32[]{:S(2)}, u32[]{:S(2)}) %all-to-all-start) | async-done | bytes 524320 | tf_op jit(solution)/shard_map/all_to_all | solution.py:360
  18.6 2.6 %collective-permute-start = (bf16[32,3328]{1,0:T(8,128)(2,1)S(1)}, bf16[32,3328]{1,0:T(8,128)(2,1)S(1)}, u32[]{:S(2)}, u32[]{:S(2)}) collective-permute-start(bf16[32,3328]{1,0:T(8,128)(2,1)S(1)} %shard_map.51), channel_id=1, source_target_pairs={{0,16},{1,17},{2,18},{3,19},{4,20},{5,21},{6,22},{7,23},{8,24},{9,... | collective-permute-start | bytes 638984 | tf_op jit(solution)/shard_map/ppermute | solution.py:36
  21.9 5.6 %collective-permute-start.10 = (bf16[64,3328]{1,0:T(8,128)(2,1)S(1)}, bf16[64,3328]{1,0:T(8,128)(2,1)S(1)}, u32[]{:S(2)}, u32[]{:S(2)}) collective-permute-start(bf16[64,3328]{1,0:T(8,128)(2,1)S(1)} %pad_maximum_fusion.refs_0_), channel_id=1, source_target_pairs={{0,32},{1,33},{2,34},{3,35},{4,36},{5,37},{6,38},{7,39},{8,232},{9... | collective-permute-start | bytes 1277960 | tf_op jit(solution)/shard_map/ppermute | solution.py:36
  27.8 1.2 %collective-permute-done.1 = bf16[32,3328]{1,0:T(8,128)(2,1)S(1)} collective-permute-done((bf16[32,3328]{1,0:T(8,128)(2,1)S(1)}, bf16[32,3328]{1,0:T(8,128)(2,1)S(1)}, u32[]{:S(2)}, u32[]{:S(2)}) %collective-permute-start.1) | collective-permute-done | bytes 213024 | tf_op jit(solution)/shard_map/ppermute | solution.py:36
  29.0 5.5 %collective-permute-start.2 = (bf16[64,3328]{1,0:T(8,128)(2,1)S(1)}, bf16[64,3328]{1,0:T(8,128)(2,1)S(1)}, u32[]{:S(2)}, u32[]{:S(2)}) collective-permute-start(bf16[64,3328]{1,0:T(8,128)(2,1)S(1)} %constant_dynamic-update-slice_fusion.refs_1_), channel_id=1, source_target_pairs={{0,32},{1,33},{2,34},{3,35},{4,36},{5,37},{6,38},{7,39},{8,232},{9... | collective-permute-start | bytes 1277960 | tf_op jit(solution)/shard_map/ppermute | solution.py:36
  34.7 2.1 %collective-permute-start.11 = (bf16[64,3328]{1,0:T(8,128)(2,1)S(1)}, bf16[64,3328]{1,0:T(8,128)(2,1)S(1)}, u32[]{:S(2)}, u32[]{:S(2)}) collective-permute-start(bf16[64,3328]{1,0:T(8,128)(2,1)S(1)} %collective-permute-done.10.refs_2_), channel_id=1, source_target_pairs={{0,32},{1,33},{2,34},{3,35},{4,36},{5,37},{6,38},{7,39},{8,232},{9... | collective-permute-start | bytes 1277960 | tf_op jit(solution)/shard_map/ppermute | solution.py:36
  37.0 2.5 %collective-permute-done.2.refs_0_ = bf16[64,3328]{1,0:T(8,128)(2,1)S(1)} collective-permute-done((bf16[64,3328]{1,0:T(8,128)(2,1)S(1)}, bf16[64,3328]{1,0:T(8,128)(2,1)S(1)}, u32[]{:S(2)}, u32[]{:S(2)}) %collective-permute-start.2) | collective-permute-done | bytes 426016 | tf_op jit(solution)/shard_map/ppermute | solution.py:36
  39.6 1.7 %collective-permute-start.12 = (bf16[64,3328]{1,0:T(8,128)(2,1)S(1)}, bf16[64,3328]{1,0:T(8,128)(2,1)S(1)}, u32[]{:S(2)}, u32[]{:S(2)}) collective-permute-start(bf16[64,3328]{1,0:T(8,128)(2,1)S(1)} %collective-permute-done.10.refs_2_), channel_id=1, source_target_pairs={{0,8},{1,9},{2,10},{3,11},{4,12},{5,13},{6,14},{7,15},{8,0},{9,1},... | collective-permute-start | bytes 1277960 | tf_op jit(solution)/shard_map/ppermute | solution.py:36
  41.3 1.7 %collective-permute-start.3 = (bf16[64,3328]{1,0:T(8,128)(2,1)S(1)}, bf16[64,3328]{1,0:T(8,128)(2,1)S(1)}, u32[]{:S(2)}, u32[]{:S(2)}) collective-permute-start(bf16[64,3328]{1,0:T(8,128)(2,1)S(1)} %collective-permute-done.2.refs_0_), channel_id=1, source_target_pairs={{0,32},{1,33},{2,34},{3,35},{4,36},{5,37},{6,38},{7,39},{8,232},{9... | collective-permute-start | bytes 1277960 | tf_op jit(solution)/shard_map/ppermute | solution.py:36
  43.0 1.1 %collective-permute-done.11.refs_2_ = bf16[64,3328]{1,0:T(8,128)(2,1)S(1)} collective-permute-done((bf16[64,3328]{1,0:T(8,128)(2,1)S(1)}, bf16[64,3328]{1,0:T(8,128)(2,1)S(1)}, u32[]{:S(2)}, u32[]{:S(2)}) %collective-permute-start.11) | collective-permute-done | bytes 426016 | tf_op jit(solution)/shard_map/ppermute | solution.py:36
  44.1 1.7 %collective-permute-start.4 = (bf16[64,3328]{1,0:T(8,128)(2,1)S(1)}, bf16[64,3328]{1,0:T(8,128)(2,1)S(1)}, u32[]{:S(2)}, u32[]{:S(2)}) collective-permute-start(bf16[64,3328]{1,0:T(8,128)(2,1)S(1)} %collective-permute-done.2.refs_0_), channel_id=1, source_target_pairs={{0,8},{1,9},{2,10},{3,11},{4,12},{5,13},{6,14},{7,15},{8,0},{9,1},... | collective-permute-start | bytes 1277960 | tf_op jit(solution)/shard_map/ppermute | solution.py:36
  45.9 1.8 %collective-permute-start.13 = (bf16[64,3328]{1,0:T(8,128)(2,1)S(1)}, bf16[64,3328]{1,0:T(8,128)(2,1)S(1)}, u32[]{:S(2)}, u32[]{:S(2)}) collective-permute-start(bf16[64,3328]{1,0:T(8,128)(2,1)S(1)} %collective-permute-done.11.refs_2_), channel_id=1, source_target_pairs={{0,32},{1,33},{2,34},{3,35},{4,36},{5,37},{6,38},{7,39},{8,232},{9... | collective-permute-start | bytes 1277960 | tf_op jit(solution)/shard_map/ppermute | solution.py:36
  47.7 1.0 collective-permute-done.3.refs_4_
  48.7 1.9 %collective-permute-start.14 = (bf16[64,3328]{1,0:T(8,128)(2,1)S(1)}, bf16[64,3328]{1,0:T(8,128)(2,1)S(1)}, u32[]{:S(2)}, u32[]{:S(2)}) collective-permute-start(bf16[64,3328]{1,0:T(8,128)(2,1)S(1)} %collective-permute-done.11.refs_2_), channel_id=1, source_target_pairs={{0,8},{1,9},{2,10},{3,11},{4,12},{5,13},{6,14},{7,15},{8,0},{9,1},... | collective-permute-start | bytes 1277960 | tf_op jit(solution)/shard_map/ppermute | solution.py:36
  50.6 1.5 %collective-permute-start.8 = (bf16[64,3328]{1,0:T(8,128)(2,1)S(1)}, bf16[64,3328]{1,0:T(8,128)(2,1)S(1)}, u32[]{:S(2)}, u32[]{:S(2)}) collective-permute-start(bf16[64,3328]{1,0:T(8,128)(2,1)S(1)} %collective-permute-done.3.refs_4_), channel_id=1, source_target_pairs={{0,32},{1,33},{2,34},{3,35},{4,36},{5,37},{6,38},{7,39},{8,232},{9... | collective-permute-start | bytes 1277960 | tf_op jit(solution)/shard_map/ppermute | solution.py:36
  52.5 1.5 %shard_map.52._ = bf16[416,3328]{1,0:T(8,128)(2,1)S(1)} custom-call(s32[32,64]{1,0:T(8,128)S(1)} %shard_map.50.table_ref, bf16[64,3328]{1,0:T(8,128)(2,1)S(1)} %pad_maximum_fusion.refs_0_, bf16[64,3328]{1,0:T(8,128)(2,1)S(1)} %constant_dynamic-update-slice_fusion.refs_1_, bf16[64,3328]{1,0:T(8,128)(2,1)S(1)} %collective-permute-done.10.refs_2_, ...), custom_call_target="tpu_custom_call" | custom-call | tf_op jit(solution)/shard_map/pallas_call | solution.py:63
  54.2 1.1 collective-permute-start.16
  55.3 1.5 %collective-permute-start.21 = (bf16[32,3328]{1,0:T(8,128)(2,1)S(1)}, bf16[32,3328]{1,0:T(8,128)(2,1)S(1)}, u32[]{:S(2)}, u32[]{:S(2)}) collective-permute-start(bf16[32,3328]{1,0:T(8,128)(2,1)S(1)} %slice.16), channel_id=1, source_target_pairs={{0,32},{1,33},{2,34},{3,35},{4,36},{5,37},{6,38},{7,39},{8,232},{9... | collective-permute-start | bytes 638984 | tf_op jit(solution)/shard_map/ppermute | solution.py:36
  56.8 1.1 collective-permute-done.8.refs_0_
  57.9 3.1 %collective-permute-start.9 = (bf16[32,3328]{1,0:T(8,128)(2,1)S(1)}, bf16[32,3328]{1,0:T(8,128)(2,1)S(1)}, u32[]{:S(2)}, u32[]{:S(2)}) collective-permute-start(bf16[32,3328]{1,0:T(8,128)(2,1)S(1)} %slice.18), channel_id=1, source_target_pairs={{0,32},{1,33},{2,34},{3,35},{4,36},{5,37},{6,38},{7,39},{8,232},{9... | collective-permute-start | bytes 638984 | tf_op jit(solution)/shard_map/ppermute | solution.py:36
  61.1 1.8 %collective-permute-done.19.far_other_ref = bf16[64,3328]{1,0:T(8,128)(2,1)S(1)} collective-permute-done((bf16[64,3328]{1,0:T(8,128)(2,1)S(1)}, bf16[64,3328]{1,0:T(8,128)(2,1)S(1)}, u32[]{:S(2)}, u32[]{:S(2)}) %collective-permute-start.19) | collective-permute-done | bytes 426016 | tf_op jit(solution)/shard_map/ppermute | solution.py:36
  63.6 1.3 %shard_map.53._ = bf16[416,3328]{1,0:T(8,128)(2,1)S(1)} custom-call(s32[32,64]{1,0:T(8,128)S(1)} %shard_map.50.table_ref, bf16[416,3328]{1,0:T(8,128)(2,1)S(1)} %shard_map.52._, bf16[64,3328]{1,0:T(8,128)(2,1)S(1)} %collective-permute-done.2.refs_0_, bf16[64,3328]{1,0:T(8,128)(2,1)S(1)} %collective-permute-done.4.refs_1_, ...), custom_call_target="tpu_custom_call", output_to_operand_aliasing={{}: (1, {})} | custom-call | tf_op jit(solution)/shard_map/pallas_call | solution.py:63
  64.9 2.3 %collective-permute-start.23 = (bf16[32,3328]{1,0:T(8,128)(2,1)S(1)}, bf16[32,3328]{1,0:T(8,128)(2,1)S(1)}, u32[]{:S(2)}, u32[]{:S(2)}) collective-permute-start(bf16[32,3328]{1,0:T(8,128)(2,1)S(1)} %collective-permute-done.9.refs_4_), channel_id=1, source_target_pairs={{0,8},{1,9},{2,10},{3,11},{4,12},{5,13},{6,14},{7,15},{8,0},{9,1},... | collective-permute-start | bytes 638984 | tf_op jit(solution)/shard_map/ppermute | solution.py:36
  67.2 1.1 collective-permute-done.23.refs_5_
  68.3 2.2 %shard_map.55 = (s16[8,432,256]{2,1,0:T(8,128)(2,1)S(1)}, bf16[416,3328]{1,0:T(8,128)(2,1)S(1)}) custom-call(s32[32,64]{1,0:T(8,128)S(1)} %shard_map.50.table_ref, bf16[416,3328]{1,0:T(8,128)(2,1)S(1)} %shard_map.53._, bf16[256,3328]{1,0:T(8,128)(2,1)S(1)} %shard_map.54.band_ref, ...), custom_call_target="tpu_custom_call", output_to_operand_aliasing={{1}: (1, {})} | custom-call | tf_op jit(solution)/shard_map/pallas_call | solution.py:63
  70.5 24.7 %all_to_all.15.got_ref = s16[8,432,256]{2,1,0:T(8,128)(2,1)S(1)} all-to-all(s16[8,432,256]{2,1,0:T(8,128)(2,1)S(1)} %get-tuple-element.30), channel_id=1, replica_groups=mesh['row'=32,'col'=8] {'col'}, dimensions={0} | all-to-all | bytes 3538944 | tf_op jit(solution)/shard_map/all_to_all | solution.py:408
  95.3 2.7 %shard_map.57 = s16[8,144,256]{2,1,0:T(8,128)(2,1)} custom-call(s32[32,64]{1,0:T(8,128)S(1)} %shard_map.50.table_ref, bf16[416,3328]{1,0:T(8,128)(2,1)S(1)} %get-tuple-element.31.factor_ref, s16[8,432,256]{2,1,0:T(8,128)(2,1)S(1)} %all_to_all.15.got_ref), custom_call_target="tpu_custom_call" | custom-call | tf_op jit(solution)/shard_map/pallas_call | solution.py:63
  98.0 3.5 %all-to-all-start.2 = ((s16[8,144,256]{2,1,0:T(8,128)(2,1)}), s16[8,144,256]{2,1,0:T(8,128)(2,1)S(1)}, u32[]{:S(2)}, u32[]{:S(2)}) async-start(s16[8,144,256]{2,1,0:T(8,128)(2,1)} %shard_map.57), calls=%async_computation.2 | async-start | bytes 1179648 | tf_op jit(solution)/shard_map/all_to_all | solution.py:412
  101.5 2.1 %shard_map.56 = f32[256,1024]{1,0:T(8,128)} custom-call(s32[32,64]{1,0:T(8,128)S(1)} %shard_map.50.table_ref, s16[8,432,256]{2,1,0:T(8,128)(2,1)S(1)} %all_to_all.15.got_ref), custom_call_target="tpu_custom_call" | custom-call | tf_op jit(solution)/shard_map/pallas_call | solution.py:63
  103.6 7.9 %all-to-all-done.2.got_ref = s16[8,144,256]{2,1,0:T(8,128)(2,1)S(1)} async-done(((s16[8,144,256]{2,1,0:T(8,128)(2,1)}), s16[8,144,256]{2,1,0:T(8,128)(2,1)S(1)}, u32[]{:S(2)}, u32[]{:S(2)}) %all-to-all-start.2) | async-done | bytes 589856 | tf_op jit(solution)/shard_map/all_to_all | solution.py:412
  111.5 1.3 %shard_map.58 = f32[256,1024]{1,0:T(8,128)} custom-call(s16[8,144,256]{2,1,0:T(8,128)(2,1)S(1)} %all-to-all-done.2.got_ref), custom_call_target="tpu_custom_call" | custom-call | tf_op jit(solution)/shard_map/pallas_call | solution.py:63
  (42 shorter events, 6.7 us)
Async XLA Ops:
  0.6 16.1 %all-to-all-start = ((bf16[8,32,1024]{2,1,0:T(8,128)(2,1)}), bf16[8,32,1024]{2,1,0:T(8,128)(2,1)S(1)}, u32[]{:S(2)}, u32[]{:S(2)}) async-start(bf16[8,32,1024]{2,1,0:T(8,128)(2,1)} %bitcast.2), calls=%async_computation | async-start | bytes 1048576 | tf_op jit(solution)/shard_map/all_to_all | solution.py:360
  7.2 0.7 copy-start
  17.6 3.6 %collective-permute-start.5 = (bf16[32,3328]{1,0:T(8,128)(2,1)S(1)}, bf16[32,3328]{1,0:T(8,128)(2,1)S(1)}, u32[]{:S(2)}, u32[]{:S(2)}) collective-permute-start(bf16[32,3328]{1,0:T(8,128)(2,1)S(1)} %shard_map.51), channel_id=1, source_target_pairs={{0,8},{1,9},{2,10},{3,11},{4,12},{5,13},{6,14},{7,15},{8,0},{9,1},... | collective-permute-start | bytes 638984 | tf_op jit(solution)/shard_map/ppermute | solution.py:36
  18.6 9.0 %collective-permute-start = (bf16[32,3328]{1,0:T(8,128)(2,1)S(1)}, bf16[32,3328]{1,0:T(8,128)(2,1)S(1)}, u32[]{:S(2)}, u32[]{:S(2)}) collective-permute-start(bf16[32,3328]{1,0:T(8,128)(2,1)S(1)} %shard_map.51), channel_id=1, source_target_pairs={{0,16},{1,17},{2,18},{3,19},{4,20},{5,21},{6,22},{7,23},{8,24},{9,... | collective-permute-start | bytes 638984 | tf_op jit(solution)/shard_map/ppermute | solution.py:36
  21.2 13.3 %collective-permute-start.6 = (bf16[64,3328]{1,0:T(8,128)(2,1)S(1)}, bf16[64,3328]{1,0:T(8,128)(2,1)S(1)}, u32[]{:S(2)}, u32[]{:S(2)}) collective-permute-start(bf16[64,3328]{1,0:T(8,128)(2,1)S(1)} %pad_maximum_fusion.refs_0_), channel_id=1, source_target_pairs={{0,1},{1,2},{2,3},{3,0},{4,5},{5,6},{6,7},{7,4},{8,11},{9,8},{10,9... | collective-permute-start | bytes 1277960 | tf_op jit(solution)/shard_map/ppermute | solution.py:36
  21.9 12.7 %collective-permute-start.10 = (bf16[64,3328]{1,0:T(8,128)(2,1)S(1)}, bf16[64,3328]{1,0:T(8,128)(2,1)S(1)}, u32[]{:S(2)}, u32[]{:S(2)}) collective-permute-start(bf16[64,3328]{1,0:T(8,128)(2,1)S(1)} %pad_maximum_fusion.refs_0_), channel_id=1, source_target_pairs={{0,32},{1,33},{2,34},{3,35},{4,36},{5,37},{6,38},{7,39},{8,232},{9... | collective-permute-start | bytes 1277960 | tf_op jit(solution)/shard_map/ppermute | solution.py:36
  27.5 1.5 %collective-permute-start.1 = (bf16[32,3328]{1,0:T(8,128)(2,1)S(1)}, bf16[32,3328]{1,0:T(8,128)(2,1)S(1)}, u32[]{:S(2)}, u32[]{:S(2)}) collective-permute-start(bf16[32,3328]{1,0:T(8,128)(2,1)S(1)} %collective-permute-done), channel_id=1, source_target_pairs={{0,8},{1,9},{2,10},{3,11},{4,12},{5,13},{6,14},{7,15},{8,0},{9,1},... | collective-permute-start | bytes 638984 | tf_op jit(solution)/shard_map/ppermute | solution.py:36
  29.0 10.6 %collective-permute-start.2 = (bf16[64,3328]{1,0:T(8,128)(2,1)S(1)}, bf16[64,3328]{1,0:T(8,128)(2,1)S(1)}, u32[]{:S(2)}, u32[]{:S(2)}) collective-permute-start(bf16[64,3328]{1,0:T(8,128)(2,1)S(1)} %constant_dynamic-update-slice_fusion.refs_1_), channel_id=1, source_target_pairs={{0,32},{1,33},{2,34},{3,35},{4,36},{5,37},{6,38},{7,39},{8,232},{9... | collective-permute-start | bytes 1277960 | tf_op jit(solution)/shard_map/ppermute | solution.py:36
  34.5 6.7 %collective-permute-start.17 = (bf16[32,3328]{1,0:T(8,128)(2,1)S(1)}, bf16[32,3328]{1,0:T(8,128)(2,1)S(1)}, u32[]{:S(2)}, u32[]{:S(2)}) collective-permute-start(bf16[32,3328]{1,0:T(8,128)(2,1)S(1)} %get-tuple-element.32), channel_id=1, source_target_pairs={{0,8},{1,9},{2,10},{3,11},{4,12},{5,13},{6,14},{7,15},{8,0},{9,1},... | collective-permute-start | bytes 638984 | tf_op jit(solution)/shard_map/ppermute | solution.py:36
  34.7 9.5 %collective-permute-start.11 = (bf16[64,3328]{1,0:T(8,128)(2,1)S(1)}, bf16[64,3328]{1,0:T(8,128)(2,1)S(1)}, u32[]{:S(2)}, u32[]{:S(2)}) collective-permute-start(bf16[64,3328]{1,0:T(8,128)(2,1)S(1)} %collective-permute-done.10.refs_2_), channel_id=1, source_target_pairs={{0,32},{1,33},{2,34},{3,35},{4,36},{5,37},{6,38},{7,39},{8,232},{9... | collective-permute-start | bytes 1277960 | tf_op jit(solution)/shard_map/ppermute | solution.py:36
  36.7 15.4 %collective-permute-start.18 = (bf16[32,3328]{1,0:T(8,128)(2,1)S(1)}, bf16[32,3328]{1,0:T(8,128)(2,1)S(1)}, u32[]{:S(2)}, u32[]{:S(2)}) collective-permute-start(bf16[32,3328]{1,0:T(8,128)(2,1)S(1)} %get-tuple-element.33), channel_id=1, source_target_pairs={{0,1},{1,2},{2,3},{3,0},{4,5},{5,6},{6,7},{7,4},{8,11},{9,8},{10,9... | collective-permute-start | bytes 638984 | tf_op jit(solution)/shard_map/ppermute | solution.py:36
  36.8 13.8 %collective-permute-start.7 = (bf16[64,3328]{1,0:T(8,128)(2,1)S(1)}, bf16[64,3328]{1,0:T(8,128)(2,1)S(1)}, u32[]{:S(2)}, u32[]{:S(2)}) collective-permute-start(bf16[64,3328]{1,0:T(8,128)(2,1)S(1)} %pad_maximum_fusion.1.own_ref), channel_id=1, source_target_pairs={{0,4},{1,5},{2,6},{3,7},{4,0},{5,1},{6,2},{7,3},{8,12},{9,13},{10,... | collective-permute-start | bytes 1277960 | tf_op jit(solution)/shard_map/ppermute | solution.py:36
  39.6 6.3 %collective-permute-start.12 = (bf16[64,3328]{1,0:T(8,128)(2,1)S(1)}, bf16[64,3328]{1,0:T(8,128)(2,1)S(1)}, u32[]{:S(2)}, u32[]{:S(2)}) collective-permute-start(bf16[64,3328]{1,0:T(8,128)(2,1)S(1)} %collective-permute-done.10.refs_2_), channel_id=1, source_target_pairs={{0,8},{1,9},{2,10},{3,11},{4,12},{5,13},{6,14},{7,15},{8,0},{9,1},... | collective-permute-start | bytes 1277960 | tf_op jit(solution)/shard_map/ppermute | solution.py:36
  41.3 7.4 %collective-permute-start.3 = (bf16[64,3328]{1,0:T(8,128)(2,1)S(1)}, bf16[64,3328]{1,0:T(8,128)(2,1)S(1)}, u32[]{:S(2)}, u32[]{:S(2)}) collective-permute-start(bf16[64,3328]{1,0:T(8,128)(2,1)S(1)} %collective-permute-done.2.refs_0_), channel_id=1, source_target_pairs={{0,32},{1,33},{2,34},{3,35},{4,36},{5,37},{6,38},{7,39},{8,232},{9... | collective-permute-start | bytes 1277960 | tf_op jit(solution)/shard_map/ppermute | solution.py:36
  44.1 6.5 %collective-permute-start.4 = (bf16[64,3328]{1,0:T(8,128)(2,1)S(1)}, bf16[64,3328]{1,0:T(8,128)(2,1)S(1)}, u32[]{:S(2)}, u32[]{:S(2)}) collective-permute-start(bf16[64,3328]{1,0:T(8,128)(2,1)S(1)} %collective-permute-done.2.refs_0_), channel_id=1, source_target_pairs={{0,8},{1,9},{2,10},{3,11},{4,12},{5,13},{6,14},{7,15},{8,0},{9,1},... | collective-permute-start | bytes 1277960 | tf_op jit(solution)/shard_map/ppermute | solution.py:36
  45.9 8.3 %collective-permute-start.13 = (bf16[64,3328]{1,0:T(8,128)(2,1)S(1)}, bf16[64,3328]{1,0:T(8,128)(2,1)S(1)}, u32[]{:S(2)}, u32[]{:S(2)}) collective-permute-start(bf16[64,3328]{1,0:T(8,128)(2,1)S(1)} %collective-permute-done.11.refs_2_), channel_id=1, source_target_pairs={{0,32},{1,33},{2,34},{3,35},{4,36},{5,37},{6,38},{7,39},{8,232},{9... | collective-permute-start | bytes 1277960 | tf_op jit(solution)/shard_map/ppermute | solution.py:36
  48.7 5.5 %collective-permute-start.14 = (bf16[64,3328]{1,0:T(8,128)(2,1)S(1)}, bf16[64,3328]{1,0:T(8,128)(2,1)S(1)}, u32[]{:S(2)}, u32[]{:S(2)}) collective-permute-start(bf16[64,3328]{1,0:T(8,128)(2,1)S(1)} %collective-permute-done.11.refs_2_), channel_id=1, source_target_pairs={{0,8},{1,9},{2,10},{3,11},{4,12},{5,13},{6,14},{7,15},{8,0},{9,1},... | collective-permute-start | bytes 1277960 | tf_op jit(solution)/shard_map/ppermute | solution.py:36
  50.6 7.3 %collective-permute-start.8 = (bf16[64,3328]{1,0:T(8,128)(2,1)S(1)}, bf16[64,3328]{1,0:T(8,128)(2,1)S(1)}, u32[]{:S(2)}, u32[]{:S(2)}) collective-permute-start(bf16[64,3328]{1,0:T(8,128)(2,1)S(1)} %collective-permute-done.3.refs_4_), channel_id=1, source_target_pairs={{0,32},{1,33},{2,34},{3,35},{4,36},{5,37},{6,38},{7,39},{8,232},{9... | collective-permute-start | bytes 1277960 | tf_op jit(solution)/shard_map/ppermute | solution.py:36
  52.2 10.7 %collective-permute-start.19 = (bf16[64,3328]{1,0:T(8,128)(2,1)S(1)}, bf16[64,3328]{1,0:T(8,128)(2,1)S(1)}, u32[]{:S(2)}, u32[]{:S(2)}) collective-permute-start(bf16[64,3328]{1,0:T(8,128)(2,1)S(1)} %constant_dynamic-update-slice_fusion.2.far_own_ref), channel_id=1, source_target_pairs={{0,4},{1,5},{2,6},{3,7},{4,0},{5,1},{6,2},{7,3},{8,12},{9,13},{10,... | collective-permute-start | bytes 1277960 | tf_op jit(solution)/shard_map/ppermute | solution.py:36
  54.1 9.5 %collective-permute-start.15 = (bf16[64,3328]{1,0:T(8,128)(2,1)S(1)}, bf16[64,3328]{1,0:T(8,128)(2,1)S(1)}, u32[]{:S(2)}, u32[]{:S(2)}) collective-permute-start(bf16[64,3328]{1,0:T(8,128)(2,1)S(1)} %collective-permute-done.3.refs_4_), channel_id=1, source_target_pairs={{0,8},{1,9},{2,10},{3,11},{4,12},{5,13},{6,14},{7,15},{8,0},{9,1},... | collective-permute-start | bytes 1277960 | tf_op jit(solution)/shard_map/ppermute | solution.py:36
  54.2 9.4 %collective-permute-start.16 = (bf16[64,3328]{1,0:T(8,128)(2,1)S(1)}, bf16[64,3328]{1,0:T(8,128)(2,1)S(1)}, u32[]{:S(2)}, u32[]{:S(2)}) collective-permute-start(bf16[64,3328]{1,0:T(8,128)(2,1)S(1)} %collective-permute-done.13.refs_6_), channel_id=1, source_target_pairs={{0,8},{1,9},{2,10},{3,11},{4,12},{5,13},{6,14},{7,15},{8,0},{9,1},... | collective-permute-start | bytes 1277960 | tf_op jit(solution)/shard_map/ppermute | solution.py:36
  55.3 7.7 %collective-permute-start.21 = (bf16[32,3328]{1,0:T(8,128)(2,1)S(1)}, bf16[32,3328]{1,0:T(8,128)(2,1)S(1)}, u32[]{:S(2)}, u32[]{:S(2)}) collective-permute-start(bf16[32,3328]{1,0:T(8,128)(2,1)S(1)} %slice.16), channel_id=1, source_target_pairs={{0,32},{1,33},{2,34},{3,35},{4,36},{5,37},{6,38},{7,39},{8,232},{9... | collective-permute-start | bytes 638984 | tf_op jit(solution)/shard_map/ppermute | solution.py:36
  57.9 7.0 %collective-permute-start.9 = (bf16[32,3328]{1,0:T(8,128)(2,1)S(1)}, bf16[32,3328]{1,0:T(8,128)(2,1)S(1)}, u32[]{:S(2)}, u32[]{:S(2)}) collective-permute-start(bf16[32,3328]{1,0:T(8,128)(2,1)S(1)} %slice.18), channel_id=1, source_target_pairs={{0,32},{1,33},{2,34},{3,35},{4,36},{5,37},{6,38},{7,39},{8,232},{9... | collective-permute-start | bytes 638984 | tf_op jit(solution)/shard_map/ppermute | solution.py:36
  62.8 5.4 %collective-permute-start.20 = (bf16[64,3328]{1,0:T(8,128)(2,1)S(1)}, bf16[64,3328]{1,0:T(8,128)(2,1)S(1)}, u32[]{:S(2)}, u32[]{:S(2)}) collective-permute-start(bf16[64,3328]{1,0:T(8,128)(2,1)S(1)} %collective-permute-done.8.refs_0_), channel_id=1, source_target_pairs={{0,8},{1,9},{2,10},{3,11},{4,12},{5,13},{6,14},{7,15},{8,0},{9,1},... | collective-permute-start | bytes 1277960 | tf_op jit(solution)/shard_map/ppermute | solution.py:36
  63.0 4.2 %collective-permute-start.22 = (bf16[32,3328]{1,0:T(8,128)(2,1)S(1)}, bf16[32,3328]{1,0:T(8,128)(2,1)S(1)}, u32[]{:S(2)}, u32[]{:S(2)}) collective-permute-start(bf16[32,3328]{1,0:T(8,128)(2,1)S(1)} %collective-permute-done.21.refs_2_), channel_id=1, source_target_pairs={{0,8},{1,9},{2,10},{3,11},{4,12},{5,13},{6,14},{7,15},{8,0},{9,1},... | collective-permute-start | bytes 638984 | tf_op jit(solution)/shard_map/ppermute | solution.py:36
  64.9 3.4 %collective-permute-start.23 = (bf16[32,3328]{1,0:T(8,128)(2,1)S(1)}, bf16[32,3328]{1,0:T(8,128)(2,1)S(1)}, u32[]{:S(2)}, u32[]{:S(2)}) collective-permute-start(bf16[32,3328]{1,0:T(8,128)(2,1)S(1)} %collective-permute-done.9.refs_4_), channel_id=1, source_target_pairs={{0,8},{1,9},{2,10},{3,11},{4,12},{5,13},{6,14},{7,15},{8,0},{9,1},... | collective-permute-start | bytes 638984 | tf_op jit(solution)/shard_map/ppermute | solution.py:36
  98.0 13.6 %all-to-all-start.2 = ((s16[8,144,256]{2,1,0:T(8,128)(2,1)}), s16[8,144,256]{2,1,0:T(8,128)(2,1)S(1)}, u32[]{:S(2)}, u32[]{:S(2)}) async-start(s16[8,144,256]{2,1,0:T(8,128)(2,1)} %shard_map.57), calls=%async_computation.2 | async-start | bytes 1179648 | tf_op jit(solution)/shard_map/all_to_all | solution.py:412

commit v7 on v6

--- a/solution.py
+++ b/solution.py
@@ -335,16 +335,30 @@
 
 
 def cube_home_kernel(got_ref, cubed_ref, held):
+    spot = pl.program_id(0)
     cols = got_ref.shape[0]
     depth = TILE // cols
-    sizes = [steps_of(got_ref, strip) for strip in range(cols)]
-    for spot in range(cubed_ref.shape[1] // TILE):
-        for strip in range(cols):
-            steps = got_ref[strip, spot * depth : (spot + 1) * depth, :]
-            held[strip * depth : (strip + 1) * depth, :] = decode(
-                steps, sizes[strip][spot : spot + 1]
-            )
-        cubed_ref[:, spot * TILE : (spot + 1) * TILE] = held[...].T
+    start = pl.multiple_of(spot * depth, depth)
+    for strip in range(cols):
+        sizes = steps_of(got_ref, strip)
+        index = lax.broadcasted_iota(jnp.int32, sizes.shape, 0)
+        size = jnp.sum(jnp.where(index == spot, sizes, 0.0), axis=0, keepdims=True)
+        held[strip * depth : (strip + 1) * depth, :] = decode(
+            got_ref[strip, pl.ds(start, depth), :], size
+        )
+    cubed_ref[...] = held[...].T
+
+
+def cube_home(got, shape):
+    return pl.pallas_call(
+        cube_home_kernel,
+        grid=(shape[1] // TILE,),
+        out_shape=jax.ShapeDtypeStruct(shape, jnp.float32),
+        in_specs=[pl.BlockSpec(got.shape, lambda spot: (0, 0, 0))],
+        out_specs=pl.BlockSpec((shape[0], TILE), lambda spot: (0, spot)),
+        scratch_shapes=[pltpu.VMEM((TILE, TILE), jnp.float32)],
+        compiler_params=pltpu.CompilerParams(vmem_limit_bytes=16 * MIB),
+    )(got)
 
 
 def home(kernel, operands, tables, shape):
@@ -409,7 +423,7 @@
     scale = (rows * lax.axis_size("row") / 2.0) ** (-0.25)
     coded = cube_strips(table, factor, got, scale)
     square = home(square_home_kernel, (table, got), 1, (rows, columns))
-    cubed = home(cube_home_kernel, (lax.all_to_all(coded, "col", 0, 0),), 0, (rows, columns))
+    cubed = cube_home(lax.all_to_all(coded, "col", 0, 0), (rows, columns))
     return square, cubed
 
 

time: 115 us -> 115 us (level); the launches traced: 113 us -> 115 us
  Pallas kernels: 13 us -> 14.2 us
    pallas_call x0 -> x1, Pallas kernels: none -> 1.87 us  [cube_home(): pl.pallas_call(cube_home_kernel, grid=(shape[1] // TILE,), out_shape=jax....]
    pallas_call x9 -> x8, Pallas kernels: 13 us -> 12.3 us  [call(): pl.pallas_call(kernel, out_shape=out_shape, in_specs=[SMEM] * tables + [V...]
  transfers between devices with their start and end apart: 26 -> 26, of which waited for: 9 -> 9; matrix products, arithmetic and copies ran while one was open for 1% -> 1% of each run, Pallas kernels for 5% -> 6%
where the time goes in v7:
time: 115 us
  starting transfers between devices  46.7 us (41%)
  waiting for transfers between devices  26.2 us (23%)
  blocking collectives  25.8 us (22%)
  Pallas kernels  14.2 us (12%)
  local copies, waits for them, and re-layouts  1.57 us (1%)
    ppermute x24, starting transfers between devices, move(): return lax.ppermute(block, BOTH, pairs(place))  37.2 us
    all_to_all x1, blocking collectives, local(): got = lax.all_to_all(spread, 'col', 0, 0)  25.8 us
    pallas_call x8, Pallas kernels, call(): pl.pallas_call(kernel, out_shape=out_shape, in_specs=[SMEM] * tables + [V...  12.3 us
    ppermute x24, waiting for transfers between devices, move(): return lax.ppermute(block, BOTH, pairs(place))  9.41 us
    all_to_all x1, waiting for transfers between devices, local(): cubed = cube_home(lax.all_to_all(coded, 'col', 0, 0), (rows, columns))  8.69 us
    all_to_all x1, waiting for transfers between devices, local(): strips = lax.all_to_all(density.reshape(COL, depth, columns), 'col', 0, 0)  8.06 us
    all_to_all x1, starting transfers between devices, local(): strips = lax.all_to_all(density.reshape(COL, depth, columns), 'col', 0, 0)  5.87 us
    all_to_all x1, starting transfers between devices, local(): cubed = cube_home(lax.all_to_all(coded, 'col', 0, 0), (rows, columns))  3.54 us
  transfers between devices with their start and end apart: 26, of which 9 were waited for; matrix products, arithmetic and copies ran while one was open for 1% of the time, Pallas kernels for 6%

profile of v7, /device:TPU:1, one launch (start us, length us, event | category | flops | bytes accessed | tf_op | source)
XLA Modules:
  0.0 115.2 jit_solution(8285236549992887110)
XLA Ops:
  0.6 5.9 %all-to-all-start = ((bf16[8,32,1024]{2,1,0:T(8,128)(2,1)}), bf16[8,32,1024]{2,1,0:T(8,128)(2,1)S(1)}, u32[]{:S(2)}, u32[]{:S(2)}) async-start(bf16[8,32,1024]{2,1,0:T(8,128)(2,1)} %bitcast.2), calls=%async_computation | async-start | bytes 1048576 | tf_op jit(solution)/shard_map/all_to_all | solution.py:374
  8.6 8.1 %all-to-all-done.strips_ref = bf16[8,32,1024]{2,1,0:T(8,128)(2,1)S(1)} async-done(((bf16[8,32,1024]{2,1,0:T(8,128)(2,1)}), bf16[8,32,1024]{2,1,0:T(8,128)(2,1)S(1)}, u32[]{:S(2)}, u32[]{:S(2)}) %all-to-all-start) | async-done | bytes 524320 | tf_op jit(solution)/shard_map/all_to_all | solution.py:374
  16.7 0.9 shard_map.51
  17.6 0.9 collective-permute-start.5
  18.6 2.6 %collective-permute-start = (bf16[32,3328]{1,0:T(8,128)(2,1)S(1)}, bf16[32,3328]{1,0:T(8,128)(2,1)S(1)}, u32[]{:S(2)}, u32[]{:S(2)}) collective-permute-start(bf16[32,3328]{1,0:T(8,128)(2,1)S(1)} %shard_map.51), channel_id=1, source_target_pairs={{0,16},{1,17},{2,18},{3,19},{4,20},{5,21},{6,22},{7,23},{8,24},{9,... | collective-permute-start | bytes 638984 | tf_op jit(solution)/shard_map/ppermute | solution.py:36
  21.9 5.6 %collective-permute-start.10 = (bf16[64,3328]{1,0:T(8,128)(2,1)S(1)}, bf16[64,3328]{1,0:T(8,128)(2,1)S(1)}, u32[]{:S(2)}, u32[]{:S(2)}) collective-permute-start(bf16[64,3328]{1,0:T(8,128)(2,1)S(1)} %pad_maximum_fusion.refs_0_), channel_id=1, source_target_pairs={{0,32},{1,33},{2,34},{3,35},{4,36},{5,37},{6,38},{7,39},{8,232},{9... | collective-permute-start | bytes 1277960 | tf_op jit(solution)/shard_map/ppermute | solution.py:36
  27.8 1.2 %collective-permute-done.1 = bf16[32,3328]{1,0:T(8,128)(2,1)S(1)} collective-permute-done((bf16[32,3328]{1,0:T(8,128)(2,1)S(1)}, bf16[32,3328]{1,0:T(8,128)(2,1)S(1)}, u32[]{:S(2)}, u32[]{:S(2)}) %collective-permute-start.1) | collective-permute-done | bytes 213024 | tf_op jit(solution)/shard_map/ppermute | solution.py:36
  29.0 5.5 %collective-permute-start.2 = (bf16[64,3328]{1,0:T(8,128)(2,1)S(1)}, bf16[64,3328]{1,0:T(8,128)(2,1)S(1)}, u32[]{:S(2)}, u32[]{:S(2)}) collective-permute-start(bf16[64,3328]{1,0:T(8,128)(2,1)S(1)} %constant_dynamic-update-slice_fusion.refs_1_), channel_id=1, source_target_pairs={{0,32},{1,33},{2,34},{3,35},{4,36},{5,37},{6,38},{7,39},{8,232},{9... | collective-permute-start | bytes 1277960 | tf_op jit(solution)/shard_map/ppermute | solution.py:36
  34.7 2.1 %collective-permute-start.11 = (bf16[64,3328]{1,0:T(8,128)(2,1)S(1)}, bf16[64,3328]{1,0:T(8,128)(2,1)S(1)}, u32[]{:S(2)}, u32[]{:S(2)}) collective-permute-start(bf16[64,3328]{1,0:T(8,128)(2,1)S(1)} %collective-permute-done.10.refs_2_), channel_id=1, source_target_pairs={{0,32},{1,33},{2,34},{3,35},{4,36},{5,37},{6,38},{7,39},{8,232},{9... | collective-permute-start | bytes 1277960 | tf_op jit(solution)/shard_map/ppermute | solution.py:36
  37.0 2.5 %collective-permute-done.2.refs_0_ = bf16[64,3328]{1,0:T(8,128)(2,1)S(1)} collective-permute-done((bf16[64,3328]{1,0:T(8,128)(2,1)S(1)}, bf16[64,3328]{1,0:T(8,128)(2,1)S(1)}, u32[]{:S(2)}, u32[]{:S(2)}) %collective-permute-start.2) | collective-permute-done | bytes 426016 | tf_op jit(solution)/shard_map/ppermute | solution.py:36
  39.6 1.7 %collective-permute-start.12 = (bf16[64,3328]{1,0:T(8,128)(2,1)S(1)}, bf16[64,3328]{1,0:T(8,128)(2,1)S(1)}, u32[]{:S(2)}, u32[]{:S(2)}) collective-permute-start(bf16[64,3328]{1,0:T(8,128)(2,1)S(1)} %collective-permute-done.10.refs_2_), channel_id=1, source_target_pairs={{0,8},{1,9},{2,10},{3,11},{4,12},{5,13},{6,14},{7,15},{8,0},{9,1},... | collective-permute-start | bytes 1277960 | tf_op jit(solution)/shard_map/ppermute | solution.py:36
  41.3 1.7 %collective-permute-start.3 = (bf16[64,3328]{1,0:T(8,128)(2,1)S(1)}, bf16[64,3328]{1,0:T(8,128)(2,1)S(1)}, u32[]{:S(2)}, u32[]{:S(2)}) collective-permute-start(bf16[64,3328]{1,0:T(8,128)(2,1)S(1)} %collective-permute-done.2.refs_0_), channel_id=1, source_target_pairs={{0,32},{1,33},{2,34},{3,35},{4,36},{5,37},{6,38},{7,39},{8,232},{9... | collective-permute-start | bytes 1277960 | tf_op jit(solution)/shard_map/ppermute | solution.py:36
  43.0 1.1 collective-permute-done.11.refs_2_
  44.1 1.7 %collective-permute-start.4 = (bf16[64,3328]{1,0:T(8,128)(2,1)S(1)}, bf16[64,3328]{1,0:T(8,128)(2,1)S(1)}, u32[]{:S(2)}, u32[]{:S(2)}) collective-permute-start(bf16[64,3328]{1,0:T(8,128)(2,1)S(1)} %collective-permute-done.2.refs_0_), channel_id=1, source_target_pairs={{0,8},{1,9},{2,10},{3,11},{4,12},{5,13},{6,14},{7,15},{8,0},{9,1},... | collective-permute-start | bytes 1277960 | tf_op jit(solution)/shard_map/ppermute | solution.py:36
  45.9 1.8 %collective-permute-start.13 = (bf16[64,3328]{1,0:T(8,128)(2,1)S(1)}, bf16[64,3328]{1,0:T(8,128)(2,1)S(1)}, u32[]{:S(2)}, u32[]{:S(2)}) collective-permute-start(bf16[64,3328]{1,0:T(8,128)(2,1)S(1)} %collective-permute-done.11.refs_2_), channel_id=1, source_target_pairs={{0,32},{1,33},{2,34},{3,35},{4,36},{5,37},{6,38},{7,39},{8,232},{9... | collective-permute-start | bytes 1277960 | tf_op jit(solution)/shard_map/ppermute | solution.py:36
  47.7 1.0 collective-permute-done.3.refs_4_
  48.7 1.9 %collective-permute-start.14 = (bf16[64,3328]{1,0:T(8,128)(2,1)S(1)}, bf16[64,3328]{1,0:T(8,128)(2,1)S(1)}, u32[]{:S(2)}, u32[]{:S(2)}) collective-permute-start(bf16[64,3328]{1,0:T(8,128)(2,1)S(1)} %collective-permute-done.11.refs_2_), channel_id=1, source_target_pairs={{0,8},{1,9},{2,10},{3,11},{4,12},{5,13},{6,14},{7,15},{8,0},{9,1},... | collective-permute-start | bytes 1277960 | tf_op jit(solution)/shard_map/ppermute | solution.py:36
  50.6 1.5 %collective-permute-start.8 = (bf16[64,3328]{1,0:T(8,128)(2,1)S(1)}, bf16[64,3328]{1,0:T(8,128)(2,1)S(1)}, u32[]{:S(2)}, u32[]{:S(2)}) collective-permute-start(bf16[64,3328]{1,0:T(8,128)(2,1)S(1)} %collective-permute-done.3.refs_4_), channel_id=1, source_target_pairs={{0,32},{1,33},{2,34},{3,35},{4,36},{5,37},{6,38},{7,39},{8,232},{9... | collective-permute-start | bytes 1277960 | tf_op jit(solution)/shard_map/ppermute | solution.py:36
  52.5 2.1 %shard_map.52._ = bf16[416,3328]{1,0:T(8,128)(2,1)S(1)} custom-call(s32[32,64]{1,0:T(8,128)S(1)} %shard_map.50.table_ref, bf16[64,3328]{1,0:T(8,128)(2,1)S(1)} %pad_maximum_fusion.refs_0_, bf16[64,3328]{1,0:T(8,128)(2,1)S(1)} %constant_dynamic-update-slice_fusion.refs_1_, bf16[64,3328]{1,0:T(8,128)(2,1)S(1)} %collective-permute-done.10.refs_2_, ...), custom_call_target="tpu_custom_call" | custom-call | tf_op jit(solution)/shard_map/pallas_call | solution.py:63
  55.3 2.0 %collective-permute-start.21 = (bf16[32,3328]{1,0:T(8,128)(2,1)S(1)}, bf16[32,3328]{1,0:T(8,128)(2,1)S(1)}, u32[]{:S(2)}, u32[]{:S(2)}) collective-permute-start(bf16[32,3328]{1,0:T(8,128)(2,1)S(1)} %slice.16), channel_id=1, source_target_pairs={{0,32},{1,33},{2,34},{3,35},{4,36},{5,37},{6,38},{7,39},{8,232},{9... | collective-permute-start | bytes 638984 | tf_op jit(solution)/shard_map/ppermute | solution.py:36
  57.9 3.1 %collective-permute-start.9 = (bf16[32,3328]{1,0:T(8,128)(2,1)S(1)}, bf16[32,3328]{1,0:T(8,128)(2,1)S(1)}, u32[]{:S(2)}, u32[]{:S(2)}) collective-permute-start(bf16[32,3328]{1,0:T(8,128)(2,1)S(1)} %slice.18), channel_id=1, source_target_pairs={{0,32},{1,33},{2,34},{3,35},{4,36},{5,37},{6,38},{7,39},{8,232},{9... | collective-permute-start | bytes 638984 | tf_op jit(solution)/shard_map/ppermute | solution.py:36
  61.1 1.8 %collective-permute-done.19.far_other_ref = bf16[64,3328]{1,0:T(8,128)(2,1)S(1)} collective-permute-done((bf16[64,3328]{1,0:T(8,128)(2,1)S(1)}, bf16[64,3328]{1,0:T(8,128)(2,1)S(1)}, u32[]{:S(2)}, u32[]{:S(2)}) %collective-permute-start.19) | collective-permute-done | bytes 426016 | tf_op jit(solution)/shard_map/ppermute | solution.py:36
  63.6 1.4 %shard_map.53._ = bf16[416,3328]{1,0:T(8,128)(2,1)S(1)} custom-call(s32[32,64]{1,0:T(8,128)S(1)} %shard_map.50.table_ref, bf16[416,3328]{1,0:T(8,128)(2,1)S(1)} %shard_map.52._, bf16[64,3328]{1,0:T(8,128)(2,1)S(1)} %collective-permute-done.2.refs_0_, bf16[64,3328]{1,0:T(8,128)(2,1)S(1)} %collective-permute-done.4.refs_1_, ...), custom_call_target="tpu_custom_call", output_to_operand_aliasing={{}: (1, {})} | custom-call | tf_op jit(solution)/shard_map/pallas_call | solution.py:63
  65.0 2.2 %collective-permute-start.23 = (bf16[32,3328]{1,0:T(8,128)(2,1)S(1)}, bf16[32,3328]{1,0:T(8,128)(2,1)S(1)}, u32[]{:S(2)}, u32[]{:S(2)}) collective-permute-start(bf16[32,3328]{1,0:T(8,128)(2,1)S(1)} %collective-permute-done.9.refs_4_), channel_id=1, source_target_pairs={{0,8},{1,9},{2,10},{3,11},{4,12},{5,13},{6,14},{7,15},{8,0},{9,1},... | collective-permute-start | bytes 638984 | tf_op jit(solution)/shard_map/ppermute | solution.py:36
  67.2 1.1 collective-permute-done.23.refs_5_
  68.3 2.2 %shard_map.55 = (s16[8,432,256]{2,1,0:T(8,128)(2,1)S(1)}, bf16[416,3328]{1,0:T(8,128)(2,1)S(1)}) custom-call(s32[32,64]{1,0:T(8,128)S(1)} %shard_map.50.table_ref, bf16[416,3328]{1,0:T(8,128)(2,1)S(1)} %shard_map.53._, bf16[256,3328]{1,0:T(8,128)(2,1)S(1)} %shard_map.54.band_ref, ...), custom_call_target="tpu_custom_call", output_to_operand_aliasing={{1}: (1, {})} | custom-call | tf_op jit(solution)/shard_map/pallas_call | solution.py:63
  70.5 25.8 %all_to_all.15.got_ref = s16[8,432,256]{2,1,0:T(8,128)(2,1)S(1)} all-to-all(s16[8,432,256]{2,1,0:T(8,128)(2,1)S(1)} %get-tuple-element.30), channel_id=1, replica_groups=mesh['row'=32,'col'=8] {'col'}, dimensions={0} | all-to-all | bytes 3538944 | tf_op jit(solution)/shard_map/all_to_all | solution.py:422
  96.2 2.7 %shard_map.57 = s16[8,144,256]{2,1,0:T(8,128)(2,1)} custom-call(s32[32,64]{1,0:T(8,128)S(1)} %shard_map.50.table_ref, bf16[416,3328]{1,0:T(8,128)(2,1)S(1)} %get-tuple-element.31.factor_ref, s16[8,432,256]{2,1,0:T(8,128)(2,1)S(1)} %all_to_all.15.got_ref), custom_call_target="tpu_custom_call" | custom-call | tf_op jit(solution)/shard_map/pallas_call | solution.py:63
  98.9 3.5 %all-to-all-start.2 = ((s16[8,144,256]{2,1,0:T(8,128)(2,1)}), s16[8,144,256]{2,1,0:T(8,128)(2,1)S(1)}, u32[]{:S(2)}, u32[]{:S(2)}) async-start(s16[8,144,256]{2,1,0:T(8,128)(2,1)} %shard_map.57), calls=%async_computation.2 | async-start | bytes 1179648 | tf_op jit(solution)/shard_map/all_to_all | solution.py:426
  102.5 2.1 %shard_map.56 = f32[256,1024]{1,0:T(8,128)} custom-call(s32[32,64]{1,0:T(8,128)S(1)} %shard_map.50.table_ref, s16[8,432,256]{2,1,0:T(8,128)(2,1)S(1)} %all_to_all.15.got_ref), custom_call_target="tpu_custom_call" | custom-call | tf_op jit(solution)/shard_map/pallas_call | solution.py:63
  104.6 8.7 %all-to-all-done.2.got_ref = s16[8,144,256]{2,1,0:T(8,128)(2,1)S(1)} async-done(((s16[8,144,256]{2,1,0:T(8,128)(2,1)}), s16[8,144,256]{2,1,0:T(8,128)(2,1)S(1)}, u32[]{:S(2)}, u32[]{:S(2)}) %all-to-all-start.2) | async-done | bytes 589856 | tf_op jit(solution)/shard_map/all_to_all | solution.py:426
  113.3 1.9 %shard_map.58 = f32[256,1024]{1,0:T(8,128)} custom-call(s16[8,144,256]{2,1,0:T(8,128)(2,1)S(1)} %all-to-all-done.2.got_ref), custom_call_target="tpu_custom_call" | custom-call | tf_op jit(solution)/shard_map/pallas_call | solution.py:353
  (42 shorter events, 5.9 us)
Async XLA Ops:
  0.6 16.1 %all-to-all-start = ((bf16[8,32,1024]{2,1,0:T(8,128)(2,1)}), bf16[8,32,1024]{2,1,0:T(8,128)(2,1)S(1)}, u32[]{:S(2)}, u32[]{:S(2)}) async-start(bf16[8,32,1024]{2,1,0:T(8,128)(2,1)} %bitcast.2), calls=%async_computation | async-start | bytes 1048576 | tf_op jit(solution)/shard_map/all_to_all | solution.py:374
  7.2 0.7 copy-start
  17.6 3.6 %collective-permute-start.5 = (bf16[32,3328]{1,0:T(8,128)(2,1)S(1)}, bf16[32,3328]{1,0:T(8,128)(2,1)S(1)}, u32[]{:S(2)}, u32[]{:S(2)}) collective-permute-start(bf16[32,3328]{1,0:T(8,128)(2,1)S(1)} %shard_map.51), channel_id=1, source_target_pairs={{0,8},{1,9},{2,10},{3,11},{4,12},{5,13},{6,14},{7,15},{8,0},{9,1},... | collective-permute-start | bytes 638984 | tf_op jit(solution)/shard_map/ppermute | solution.py:36
  18.6 9.0 %collective-permute-start = (bf16[32,3328]{1,0:T(8,128)(2,1)S(1)}, bf16[32,3328]{1,0:T(8,128)(2,1)S(1)}, u32[]{:S(2)}, u32[]{:S(2)}) collective-permute-start(bf16[32,3328]{1,0:T(8,128)(2,1)S(1)} %shard_map.51), channel_id=1, source_target_pairs={{0,16},{1,17},{2,18},{3,19},{4,20},{5,21},{6,22},{7,23},{8,24},{9,... | collective-permute-start | bytes 638984 | tf_op jit(solution)/shard_map/ppermute | solution.py:36
  21.2 13.3 %collective-permute-start.6 = (bf16[64,3328]{1,0:T(8,128)(2,1)S(1)}, bf16[64,3328]{1,0:T(8,128)(2,1)S(1)}, u32[]{:S(2)}, u32[]{:S(2)}) collective-permute-start(bf16[64,3328]{1,0:T(8,128)(2,1)S(1)} %pad_maximum_fusion.refs_0_), channel_id=1, source_target_pairs={{0,1},{1,2},{2,3},{3,0},{4,5},{5,6},{6,7},{7,4},{8,11},{9,8},{10,9... | collective-permute-start | bytes 1277960 | tf_op jit(solution)/shard_map/ppermute | solution.py:36
  21.9 12.7 %collective-permute-start.10 = (bf16[64,3328]{1,0:T(8,128)(2,1)S(1)}, bf16[64,3328]{1,0:T(8,128)(2,1)S(1)}, u32[]{:S(2)}, u32[]{:S(2)}) collective-permute-start(bf16[64,3328]{1,0:T(8,128)(2,1)S(1)} %pad_maximum_fusion.refs_0_), channel_id=1, source_target_pairs={{0,32},{1,33},{2,34},{3,35},{4,36},{5,37},{6,38},{7,39},{8,232},{9... | collective-permute-start | bytes 1277960 | tf_op jit(solution)/shard_map/ppermute | solution.py:36
  27.5 1.5 %collective-permute-start.1 = (bf16[32,3328]{1,0:T(8,128)(2,1)S(1)}, bf16[32,3328]{1,0:T(8,128)(2,1)S(1)}, u32[]{:S(2)}, u32[]{:S(2)}) collective-permute-start(bf16[32,3328]{1,0:T(8,128)(2,1)S(1)} %collective-permute-done), channel_id=1, source_target_pairs={{0,8},{1,9},{2,10},{3,11},{4,12},{5,13},{6,14},{7,15},{8,0},{9,1},... | collective-permute-start | bytes 638984 | tf_op jit(solution)/shard_map/ppermute | solution.py:36
  29.0 10.6 %collective-permute-start.2 = (bf16[64,3328]{1,0:T(8,128)(2,1)S(1)}, bf16[64,3328]{1,0:T(8,128)(2,1)S(1)}, u32[]{:S(2)}, u32[]{:S(2)}) collective-permute-start(bf16[64,3328]{1,0:T(8,128)(2,1)S(1)} %constant_dynamic-update-slice_fusion.refs_1_), channel_id=1, source_target_pairs={{0,32},{1,33},{2,34},{3,35},{4,36},{5,37},{6,38},{7,39},{8,232},{9... | collective-permute-start | bytes 1277960 | tf_op jit(solution)/shard_map/ppermute | solution.py:36
  34.5 6.7 %collective-permute-start.17 = (bf16[32,3328]{1,0:T(8,128)(2,1)S(1)}, bf16[32,3328]{1,0:T(8,128)(2,1)S(1)}, u32[]{:S(2)}, u32[]{:S(2)}) collective-permute-start(bf16[32,3328]{1,0:T(8,128)(2,1)S(1)} %get-tuple-element.32), channel_id=1, source_target_pairs={{0,8},{1,9},{2,10},{3,11},{4,12},{5,13},{6,14},{7,15},{8,0},{9,1},... | collective-permute-start | bytes 638984 | tf_op jit(solution)/shard_map/ppermute | solution.py:36
  34.7 9.5 %collective-permute-start.11 = (bf16[64,3328]{1,0:T(8,128)(2,1)S(1)}, bf16[64,3328]{1,0:T(8,128)(2,1)S(1)}, u32[]{:S(2)}, u32[]{:S(2)}) collective-permute-start(bf16[64,3328]{1,0:T(8,128)(2,1)S(1)} %collective-permute-done.10.refs_2_), channel_id=1, source_target_pairs={{0,32},{1,33},{2,34},{3,35},{4,36},{5,37},{6,38},{7,39},{8,232},{9... | collective-permute-start | bytes 1277960 | tf_op jit(solution)/shard_map/ppermute | solution.py:36
  36.7 15.4 %collective-permute-start.18 = (bf16[32,3328]{1,0:T(8,128)(2,1)S(1)}, bf16[32,3328]{1,0:T(8,128)(2,1)S(1)}, u32[]{:S(2)}, u32[]{:S(2)}) collective-permute-start(bf16[32,3328]{1,0:T(8,128)(2,1)S(1)} %get-tuple-element.33), channel_id=1, source_target_pairs={{0,1},{1,2},{2,3},{3,0},{4,5},{5,6},{6,7},{7,4},{8,11},{9,8},{10,9... | collective-permute-start | bytes 638984 | tf_op jit(solution)/shard_map/ppermute | solution.py:36
  36.8 13.8 %collective-permute-start.7 = (bf16[64,3328]{1,0:T(8,128)(2,1)S(1)}, bf16[64,3328]{1,0:T(8,128)(2,1)S(1)}, u32[]{:S(2)}, u32[]{:S(2)}) collective-permute-start(bf16[64,3328]{1,0:T(8,128)(2,1)S(1)} %pad_maximum_fusion.1.own_ref), channel_id=1, source_target_pairs={{0,4},{1,5},{2,6},{3,7},{4,0},{5,1},{6,2},{7,3},{8,12},{9,13},{10,... | collective-permute-start | bytes 1277960 | tf_op jit(solution)/shard_map/ppermute | solution.py:36
  39.6 6.3 %collective-permute-start.12 = (bf16[64,3328]{1,0:T(8,128)(2,1)S(1)}, bf16[64,3328]{1,0:T(8,128)(2,1)S(1)}, u32[]{:S(2)}, u32[]{:S(2)}) collective-permute-start(bf16[64,3328]{1,0:T(8,128)(2,1)S(1)} %collective-permute-done.10.refs_2_), channel_id=1, source_target_pairs={{0,8},{1,9},{2,10},{3,11},{4,12},{5,13},{6,14},{7,15},{8,0},{9,1},... | collective-permute-start | bytes 1277960 | tf_op jit(solution)/shard_map/ppermute | solution.py:36
  41.3 7.4 %collective-permute-start.3 = (bf16[64,3328]{1,0:T(8,128)(2,1)S(1)}, bf16[64,3328]{1,0:T(8,128)(2,1)S(1)}, u32[]{:S(2)}, u32[]{:S(2)}) collective-permute-start(bf16[64,3328]{1,0:T(8,128)(2,1)S(1)} %collective-permute-done.2.refs_0_), channel_id=1, source_target_pairs={{0,32},{1,33},{2,34},{3,35},{4,36},{5,37},{6,38},{7,39},{8,232},{9... | collective-permute-start | bytes 1277960 | tf_op jit(solution)/shard_map/ppermute | solution.py:36
  44.1 6.5 %collective-permute-start.4 = (bf16[64,3328]{1,0:T(8,128)(2,1)S(1)}, bf16[64,3328]{1,0:T(8,128)(2,1)S(1)}, u32[]{:S(2)}, u32[]{:S(2)}) collective-permute-start(bf16[64,3328]{1,0:T(8,128)(2,1)S(1)} %collective-permute-done.2.refs_0_), channel_id=1, source_target_pairs={{0,8},{1,9},{2,10},{3,11},{4,12},{5,13},{6,14},{7,15},{8,0},{9,1},... | collective-permute-start | bytes 1277960 | tf_op jit(solution)/shard_map/ppermute | solution.py:36
  45.9 8.9 %collective-permute-start.13 = (bf16[64,3328]{1,0:T(8,128)(2,1)S(1)}, bf16[64,3328]{1,0:T(8,128)(2,1)S(1)}, u32[]{:S(2)}, u32[]{:S(2)}) collective-permute-start(bf16[64,3328]{1,0:T(8,128)(2,1)S(1)} %collective-permute-done.11.refs_2_), channel_id=1, source_target_pairs={{0,32},{1,33},{2,34},{3,35},{4,36},{5,37},{6,38},{7,39},{8,232},{9... | collective-permute-start | bytes 1277960 | tf_op jit(solution)/shard_map/ppermute | solution.py:36
  48.7 6.1 %collective-permute-start.14 = (bf16[64,3328]{1,0:T(8,128)(2,1)S(1)}, bf16[64,3328]{1,0:T(8,128)(2,1)S(1)}, u32[]{:S(2)}, u32[]{:S(2)}) collective-permute-start(bf16[64,3328]{1,0:T(8,128)(2,1)S(1)} %collective-permute-done.11.refs_2_), channel_id=1, source_target_pairs={{0,8},{1,9},{2,10},{3,11},{4,12},{5,13},{6,14},{7,15},{8,0},{9,1},... | collective-permute-start | bytes 1277960 | tf_op jit(solution)/shard_map/ppermute | solution.py:36
  50.6 7.3 %collective-permute-start.8 = (bf16[64,3328]{1,0:T(8,128)(2,1)S(1)}, bf16[64,3328]{1,0:T(8,128)(2,1)S(1)}, u32[]{:S(2)}, u32[]{:S(2)}) collective-permute-start(bf16[64,3328]{1,0:T(8,128)(2,1)S(1)} %collective-permute-done.3.refs_4_), channel_id=1, source_target_pairs={{0,32},{1,33},{2,34},{3,35},{4,36},{5,37},{6,38},{7,39},{8,232},{9... | collective-permute-start | bytes 1277960 | tf_op jit(solution)/shard_map/ppermute | solution.py:36
  52.2 10.7 %collective-permute-start.19 = (bf16[64,3328]{1,0:T(8,128)(2,1)S(1)}, bf16[64,3328]{1,0:T(8,128)(2,1)S(1)}, u32[]{:S(2)}, u32[]{:S(2)}) collective-permute-start(bf16[64,3328]{1,0:T(8,128)(2,1)S(1)} %constant_dynamic-update-slice_fusion.2.far_own_ref), channel_id=1, source_target_pairs={{0,4},{1,5},{2,6},{3,7},{4,0},{5,1},{6,2},{7,3},{8,12},{9,13},{10,... | collective-permute-start | bytes 1277960 | tf_op jit(solution)/shard_map/ppermute | solution.py:36
  54.7 8.9 %collective-permute-start.15 = (bf16[64,3328]{1,0:T(8,128)(2,1)S(1)}, bf16[64,3328]{1,0:T(8,128)(2,1)S(1)}, u32[]{:S(2)}, u32[]{:S(2)}) collective-permute-start(bf16[64,3328]{1,0:T(8,128)(2,1)S(1)} %collective-permute-done.3.refs_4_), channel_id=1, source_target_pairs={{0,8},{1,9},{2,10},{3,11},{4,12},{5,13},{6,14},{7,15},{8,0},{9,1},... | collective-permute-start | bytes 1277960 | tf_op jit(solution)/shard_map/ppermute | solution.py:36
  54.8 8.8 %collective-permute-start.16 = (bf16[64,3328]{1,0:T(8,128)(2,1)S(1)}, bf16[64,3328]{1,0:T(8,128)(2,1)S(1)}, u32[]{:S(2)}, u32[]{:S(2)}) collective-permute-start(bf16[64,3328]{1,0:T(8,128)(2,1)S(1)} %collective-permute-done.13.refs_6_), channel_id=1, source_target_pairs={{0,8},{1,9},{2,10},{3,11},{4,12},{5,13},{6,14},{7,15},{8,0},{9,1},... | collective-permute-start | bytes 1277960 | tf_op jit(solution)/shard_map/ppermute | solution.py:36
  55.3 7.7 %collective-permute-start.21 = (bf16[32,3328]{1,0:T(8,128)(2,1)S(1)}, bf16[32,3328]{1,0:T(8,128)(2,1)S(1)}, u32[]{:S(2)}, u32[]{:S(2)}) collective-permute-start(bf16[32,3328]{1,0:T(8,128)(2,1)S(1)} %slice.16), channel_id=1, source_target_pairs={{0,32},{1,33},{2,34},{3,35},{4,36},{5,37},{6,38},{7,39},{8,232},{9... | collective-permute-start | bytes 638984 | tf_op jit(solution)/shard_map/ppermute | solution.py:36
  57.9 7.1 %collective-permute-start.9 = (bf16[32,3328]{1,0:T(8,128)(2,1)S(1)}, bf16[32,3328]{1,0:T(8,128)(2,1)S(1)}, u32[]{:S(2)}, u32[]{:S(2)}) collective-permute-start(bf16[32,3328]{1,0:T(8,128)(2,1)S(1)} %slice.18), channel_id=1, source_target_pairs={{0,32},{1,33},{2,34},{3,35},{4,36},{5,37},{6,38},{7,39},{8,232},{9... | collective-permute-start | bytes 638984 | tf_op jit(solution)/shard_map/ppermute | solution.py:36
  62.8 5.4 %collective-permute-start.20 = (bf16[64,3328]{1,0:T(8,128)(2,1)S(1)}, bf16[64,3328]{1,0:T(8,128)(2,1)S(1)}, u32[]{:S(2)}, u32[]{:S(2)}) collective-permute-start(bf16[64,3328]{1,0:T(8,128)(2,1)S(1)} %collective-permute-done.8.refs_0_), channel_id=1, source_target_pairs={{0,8},{1,9},{2,10},{3,11},{4,12},{5,13},{6,14},{7,15},{8,0},{9,1},... | collective-permute-start | bytes 1277960 | tf_op jit(solution)/shard_map/ppermute | solution.py:36
  63.0 4.2 %collective-permute-start.22 = (bf16[32,3328]{1,0:T(8,128)(2,1)S(1)}, bf16[32,3328]{1,0:T(8,128)(2,1)S(1)}, u32[]{:S(2)}, u32[]{:S(2)}) collective-permute-start(bf16[32,3328]{1,0:T(8,128)(2,1)S(1)} %collective-permute-done.21.refs_2_), channel_id=1, source_target_pairs={{0,8},{1,9},{2,10},{3,11},{4,12},{5,13},{6,14},{7,15},{8,0},{9,1},... | collective-permute-start | bytes 638984 | tf_op jit(solution)/shard_map/ppermute | solution.py:36
  65.0 3.3 %collective-permute-start.23 = (bf16[32,3328]{1,0:T(8,128)(2,1)S(1)}, bf16[32,3328]{1,0:T(8,128)(2,1)S(1)}, u32[]{:S(2)}, u32[]{:S(2)}) collective-permute-start(bf16[32,3328]{1,0:T(8,128)(2,1)S(1)} %collective-permute-done.9.refs_4_), channel_id=1, source_target_pairs={{0,8},{1,9},{2,10},{3,11},{4,12},{5,13},{6,14},{7,15},{8,0},{9,1},... | collective-permute-start | bytes 638984 | tf_op jit(solution)/shard_map/ppermute | solution.py:36
  98.9 14.4 %all-to-all-start.2 = ((s16[8,144,256]{2,1,0:T(8,128)(2,1)}), s16[8,144,256]{2,1,0:T(8,128)(2,1)S(1)}, u32[]{:S(2)}, u32[]{:S(2)}) async-start(s16[8,144,256]{2,1,0:T(8,128)(2,1)} %shard_map.57), calls=%async_computation.2 | async-start | bytes 1179648 | tf_op jit(solution)/shard_map/all_to_all | solution.py:426
